TPU v7x, 768 devices: a whole 4x8x12 slice. The times are simulated.
768 devices in a mesh: rep: 12 (over z), dp: 16 (over y, core), tp: 4 (over x).
Axes of the slice: x: 4, y: 8, z: 12, core: 2. Of those that a mesh axis runs over, the one named last changes fastest.
Arguments:
- hidden_in: bfloat16 [73728, 8192], P(('rep', 'dp')), may hold values from -0.022094727 to 0.022094727
- value_grad: bfloat16 [73728, 512], P(('rep', 'dp'), 'tp'), may hold values from -6 to 6
- weight_shards: bfloat16 [12288, 512], P('dp', 'tp'), may hold values from -0.25 to 0.25
- shard_blocks: int32 [16], replicated, may hold values from 1 to 6, as said below
- token_counts: int32 [192], P(('rep', 'dp')), may hold values from 96 to 384, as said below
Outputs:
- input_grad: bfloat16 [73728, 8192], P(('rep', 'dp'), 'tp')
- weight_grad: float32 [12288, 512], P('dp', 'tp')
Inputs may be any that keep to these rules, and one draw needn't show every extreme that they name: `shard_blocks`: sums to 64; some owner holds exactly 6 blocks. `token_counts`: some micro-batch is full and some holds exactly 96 tokens.
All inputs are finite; a program needn't handle non-finite values.
Results may differ from a plain program's by a relative error of at most 0.013.
Values may be sent and summed in bfloat16 or wider, within the bound.
No kernel may reach another device: no remote copies, remote signals or barrier semaphores. Data moves between devices by JAX's collectives and lax.ppermute only.
A program may use at most 128 MiB of HBM per device.

v0:
```python
import jax
import jax.numpy as jnp
from jax import lax
from jax.sharding import PartitionSpec as P

BLOCK = 128


def on_device(hidden_in, value_grad, weight_shards, shard_blocks, token_counts):
    rows_dev = hidden_in.shape[0]
    width = hidden_in.shape[1]
    shard_rows = weight_shards.shape[0]
    columns = weight_shards.shape[1]
    live = lax.broadcasted_iota(jnp.int32, (rows_dev, 1), 0) < token_counts[0]
    masked = jnp.where(live, value_grad, jnp.zeros_like(value_grad))
    lengths = shard_blocks * BLOCK
    starts = jnp.cumsum(lengths) - lengths
    local = lax.broadcasted_iota(jnp.int32, (shard_rows, 1), 0)

    def own_rows(piece, index, owner):
        rows = lax.dynamic_slice_in_dim(piece, index * shard_rows, shard_rows, 0)
        return jnp.where(local < lengths[owner], rows, jnp.zeros_like(rows))

    initial = jnp.zeros((width + shard_rows, columns), jnp.bfloat16)
    piece = lax.all_gather(weight_shards, "dp", axis=0, tiled=True)

    def place_one(index, acc):
        rows = own_rows(piece, index, index)
        slab = lax.dynamic_slice_in_dim(acc, starts[index], shard_rows, 0) + rows
        return lax.dynamic_update_slice_in_dim(acc, slab, starts[index], 0)

    folded = lax.fori_loop(0, piece.shape[0] // shard_rows, place_one, initial)
    partial_dx = lax.dot_general(
        masked, folded[:width], (((1,), (1,)), ((), ())), preferred_element_type=jnp.float32
    )
    input_grad = lax.psum_scatter(
        partial_dx.astype(jnp.bfloat16), "tp", scatter_dimension=1, tiled=True
    )
    padded_in = jnp.concatenate(
        [hidden_in, jnp.zeros((rows_dev, shard_rows), hidden_in.dtype)], axis=1
    )

    def one_owner(index):
        chosen = lax.dynamic_slice_in_dim(padded_in, starts[index], shard_rows, 1)
        product = lax.dot_general(
            chosen, masked, (((0,), (0,)), ((), ())), preferred_element_type=jnp.float32
        )
        return jnp.where(local < lengths[index], product, jnp.zeros((), jnp.float32))

    pieces = lax.map(
        one_owner, jnp.arange(shard_rows * lax.axis_size("dp") // shard_rows, dtype=jnp.int32)
    )
    owned = lax.psum_scatter(
        pieces.reshape(shard_rows * lax.axis_size("dp"), columns),
        "dp",
        scatter_dimension=0,
        tiled=True,
    )
    weight_grad = lax.psum(owned, "rep")
    return (input_grad, weight_grad)


def solution(mesh):
    placed = (P(("rep", "dp"), None), P(("rep", "dp"), "tp"), P("dp", "tp"), P(), P(("rep", "dp")))
    return jax.shard_map(
        on_device,
        mesh=mesh,
        in_specs=placed,
        out_specs=(P(("rep", "dp"), "tp"), P("dp", "tp")),
        check_vma=False,
    )
```

profile of v0, /device:TPU:6, one launch (start us, length us, event | category | flops | bytes accessed | tf_op | source)
XLA Modules:
  0.0 446.1 jit_solution(13412837751238506172)
XLA Ops:
  9.5 6.1 %concatenate.3 = bf16[384,8960]{1,0:T(8,128)(2,1)} pad(bf16[384,8192]{1,0:T(8,128)(2,1)} %param.9, bf16[]{:T(256)} %constant.69.clone.1), padding=0_0x0_768 | pad | bytes 13172738 | tf_op jit(solution)/shard_map/concatenate | solution.py:39
  15.8 141.8 %while.26 = (s32[]{:T(128)}, f32[16,768,128]{2,1,0:T(8,128)}, s32[16]{0:T(128)S(1)}, s32[16]{0:T(128)S(1)}, s32[16]{0:T(128)S(1)}, /*index=5*/bf16[384,8960]{1,0...) while((s32[]{:T(128)}, f32[16,768,128]{2,1,0:T(8,128)}, ...), condition=%wide.region_5.6_spmd.clone, body=%wide.region_4.5_spmd.clone.sunk | while | flops 75596552 | bytes 1083613 | solution.py:50
  22.2 2.5 fusion.18
  31.0 2.5 fusion.18
  39.9 2.5 fusion.18
  48.7 2.6 fusion.18
  57.6 2.6 fusion.18
  66.5 2.6 fusion.18
  75.4 2.6 fusion.18
  84.3 2.5 fusion.18
  93.1 2.5 fusion.18
  102.0 2.5 fusion.18
  110.8 2.5 fusion.18
  119.7 2.5 fusion.18
  128.5 2.5 fusion.18
  137.4 2.5 fusion.18
  146.2 2.5 fusion.18
  155.1 2.6 fusion.18
  158.1 89.1 %while.25 = (s32[]{:T(128)}, bf16[8960,128]{1,0:T(8,128)(2,1)S(1)}, s32[16]{0:T(128)S(1)}, s32[16]{0:T(128)S(1)}, bf16[12288,128]{1,0:T(8,128)(2,1)}, /*index=5*...) while((s32[]{:T(128)}, bf16[8960,128]{1,0:T(8,128)(2,1)S(1)}, s32[16]{0:T(128)S(1)}, ...), condition=%wide.region_2.3_spmd.clone, body=%wide.region_1.2_spmd.clone.sunk | while | flops 492297 | bytes 984797 | solution.py:32
  200.8 1.1 select_add_fusion.2
  247.3 4.5 %convolution_convert_fusion = bf16[384,8192]{1,0:T(8,128)(2,1)} fusion(bf16[384,128]{1,0:T(8,128)(2,1)S(1)} %get-tuple-element.356, bf16[8960,128]{1,0:T(8,128)(2,1)S(1)} %get-tuple-element.153), kind=kOutput, calls=%fused_computation.10 | convolution fusion | flops 808452096 | bytes 8486912 | tf_op jit(solution)/shard_map/dot_general | solution.py:33
  251.8 114.9 %all-reduce.3.cloned.1.call-done = f32[768,128]{1,0:T(8,128)} async-done(((f32[768,128]{1,0:T(8,128)}), f32[768,128]{1,0:T(8,128)}) %all-reduce.3.cloned.1.call-update) | async-done | bytes 393232 | tf_op jit(solution)/shard_map/psum | solution.py:59
  366.7 71.1 %reduce-scatter.3.cloned.1.call-done = bf16[384,2048]{1,0:T(8,128)(2,1)} async-done(((bf16[384,8192]{1,0:T(8,128)(2,1)}), bf16[384,2048]{1,0:T(8,128)(2,1)}) %reduce-scatter.3.cloned.1.call-update) | async-done | bytes 1572880 | tf_op jit(solution)/shard_map/reduce_scatter | solution.py:36
  437.8 1.8 copy.25
  (167 shorter events, 97.3 us)
Async XLA Ops:
  7.2 150.6 %all-gather.2.cloned.1.call-start = ((), (), s32[]{:S(2)}) async-start(), calls=%async_computation.2 | async-start | bytes 3342336 | tf_op jit(solution)/shard_map/all_gather | solution.py:25
  7.9 239.3 %reduce-scatter.5.cloned.1.call-start = ((), (), s32[]{:S(2)}) async-start(), calls=%async_computation.4 | async-start | bytes 6684672 | tf_op jit(solution)/shard_map/reduce_scatter | solution.py:53
  9.5 6.2 %copy-start.1 = (s32[16]{0:T(128)S(1)}, s32[16]{0:T(128)}, u32[]{:S(2)}) copy-start(s32[16]{0:T(128)} %param.12) | copy-start | bytes 196
  9.5 6.2 %copy-start = (bf16[384,128]{1,0:T(8,128)(2,1)S(1)}, bf16[384,128]{1,0:T(8,128)(2,1)}, u32[]{:S(2)}) copy-start(bf16[384,128]{1,0:T(8,128)(2,1)} %param.10) | copy-start | bytes 294916
  157.6 209.0 %all-reduce.3.cloned.1.call-start = ((), (), s32[]{:S(2)}) async-start(), calls=%async_computation.5 | async-start | bytes 786432 | tf_op jit(solution)/shard_map/psum | solution.py:59
  247.2 190.6 %reduce-scatter.3.cloned.1.call-start = ((), (), s32[]{:S(2)}) async-start(), calls=%async_computation.3 | async-start | bytes 7864320 | tf_op jit(solution)/shard_map/reduce_scatter | solution.py:36
Sparse Core Ops, SparseCore 0:
  10.4 52.8 all-gather.1
  157.8 78.5 reduce-scatter.4
  247.3 119.3 all-reduce.2
  370.6 67.1 reduce-scatter.2
where the time goes:
time: 452 us; the launch traced here: 446 us
  waiting for transfers between devices  187 us (41%)
  loops' own time  94 us (21%)
  local copies, waits for them, and re-layouts  65.4 us (14%)
  matrix products  45.2 us (10%)
  other arithmetic  40 us (9%)
  between operations  14.5 us (3%)
    psum x1, waiting for transfers between devices, on_device(): weight_grad = lax.psum(owned, 'rep')  115 us
    reduce_scatter x1, waiting for transfers between devices, on_device(): lax.psum_scatter(partial_dx.astype(jnp.bfloat16), 'tp', scatter_dimension...  71.1 us
    another operation x1, loops' own time, on_device(): lax.map(one_owner, jnp.arange(shard_rows * lax.axis_size('dp') // shard_r...  62.3 us
    dot_general x16, matrix products, one_owner(): lax.dot_general(chosen, masked, (((0,), (0,)), ((), ())), preferred_eleme...  40.7 us
    another operation x1, loops' own time, on_device(): folded = lax.fori_loop(0, piece.shape[0] // shard_rows, place_one, initial)  31.8 us
    add x16, other arithmetic, place_one(): slab = lax.dynamic_slice_in_dim(acc, starts[index], shard_rows, 0) + rows  17.7 us
    lt x16, other arithmetic, own_rows(): return jnp.where(local < lengths[owner], rows, jnp.zeros_like(rows))  10.7 us
    lt x16, other arithmetic, one_owner(): local < lengths[index]  10.7 us
  transfers between devices with their start and end apart: 4, of which 2 were waited for; matrix products, arithmetic and copies ran while one was open for 33% of the time, Pallas kernels for 0%

commit v1 on v0

v1 whole, which is shorter than its diff:
```python
import functools

import jax
import jax.numpy as jnp
from jax import lax
from jax.experimental import pallas as pl
from jax.experimental.pallas import tpu as pltpu
from jax.sharding import PartitionSpec as P

BLOCK = 128
SPLIT = 3
PIECE = 48
PIECE_AT = (0, 48, 80)
BIG_VMEM = 58 * 1024 * 1024
SMALL = pltpu.CompilerParams(vmem_limit_bytes=12 * 1024 * 1024)


def fill_places(blocks_ref, place, slot_blocks):
    def owner_places(owner, first):
        def one(at, carry):
            place[first + at] = owner * slot_blocks + at
            return carry

        lax.fori_loop(0, blocks_ref[owner], one, 0)
        return first + blocks_ref[owner]

    lax.fori_loop(0, blocks_ref.shape[0], owner_places, 0)


def grad_kernel(per_step, slot_blocks, counts_ref, blocks_ref, hidden_ref, grad_ref, send_ref, keep_ref, place, masked_t):
    step = pl.program_id(0)
    core = lax.rem(lax.axis_index("dp"), 2)
    turn = lax.rem(lax.axis_index("rep"), SPLIT)
    owners = blocks_ref.shape[0]
    part_blocks = slot_blocks // SPLIT

    @pl.when(step == 0)
    def _():
        fill_places(blocks_ref, place, slot_blocks)
        send_ref[...] = jnp.zeros_like(send_ref)
        keep_ref[...] = jnp.zeros_like(keep_ref)
        live = lax.broadcasted_iota(jnp.int32, grad_ref.shape, 0) < counts_ref[0]
        masked = jnp.where(live, grad_ref[...].astype(jnp.float32), 0.0)
        masked_t[...] = masked.T.astype(masked_t.dtype)

    product = jnp.dot(masked_t[...], hidden_ref[...], preferred_element_type=jnp.float32)
    for at in range(per_step):
        slot = place[step * per_step + at]
        owner = lax.div(slot, slot_blocks)
        inside = lax.rem(slot, slot_blocks)
        part = lax.rem(lax.div(inside, part_blocks) + SPLIT - turn, SPLIT)
        block = (part * (owners // 2) + lax.div(owner, 2)) * part_blocks + lax.rem(inside, part_blocks)
        row = pl.multiple_of(block * BLOCK, BLOCK)
        tile = product[:, at * BLOCK:(at + 1) * BLOCK].astype(send_ref.dtype)
        mine = lax.rem(owner, 2) == core

        @pl.when(mine)
        def _():
            keep_ref[pl.ds(row, BLOCK), :] = tile

        @pl.when(jnp.logical_not(mine))
        def _():
            send_ref[pl.ds(row, BLOCK), :] = tile


def grad_products(counts, shard_blocks, hidden, grad, slot_rows):
    rows, width = hidden.shape
    owners = shard_blocks.shape[0]
    chunk = 1024
    half = (owners // 2) * slot_rows
    out = jax.ShapeDtypeStruct((half, grad.shape[1]), jnp.bfloat16)
    return pl.pallas_call(
        functools.partial(grad_kernel, chunk // BLOCK, slot_rows // BLOCK),
        grid=(width // chunk,),
        in_specs=[
            pl.BlockSpec(memory_space=pltpu.SMEM),
            pl.BlockSpec(memory_space=pltpu.SMEM),
            pl.BlockSpec((rows, chunk), lambda i: (0, i)),
            pl.BlockSpec(grad.shape, lambda i: (0, 0)),
        ],
        out_specs=[pl.BlockSpec(out.shape, lambda i: (0, 0))] * 2,
        out_shape=[out, out],
        scratch_shapes=[
            pltpu.SMEM((width // BLOCK,), jnp.int32),
            pltpu.VMEM((grad.shape[1], rows), jnp.bfloat16),
        ],
        compiler_params=pltpu.CompilerParams(vmem_limit_bytes=BIG_VMEM),
        cost_estimate=pl.CostEstimate(
            flops=2 * rows * width * grad.shape[1], bytes_accessed=2 * rows * width + 4 * half * 128, transcendentals=0
        ),
        name="grad_products",
    )(counts, shard_blocks, hidden, grad)


def pair_kernel(keep_ref, received_ref, *outs):
    rows = outs[0].shape[0]
    for k, out in enumerate(outs):
        here = pl.ds(k * rows, rows)
        total = keep_ref[here, :].astype(jnp.float32) + received_ref[here, :].astype(jnp.float32)
        out[...] = total.astype(out.dtype)


def paired_parts(keep, received):
    out = jax.ShapeDtypeStruct((keep.shape[0] // SPLIT, keep.shape[1]), keep.dtype)
    return pl.pallas_call(pair_kernel, out_shape=[out] * SPLIT, compiler_params=SMALL, name="pair_parts")(keep, received)


def summed(parts):
    total = parts[0].astype(jnp.float32)
    for part in parts[1:]:
        total = total + part.astype(jnp.float32)
    return total.astype(parts[0].dtype)


def finish_kernel(share, total_ref, out_ref):
    n_rep = total_ref.shape[0] // share
    per = out_ref.shape[0] // SPLIT
    rows = [None] * (out_ref.shape[0] // share)
    for rep in range(n_rep):
        first = (rep % SPLIT) * per + (rep // SPLIT) * share
        rows[first // share] = total_ref[rep * share:(rep + 1) * share, :].astype(out_ref.dtype)
    slot = jnp.concatenate(rows, axis=0)
    for at in range(out_ref.shape[0] // BLOCK):
        out_ref[at * BLOCK:(at + 1) * BLOCK, :] = slot[at * BLOCK:(at + 1) * BLOCK, :].T


def finished(total, share):
    return pl.pallas_call(
        functools.partial(finish_kernel, share),
        out_shape=jax.ShapeDtypeStruct(total.shape, jnp.float32),
        compiler_params=SMALL,
        name="finish_weight_grad",
    )(total)


def compact_kernel(slot_blocks, n_tp, blocks_ref, mine_ref, other_ref, grad_ref, out_ref, place):
    core = lax.rem(lax.axis_index("dp"), 2)
    fill_places(blocks_ref, place, slot_blocks)
    per = place.shape[0] // n_tp
    for target in range(n_tp):
        def one(at, carry):
            slot = place[target * per + at]
            owner = lax.div(slot, slot_blocks)
            block = lax.div(owner, 2) * slot_blocks + lax.rem(slot, slot_blocks)
            source = pl.ds(pl.multiple_of(block * PIECE, 16), PIECE)
            here = pl.ds(pl.multiple_of(at * PIECE, 16), PIECE)
            mine = lax.rem(owner, 2) == core

            @pl.when(mine)
            def _():
                out_ref[target, here, :] = mine_ref[source, :]

            @pl.when(jnp.logical_not(mine))
            def _():
                out_ref[target, here, :] = other_ref[source, :]

            return carry

        lax.fori_loop(0, per, one, 0)
        out_ref[target, pl.ds(per * PIECE, grad_ref.shape[0]), :] = grad_ref[...]


def compacted(shard_blocks, mine, other, grad, slot_rows, n_tp, width):
    n_blocks = width // BLOCK
    rows = n_blocks // n_tp * PIECE + grad.shape[0]
    return pl.pallas_call(
        functools.partial(compact_kernel, slot_rows // BLOCK, n_tp),
        in_specs=[pl.BlockSpec(memory_space=pltpu.SMEM)] + [pl.BlockSpec(memory_space=pltpu.VMEM)] * 3,
        out_shape=jax.ShapeDtypeStruct((n_tp, rows, grad.shape[1]), grad.dtype),
        scratch_shapes=[pltpu.SMEM((n_blocks,), jnp.int32)],
        compiler_params=SMALL,
        name="compact_rows",
    )(shard_blocks, mine, other, grad)


def input_kernel(counts_ref, own_ref, before_ref, after_ref, grads_ref, out_ref, masked, weight):
    step = pl.program_id(0)
    turn = lax.rem(lax.axis_index("rep"), SPLIT)
    heads = own_ref.shape[0]
    blocks = own_ref.shape[1] // PIECE

    @pl.when(step == 0)
    def _():
        for h in range(heads):
            grad = grads_ref[h].astype(jnp.float32)
            live = lax.broadcasted_iota(jnp.int32, grad.shape, 0) < counts_ref[0]
            masked[:, h * BLOCK:(h + 1) * BLOCK] = jnp.where(live, grad, 0.0).astype(masked.dtype)

    for own in range(SPLIT):
        @pl.when(turn == own)
        def _():
            for shift, ref in ((0, own_ref), (SPLIT - 1, before_ref), (1, after_ref)):
                piece = (own + shift) % SPLIT
                first = PIECE_AT[piece]
                for h in range(heads):
                    for b in range(blocks):
                        weight[b * BLOCK + first:b * BLOCK + first + PIECE, h * BLOCK:(h + 1) * BLOCK] = ref[
                            h, b * PIECE:(b + 1) * PIECE, :
                        ]

    out_ref[...] = lax.dot_general(
        masked[...], weight[...], (((1,), (1,)), ((), ())), preferred_element_type=jnp.float32
    ).astype(out_ref.dtype)


def input_product(counts, own, before, after, rows_dev):
    n_tp, _, head = own.shape
    pieces = before.shape[1]
    steps = 4
    blocks = pieces // PIECE // steps
    chunk = blocks * BLOCK
    piece = pl.BlockSpec((n_tp, blocks * PIECE, head), lambda i: (0, i, 0))
    return pl.pallas_call(
        input_kernel,
        grid=(steps,),
        in_specs=[
            pl.BlockSpec(memory_space=pltpu.SMEM),
            piece,
            piece,
            piece,
            pl.BlockSpec((n_tp, rows_dev, head), lambda i: (0, pieces // rows_dev, 0)),
        ],
        out_specs=pl.BlockSpec((rows_dev, chunk), lambda i: (0, i)),
        out_shape=jax.ShapeDtypeStruct((rows_dev, steps * chunk), jnp.bfloat16),
        scratch_shapes=[
            pltpu.VMEM((rows_dev, head * n_tp), jnp.bfloat16),
            pltpu.VMEM((chunk, head * n_tp), jnp.bfloat16),
        ],
        compiler_params=pltpu.CompilerParams(vmem_limit_bytes=24 * 1024 * 1024),
        cost_estimate=pl.CostEstimate(
            flops=2 * rows_dev * steps * chunk * head * n_tp,
            bytes_accessed=2 * steps * chunk * (head * n_tp + rows_dev),
            transcendentals=0,
        ),
        name="input_grad",
    )(counts, own, before, after, own)


def on_device(hidden_in, value_grad, weight_shards, shard_blocks, token_counts):
    rows_dev, width = hidden_in.shape
    slot_rows, head = weight_shards.shape
    n_dp, n_tp, n_rep = lax.axis_size("dp"), lax.axis_size("tp"), lax.axis_size("rep")
    n_y = n_dp // 2
    slot_blocks = slot_rows // BLOCK
    core_swap = [(i, i ^ 1) for i in range(n_dp)]
    along_y = [[c + 2 * y for y in range(n_y)] for c in range(2)]
    up = [(i, (i + 1) % n_rep) for i in range(n_rep)]
    down = [(i, (i - 1) % n_rep) for i in range(n_rep)]

    turn = lax.rem(lax.axis_index("rep"), SPLIT)
    first = turn * PIECE_AT[1] - jnp.where(turn == 2, 2 * PIECE_AT[1] - PIECE_AT[2], 0)
    piece = lax.dynamic_slice_in_dim(weight_shards.reshape(slot_blocks, BLOCK, head), first, PIECE, 1)
    piece = piece.reshape(1, slot_blocks * PIECE, head)
    held = lax.all_to_all(
        jnp.broadcast_to(piece, (n_y,) + piece.shape[1:]), "dp", 0, 0, axis_index_groups=along_y
    ).reshape(n_y * slot_blocks * PIECE, head)
    other = lax.ppermute(held, "dp", core_swap)
    sent = compacted(shard_blocks, held, other, value_grad, slot_rows, n_tp, width)
    own = lax.all_to_all(sent, "tp", 0, 0)
    pieces = own[:, : own.shape[1] - rows_dev]
    before = lax.ppermute(pieces, "rep", up)
    after = lax.ppermute(pieces, "rep", down)
    input_grad = input_product(token_counts, own, before, after, rows_dev)

    send, keep = grad_products(token_counts, shard_blocks, hidden_in, value_grad, slot_rows)
    received = lax.ppermute(send, "dp", core_swap)
    stay, to_next, to_last = paired_parts(keep, received)
    part = summed([stay, lax.ppermute(to_next, "rep", up), lax.ppermute(to_last, "rep", down)])
    spread = lax.all_to_all(part.reshape(n_y, slot_rows // SPLIT, head), "dp", 0, 0, axis_index_groups=along_y)
    owned = summed([spread[y] for y in range(n_y)])
    fellows = [[k + SPLIT * q for q in range(n_rep // SPLIT)] for k in range(SPLIT)]
    share_rows = slot_rows // n_rep
    shares = lax.all_to_all(
        owned.reshape(n_rep // SPLIT, share_rows, head), "rep", 0, 0, axis_index_groups=fellows
    )
    share = summed([shares[q] for q in range(n_rep // SPLIT)])
    total = lax.all_to_all(jnp.broadcast_to(share[None], (n_rep,) + share.shape), "rep", 0, 0)
    weight_grad = finished(total.reshape(slot_rows, head), share_rows)
    return (input_grad, weight_grad)


def solution(mesh):
    placed = (P(("rep", "dp"), None), P(("rep", "dp"), "tp"), P("dp", "tp"), P(), P(("rep", "dp")))
    return jax.shard_map(
        on_device,
        mesh=mesh,
        in_specs=placed,
        out_specs=(P(("rep", "dp"), "tp"), P("dp", "tp")),
        check_vma=False,
    )
```

time: 452 us -> 139 us (0.31)
  waiting for transfers between devices: 187 us -> 49.6 us
  loops' own time: 94 us -> 0 us
  local copies, waits for them, and re-layouts: 65.4 us -> 2.56 us
  starting transfers between devices: 0.16 us -> 61.5 us
  matrix products: 45.2 us -> 0 us
  other arithmetic: 40 us -> 1.73 us
  Pallas kernels: 0 us -> 20.3 us
  between operations: 14.5 us -> 1.45 us
    psum x1 -> x0, waiting for transfers between devices: 115 us -> none  [on_device(): weight_grad = lax.psum(owned, 'rep')]
    another operation x2 -> x0, loops' own time: 94 us -> none  [the longest x1 62.3 us: on_device(): lax.map(one_owner, jnp.arange(shard_rows * lax.axis_size('dp') // shard_r...]
    reduce_scatter x2 -> x0, waiting for transfers between devices: 71.1 us -> none  [the longest x1 71.1 us: on_device(): lax.psum_scatter(partial_dx.astype(jnp.bfloat16), 'tp', scatter_dimension...]
    dynamic_slice x80 -> x1, local copies, waits for them, and re-layouts: 46.9 us -> 0.01 us  [on_device(): lax.dynamic_slice_in_dim(weight_shards.reshape(slot_blocks, BLOCK, head),...]
    dot_general x17 -> x0, matrix products: 45.2 us -> none  [the longest x16 40.7 us: one_owner(): lax.dot_general(chosen, masked, (((0,), (0,)), ((), ())), preferred_eleme...]
    all_to_all x0 -> x5, starting transfers between devices: none -> 32.7 us  [the longest x1 8.4 us: on_device(): lax.all_to_all(jnp.broadcast_to(share[None], (n_rep,) + share.shape), 're...]
    ppermute x0 -> x6, starting transfers between devices: none -> 28.7 us  [the longest x1 12.2 us: on_device(): lax.ppermute(to_last, 'rep', down)]
    all_to_all x0 -> x5, waiting for transfers between devices: none -> 26.5 us  [the longest x1 11.9 us: on_device(): own = lax.all_to_all(sent, 'tp', 0, 0)]
  transfers between devices with their start and end apart: 4 -> 11, of which waited for: 2 -> 9; matrix products, arithmetic and copies ran while one was open for 33% -> 3% of each run, Pallas kernels for 0% -> 7%
where the time goes in v1:
time: 139 us; the launch traced here: 137 us
  starting transfers between devices  61.5 us (44%)
  waiting for transfers between devices  49.6 us (36%)
  Pallas kernels  20.3 us (15%)
  local copies, waits for them, and re-layouts  2.56 us (2%)
  other arithmetic  1.73 us (1%)
  between operations  1.45 us (1%)
    ppermute x1, starting transfers between devices, on_device(): lax.ppermute(to_last, 'rep', down)  12.2 us
    all_to_all x1, waiting for transfers between devices, on_device(): own = lax.all_to_all(sent, 'tp', 0, 0)  11.9 us
    pallas_call x1, Pallas kernels, grad_products(): pl.pallas_call(functools.partial(grad_kernel, chunk // BLOCK, slot_rows /...  10.4 us
    ppermute x1, waiting for transfers between devices, on_device(): lax.ppermute(to_next, 'rep', up)  10.4 us
    all_to_all x1, waiting for transfers between devices, on_device(): lax.all_to_all(part.reshape(n_y, slot_rows // SPLIT, head), 'dp', 0, 0, a...  9 us
    all_to_all x1, starting transfers between devices, on_device(): lax.all_to_all(jnp.broadcast_to(share[None], (n_rep,) + share.shape), 're...  8.4 us
    all_to_all x1, starting transfers between devices, on_device(): lax.all_to_all(jnp.broadcast_to(piece, (n_y,) + piece.shape[1:]), 'dp', 0...  7.11 us
    all_to_all x1, starting transfers between devices, on_device(): lax.all_to_all(part.reshape(n_y, slot_rows // SPLIT, head), 'dp', 0, 0, a...  6.92 us
  transfers between devices with their start and end apart: 11, of which 9 were waited for; matrix products, arithmetic and copies ran while one was open for 3% of the time, Pallas kernels for 7%

profile of v1, /device:TPU:6, one launch (start us, length us, event | category | flops | bytes accessed | tf_op | source)
XLA Modules:
  0.0 137.1 jit_solution(12085171531925333352)
XLA Ops:
  1.3 10.4 %grad_products.1 = (bf16[6144,128]{1,0:T(8,128)(2,1)}, bf16[6144,128]{1,0:T(8,128)(2,1)}) custom-call(s32[1]{0:T(128)S(6)} %copy.7.counts_ref, s32[16]{0:T(128)} %blocks_ref.3, bf16[384,8192]{1,0:T(8,128)(2,1)} %hidden_ref.1, bf16[384,128]{1,0:T(8,128)(2,1)} %grad_ref.3), custom_call_target="tpu_custom_call" | custom-call | flops 805306368 | bytes 9437184 | tf_op jit(solution)/shard_map/grad_products/pallas_call | solution.py:72
  11.7 2.0 %collective-permute-start.3 = (bf16[6144,128]{1,0:T(8,128)(2,1)}, bf16[6144,128]{1,0:T(8,128)(2,1)}, u32[]{:S(2)}, u32[]{:S(2)}) collective-permute-start(bf16[6144,128]{1,0:T(8,128)(2,1)} %get-tuple-element.8), channel_id=1, source_target_pairs={{0,4},{4,0},{8,12},{12,8},{16,20},{20,16},{24,28},{28,24},{32,36},... | collective-permute-start | bytes 4718600 | tf_op jit(solution)/shard_map/ppermute | solution.py:266
  14.7 7.1 %all-to-all-start = ((bf16[8,288,128]{2,1,0:T(8,128)(2,1)}), bf16[8,288,128]{2,1,0:T(8,128)(2,1)S(1)}, u32[]{:S(2)}, u32[]{:S(2)}) async-start(bf16[8,288,128]{2,1,0:T(8,128)(2,1)} %broadcast_in_dim.16), calls=%async_computation | async-start | bytes 1179648 | tf_op jit(solution)/shard_map/all_to_all | solution.py:254
  21.8 1.8 %pair_parts.1 = (bf16[2048,128]{1,0:T(8,128)(2,1)S(1)}, bf16[2048,128]{1,0:T(8,128)(2,1)S(1)}, bf16[2048,128]{1,0:T(8,128)(2,1)S(1)}) custom-call(bf16[6144,128]{1,0:T(8,128)(2,1)S(1)} %copy-done.1, bf16[6144,128]{1,0:T(8,128)(2,1)} %collective-permute-done.3.received_ref), custom_call_target="tpu_custom_call" | custom-call | tf_op jit(solution)/shard_map/pair_parts/pallas_call | solution.py:105
  23.6 4.3 %collective-permute-start.4 = (bf16[2048,128]{1,0:T(8,128)(2,1)S(1)}, bf16[2048,128]{1,0:T(8,128)(2,1)S(1)}, u32[]{:S(2)}, u32[]{:S(2)}) collective-permute-start(bf16[2048,128]{1,0:T(8,128)(2,1)S(1)} %get-tuple-element.10), channel_id=1, source_target_pairs={{0,64},{64,128},{128,192},{192,256},{256,320},{320,384},{384,448},... | collective-permute-start | bytes 1572872 | tf_op jit(solution)/shard_map/ppermute | solution.py:268
  27.9 12.2 %collective-permute-start.5 = (bf16[2048,128]{1,0:T(8,128)(2,1)S(1)}, bf16[2048,128]{1,0:T(8,128)(2,1)S(1)}, u32[]{:S(2)}, u32[]{:S(2)}) collective-permute-start(bf16[2048,128]{1,0:T(8,128)(2,1)S(1)} %get-tuple-element.11), channel_id=1, source_target_pairs={{0,704},{64,0},{128,64},{192,128},{256,192},{320,256},{384,320},{4... | collective-permute-start | bytes 1572872 | tf_op jit(solution)/shard_map/ppermute | solution.py:268
  40.1 10.4 %collective-permute-done.4 = bf16[2048,128]{1,0:T(8,128)(2,1)S(1)} collective-permute-done((bf16[2048,128]{1,0:T(8,128)(2,1)S(1)}, bf16[2048,128]{1,0:T(8,128)(2,1)S(1)}, u32[]{:S(2)}, u32[]{:S(2)}) %collective-permute-start.4) | collective-permute-done | bytes 524320 | tf_op jit(solution)/shard_map/ppermute | solution.py:268
  50.5 1.2 collective-permute-done.5
  52.7 6.9 %all-to-all-start.2 = ((bf16[8,256,128]{2,1,0:T(8,128)(2,1)}), bf16[8,256,128]{2,1,0:T(8,128)(2,1)S(1)}, u32[]{:S(2)}, u32[]{:S(2)}) async-start(bf16[8,256,128]{2,1,0:T(8,128)(2,1)} %bitcast.3), calls=%async_computation.2 | async-start | bytes 1048576 | tf_op jit(solution)/shard_map/all_to_all | solution.py:269
  59.6 1.9 %collective-permute-start = (bf16[2304,128]{1,0:T(8,128)(2,1)S(1)}, bf16[2304,128]{1,0:T(8,128)(2,1)S(1)}, u32[]{:S(2)}, u32[]{:S(2)}) collective-permute-start(bf16[2304,128]{1,0:T(8,128)(2,1)S(1)} %bitcast.9), channel_id=1, source_target_pairs={{0,4},{4,0},{8,12},{12,8},{16,20},{20,16},{24,28},{28,24},{32,36},... | collective-permute-start | bytes 1769480 | tf_op jit(solution)/shard_map/ppermute | solution.py:257
  61.5 2.0 %collective-permute-done.other_ref = bf16[2304,128]{1,0:T(8,128)(2,1)S(1)} collective-permute-done((bf16[2304,128]{1,0:T(8,128)(2,1)S(1)}, bf16[2304,128]{1,0:T(8,128)(2,1)S(1)}, u32[]{:S(2)}, u32[]{:S(2)}) %collective-permute-start) | collective-permute-done | bytes 589856 | tf_op jit(solution)/shard_map/ppermute | solution.py:257
  63.5 3.8 %compact_rows.1 = bf16[4,1152,128]{2,1,0:T(8,128)(2,1)} custom-call(s32[16]{0:T(128)S(1)} %copy-done.3, bf16[2304,128]{1,0:T(8,128)(2,1)S(1)} %bitcast.10, bf16[2304,128]{1,0:T(8,128)(2,1)S(1)} %collective-permute-done.other_ref, bf16[384,128]{1,0:T(8,128)(2,1)S(1)} %copy-done.2), custom_call_target="tpu_custom_call" | custom-call | tf_op jit(solution)/shard_map/compact_rows/pallas_call | solution.py:166
  67.4 9.0 %all-to-all-done.2 = bf16[8,256,128]{2,1,0:T(8,128)(2,1)S(1)} async-done(((bf16[8,256,128]{2,1,0:T(8,128)(2,1)}), bf16[8,256,128]{2,1,0:T(8,128)(2,1)S(1)}, u32[]{:S(2)}, u32[]{:S(2)}) %all-to-all-start.2) | async-done | bytes 524320 | tf_op jit(solution)/shard_map/all_to_all | solution.py:269
  76.4 4.8 %all-to-all-start.1 = ((bf16[4,1152,128]{2,1,0:T(8,128)(2,1)}), bf16[4,1152,128]{2,1,0:T(8,128)(2,1)S(1)}, u32[]{:S(2)}, u32[]{:S(2)}) async-start(bf16[4,1152,128]{2,1,0:T(8,128)(2,1)} %compact_rows.1), calls=%async_computation.1 | async-start | bytes 2359296 | tf_op jit(solution)/shard_map/all_to_all | solution.py:259
  81.8 11.9 %all-to-all-done.1.own_ref.grads_ref = bf16[4,1152,128]{2,1,0:T(8,128)(2,1)S(1)} async-done(((bf16[4,1152,128]{2,1,0:T(8,128)(2,1)}), bf16[4,1152,128]{2,1,0:T(8,128)(2,1)S(1)}, u32[]{:S(2)}, u32[]{:S(2)}) %all-to-all-start.1) | async-done | bytes 1179680 | tf_op jit(solution)/shard_map/all_to_all | solution.py:259
  93.7 5.6 %all-to-all-start.3 = ((bf16[4,64,128]{2,1,0:T(8,128)(2,1)}), bf16[4,64,128]{2,1,0:T(8,128)(2,1)S(1)}, u32[]{:S(2)}, u32[]{:S(2)}) async-start(bf16[4,64,128]{2,1,0:T(8,128)(2,1)} %bitcast.4), calls=%async_computation.3 | async-start | bytes 131072 | tf_op jit(solution)/shard_map/all_to_all | solution.py:273
  100.2 6.3 %collective-permute-start.2 = (bf16[4,768,128]{2,1,0:T(8,128)(2,1)}, bf16[4,768,128]{2,1,0:T(8,128)(2,1)S(1)}, u32[]{:S(2)}, u32[]{:S(2)}) collective-permute-start(bf16[4,768,128]{2,1,0:T(8,128)(2,1)} %slice.52), channel_id=1, source_target_pairs={{0,704},{64,0},{128,64},{192,128},{256,192},{320,256},{384,320},{4... | collective-permute-start | bytes 2359304 | tf_op jit(solution)/shard_map/ppermute | solution.py:262
  106.5 1.9 %collective-permute-start.1 = (bf16[4,768,128]{2,1,0:T(8,128)(2,1)}, bf16[4,768,128]{2,1,0:T(8,128)(2,1)S(1)}, u32[]{:S(2)}, u32[]{:S(2)}) collective-permute-start(bf16[4,768,128]{2,1,0:T(8,128)(2,1)} %slice.52), channel_id=1, source_target_pairs={{0,64},{64,128},{128,192},{192,256},{256,320},{320,384},{384,448},... | collective-permute-start | bytes 2359304 | tf_op jit(solution)/shard_map/ppermute | solution.py:261
  108.5 1.3 all-to-all-done.3
  110.5 8.4 %all-to-all-start.4 = ((bf16[12,64,128]{2,1,0:T(8,128)(2,1)}), bf16[12,64,128]{2,1,0:T(8,128)(2,1)S(1)}, u32[]{:S(2)}, u32[]{:S(2)}) async-start(bf16[12,64,128]{2,1,0:T(8,128)(2,1)} %broadcast_in_dim.18), calls=%async_computation.4 | async-start | bytes 393216 | tf_op jit(solution)/shard_map/all_to_all | solution.py:277
  118.9 6.5 %collective-permute-done.2.after_ref = bf16[4,768,128]{2,1,0:T(8,128)(2,1)S(1)} collective-permute-done((bf16[4,768,128]{2,1,0:T(8,128)(2,1)}, bf16[4,768,128]{2,1,0:T(8,128)(2,1)S(1)}, u32[]{:S(2)}, u32[]{:S(2)}) %collective-permute-start.2) | collective-permute-done | bytes 786464 | tf_op jit(solution)/shard_map/ppermute | solution.py:262
  125.3 3.2 %collective-permute-done.1.before_ref = bf16[4,768,128]{2,1,0:T(8,128)(2,1)S(1)} collective-permute-done((bf16[4,768,128]{2,1,0:T(8,128)(2,1)}, bf16[4,768,128]{2,1,0:T(8,128)(2,1)S(1)}, u32[]{:S(2)}, u32[]{:S(2)}) %collective-permute-start.1) | collective-permute-done | bytes 786464 | tf_op jit(solution)/shard_map/ppermute | solution.py:261
  128.5 3.4 %input_grad.1 = bf16[384,2048]{1,0:T(8,128)(2,1)} custom-call(s32[1]{0:T(128)S(6)} %copy.7.counts_ref, bf16[4,1152,128]{2,1,0:T(8,128)(2,1)S(1)} %all-to-all-done.1.own_ref.grads_ref, bf16[4,768,128]{2,1,0:T(8,128)(2,1)S(1)} %collective-permute-done.1.before_ref, bf16[4,768,128]{2,1,0:T(8,128)(2,1)S(1)} %collective-permute-done.2.after_ref, ...), custom_call_target="tpu_custom_call" | custom-call | flops 805306368 | bytes 3670016 | tf_op jit(solution)/shard_map/input_grad/pallas_call | solution.py:213
  131.9 4.3 %all-to-all-done.4 = bf16[12,64,128]{2,1,0:T(8,128)(2,1)S(1)} async-done(((bf16[12,64,128]{2,1,0:T(8,128)(2,1)}), bf16[12,64,128]{2,1,0:T(8,128)(2,1)S(1)}, u32[]{:S(2)}, u32[]{:S(2)}) %all-to-all-start.4) | async-done | bytes 196640 | tf_op jit(solution)/shard_map/all_to_all | solution.py:277
  (18 shorter events, 5.2 us)
Async XLA Ops:
  0.6 13.2 %copy-start = (bf16[768,128]{1,0:T(8,128)(2,1)S(1)}, bf16[768,128]{1,0:T(8,128)(2,1)}, u32[]{:S(2)}) copy-start(bf16[768,128]{1,0:T(8,128)(2,1)} %param.7) | copy-start | bytes 589828
  11.7 10.1 %copy-start.1 = (bf16[6144,128]{1,0:T(8,128)(2,1)S(1)}, bf16[6144,128]{1,0:T(8,128)(2,1)}, u32[]{:S(2)}) copy-start(bf16[6144,128]{1,0:T(8,128)(2,1)} %get-tuple-element.7.keep_ref) | copy-start | bytes 4718596
  11.7 10.1 %collective-permute-start.3 = (bf16[6144,128]{1,0:T(8,128)(2,1)}, bf16[6144,128]{1,0:T(8,128)(2,1)}, u32[]{:S(2)}, u32[]{:S(2)}) collective-permute-start(bf16[6144,128]{1,0:T(8,128)(2,1)} %get-tuple-element.8), channel_id=1, source_target_pairs={{0,4},{4,0},{8,12},{12,8},{16,20},{20,16},{24,28},{28,24},{32,36},... | collective-permute-start | bytes 4718600 | tf_op jit(solution)/shard_map/ppermute | solution.py:266
  14.7 38.0 %all-to-all-start = ((bf16[8,288,128]{2,1,0:T(8,128)(2,1)}), bf16[8,288,128]{2,1,0:T(8,128)(2,1)S(1)}, u32[]{:S(2)}, u32[]{:S(2)}) async-start(bf16[8,288,128]{2,1,0:T(8,128)(2,1)} %broadcast_in_dim.16), calls=%async_computation | async-start | bytes 1179648 | tf_op jit(solution)/shard_map/all_to_all | solution.py:254
  23.6 26.9 %collective-permute-start.4 = (bf16[2048,128]{1,0:T(8,128)(2,1)S(1)}, bf16[2048,128]{1,0:T(8,128)(2,1)S(1)}, u32[]{:S(2)}, u32[]{:S(2)}) collective-permute-start(bf16[2048,128]{1,0:T(8,128)(2,1)S(1)} %get-tuple-element.10), channel_id=1, source_target_pairs={{0,64},{64,128},{128,192},{192,256},{256,320},{320,384},{384,448},... | collective-permute-start | bytes 1572872 | tf_op jit(solution)/shard_map/ppermute | solution.py:268
  27.9 23.8 %collective-permute-start.5 = (bf16[2048,128]{1,0:T(8,128)(2,1)S(1)}, bf16[2048,128]{1,0:T(8,128)(2,1)S(1)}, u32[]{:S(2)}, u32[]{:S(2)}) collective-permute-start(bf16[2048,128]{1,0:T(8,128)(2,1)S(1)} %get-tuple-element.11), channel_id=1, source_target_pairs={{0,704},{64,0},{128,64},{192,128},{256,192},{320,256},{384,320},{4... | collective-permute-start | bytes 1572872 | tf_op jit(solution)/shard_map/ppermute | solution.py:268
  51.7 11.8 %copy-start.2 = (bf16[384,128]{1,0:T(8,128)(2,1)S(1)}, bf16[384,128]{1,0:T(8,128)(2,1)}, u32[]{:S(2)}) copy-start(bf16[384,128]{1,0:T(8,128)(2,1)} %grad_ref.3) | copy-start | bytes 294916
  51.7 11.8 %copy-start.3 = (s32[16]{0:T(128)S(1)}, s32[16]{0:T(128)}, u32[]{:S(2)}) copy-start(s32[16]{0:T(128)} %blocks_ref.3) | copy-start | bytes 196
  52.7 23.7 %all-to-all-start.2 = ((bf16[8,256,128]{2,1,0:T(8,128)(2,1)}), bf16[8,256,128]{2,1,0:T(8,128)(2,1)S(1)}, u32[]{:S(2)}, u32[]{:S(2)}) async-start(bf16[8,256,128]{2,1,0:T(8,128)(2,1)} %bitcast.3), calls=%async_computation.2 | async-start | bytes 1048576 | tf_op jit(solution)/shard_map/all_to_all | solution.py:269
  59.6 3.9 %collective-permute-start = (bf16[2304,128]{1,0:T(8,128)(2,1)S(1)}, bf16[2304,128]{1,0:T(8,128)(2,1)S(1)}, u32[]{:S(2)}, u32[]{:S(2)}) collective-permute-start(bf16[2304,128]{1,0:T(8,128)(2,1)S(1)} %bitcast.9), channel_id=1, source_target_pairs={{0,4},{4,0},{8,12},{12,8},{16,20},{20,16},{24,28},{28,24},{32,36},... | collective-permute-start | bytes 1769480 | tf_op jit(solution)/shard_map/ppermute | solution.py:257
  76.4 17.4 %all-to-all-start.1 = ((bf16[4,1152,128]{2,1,0:T(8,128)(2,1)}), bf16[4,1152,128]{2,1,0:T(8,128)(2,1)S(1)}, u32[]{:S(2)}, u32[]{:S(2)}) async-start(bf16[4,1152,128]{2,1,0:T(8,128)(2,1)} %compact_rows.1), calls=%async_computation.1 | async-start | bytes 2359296 | tf_op jit(solution)/shard_map/all_to_all | solution.py:259
  93.7 16.0 %all-to-all-start.3 = ((bf16[4,64,128]{2,1,0:T(8,128)(2,1)}), bf16[4,64,128]{2,1,0:T(8,128)(2,1)S(1)}, u32[]{:S(2)}, u32[]{:S(2)}) async-start(bf16[4,64,128]{2,1,0:T(8,128)(2,1)} %bitcast.4), calls=%async_computation.3 | async-start | bytes 131072 | tf_op jit(solution)/shard_map/all_to_all | solution.py:273
  100.2 25.1 %collective-permute-start.2 = (bf16[4,768,128]{2,1,0:T(8,128)(2,1)}, bf16[4,768,128]{2,1,0:T(8,128)(2,1)S(1)}, u32[]{:S(2)}, u32[]{:S(2)}) collective-permute-start(bf16[4,768,128]{2,1,0:T(8,128)(2,1)} %slice.52), channel_id=1, source_target_pairs={{0,704},{64,0},{128,64},{192,128},{256,192},{320,256},{384,320},{4... | collective-permute-start | bytes 2359304 | tf_op jit(solution)/shard_map/ppermute | solution.py:262
  106.5 21.9 %collective-permute-start.1 = (bf16[4,768,128]{2,1,0:T(8,128)(2,1)}, bf16[4,768,128]{2,1,0:T(8,128)(2,1)S(1)}, u32[]{:S(2)}, u32[]{:S(2)}) collective-permute-start(bf16[4,768,128]{2,1,0:T(8,128)(2,1)} %slice.52), channel_id=1, source_target_pairs={{0,64},{64,128},{128,192},{192,256},{256,320},{320,384},{384,448},... | collective-permute-start | bytes 2359304 | tf_op jit(solution)/shard_map/ppermute | solution.py:261
  110.5 25.7 %all-to-all-start.4 = ((bf16[12,64,128]{2,1,0:T(8,128)(2,1)}), bf16[12,64,128]{2,1,0:T(8,128)(2,1)S(1)}, u32[]{:S(2)}, u32[]{:S(2)}) async-start(bf16[12,64,128]{2,1,0:T(8,128)(2,1)} %broadcast_in_dim.18), calls=%async_computation.4 | async-start | bytes 393216 | tf_op jit(solution)/shard_map/all_to_all | solution.py:277

commit v2 on v1

v2 whole, which is shorter than its diff:
```python
import functools

import jax
import jax.numpy as jnp
from jax import lax
from jax.experimental import pallas as pl
from jax.experimental.pallas import tpu as pltpu
from jax.sharding import PartitionSpec as P

BLOCK = 128
SPLIT = 3
PIECE = 48
PIECE_AT = (0, 48, 80)
SMALL = pltpu.CompilerParams(vmem_limit_bytes=12 * 1024 * 1024)


def fill_places(blocks_ref, place, slot_blocks, code):
    first = 0
    for owner in range(blocks_ref.shape[0]):
        for at in range(slot_blocks):
            place[first + at] = code(owner, at)
        first = first + blocks_ref[owner]


def grad_kernel(
    chunk, slot_blocks, counts_ref, blocks_ref, hidden_ref, grad_ref, send_ref, keep_ref, place, masked_t, chunks, sems
):
    steps = hidden_ref.shape[1] // chunk

    def load(step):
        return pltpu.make_async_copy(
            hidden_ref.at[:, pl.ds(step * chunk, chunk)], chunks.at[step], sems.at[step]
        )

    for step in range(steps):
        load(step).start()
    core = lax.rem(lax.axis_index("dp"), 2)
    turn = lax.rem(lax.axis_index("rep"), SPLIT)
    half = send_ref.shape[0]
    part_blocks = slot_blocks // SPLIT
    part_first = [lax.rem(part + SPLIT - turn, SPLIT) * (half // SPLIT) for part in range(SPLIT)]
    side = [jnp.where(core == parity, 0, half) for parity in range(2)]

    def code(owner, at):
        row = ((owner // 2) * part_blocks + at % part_blocks) * BLOCK
        return part_first[at // part_blocks] + side[owner % 2] + row

    fill_places(blocks_ref, place, slot_blocks, code)
    send_ref[...] = jnp.zeros_like(send_ref)
    keep_ref[...] = jnp.zeros_like(keep_ref)
    live = lax.broadcasted_iota(jnp.int32, grad_ref.shape, 0) < counts_ref[0]
    masked = jnp.where(live, grad_ref[...].astype(jnp.float32), 0.0)
    masked_t[...] = masked.T.astype(masked_t.dtype)

    def one(step, carry):
        load(step).wait()
        product = jnp.dot(masked_t[...], chunks[step], preferred_element_type=jnp.float32)
        for at in range(chunk // BLOCK):
            row = place[step * (chunk // BLOCK) + at]
            tile = product[:, at * BLOCK:(at + 1) * BLOCK].astype(send_ref.dtype)

            @pl.when(row < half)
            def _():
                keep_ref[pl.ds(pl.multiple_of(row, BLOCK), BLOCK), :] = tile

            @pl.when(row >= half)
            def _():
                send_ref[pl.ds(pl.multiple_of(row - half, BLOCK), BLOCK), :] = tile

        return carry

    lax.fori_loop(0, steps, one, 0)


def grad_products(counts, shard_blocks, hidden, grad, slot_rows):
    rows, width = hidden.shape
    owners = shard_blocks.shape[0]
    chunk = 1024
    steps = width // chunk
    half = (owners // 2) * slot_rows
    slot_blocks = slot_rows // BLOCK
    out = jax.ShapeDtypeStruct((half, grad.shape[1]), jnp.bfloat16)
    vmem = pl.BlockSpec(memory_space=pltpu.VMEM)
    return pl.pallas_call(
        functools.partial(grad_kernel, chunk, slot_blocks),
        in_specs=[
            pl.BlockSpec(memory_space=pltpu.SMEM),
            pl.BlockSpec(memory_space=pltpu.SMEM),
            pl.BlockSpec(memory_space=pltpu.HBM),
            vmem,
        ],
        out_specs=[vmem, vmem],
        out_shape=[out, out],
        scratch_shapes=[
            pltpu.SMEM((width // BLOCK + slot_blocks,), jnp.int32),
            pltpu.VMEM((grad.shape[1], rows), jnp.bfloat16),
            pltpu.VMEM((steps, rows, chunk), jnp.bfloat16),
            pltpu.SemaphoreType.DMA((steps,)),
        ],
        compiler_params=pltpu.CompilerParams(vmem_limit_bytes=59 * 1024 * 1024),
        cost_estimate=pl.CostEstimate(
            flops=2 * rows * width * grad.shape[1], bytes_accessed=2 * rows * width + 4 * half * 128, transcendentals=0
        ),
        name="grad_products",
    )(counts, shard_blocks, hidden, grad)


def pair_kernel(keep_ref, received_ref, *outs):
    rows = outs[0].shape[0]
    for k, out in enumerate(outs):
        here = pl.ds(k * rows, rows)
        total = keep_ref[here, :].astype(jnp.float32) + received_ref[here, :].astype(jnp.float32)
        out[...] = total.astype(out.dtype)


def paired_parts(keep, received):
    out = jax.ShapeDtypeStruct((keep.shape[0] // SPLIT, keep.shape[1]), keep.dtype)
    return pl.pallas_call(pair_kernel, out_shape=[out] * SPLIT, compiler_params=SMALL, name="pair_parts")(keep, received)


def summed(parts):
    total = parts[0].astype(jnp.float32)
    for part in parts[1:]:
        total = total + part.astype(jnp.float32)
    return total.astype(parts[0].dtype)


def finish_kernel(share, total_ref, out_ref):
    n_rep = total_ref.shape[0] // share
    per = out_ref.shape[0] // SPLIT
    rows = [None] * (out_ref.shape[0] // share)
    for rep in range(n_rep):
        first = (rep % SPLIT) * per + (rep // SPLIT) * share
        rows[first // share] = total_ref[rep * share:(rep + 1) * share, :].astype(out_ref.dtype)
    slot = jnp.concatenate(rows, axis=0)
    for at in range(out_ref.shape[0] // BLOCK):
        out_ref[at * BLOCK:(at + 1) * BLOCK, :] = slot[at * BLOCK:(at + 1) * BLOCK, :].T


def finished(total, share):
    return pl.pallas_call(
        functools.partial(finish_kernel, share),
        out_shape=jax.ShapeDtypeStruct(total.shape, jnp.float32),
        compiler_params=SMALL,
        name="finish_weight_grad",
    )(total)


def compact_kernel(slot_blocks, n_tp, blocks_ref, held_ref, grad_ref, *rest):
    outs, place = rest[:n_tp], rest[n_tp]
    index = lax.axis_index("tp")
    half = held_ref.shape[0] // 2
    fill_places(
        blocks_ref, place, slot_blocks,
        lambda owner, at: (owner % 2) * half + ((owner // 2) * slot_blocks + at) * PIECE,
    )
    per = (outs[0].shape[0] - grad_ref.shape[0]) // PIECE
    for k, out_ref in enumerate(outs):
        first = lax.rem(index + k, n_tp) * per
        for at in range(per):
            source = pl.multiple_of(place[first + at], 16)
            out_ref[at * PIECE:(at + 1) * PIECE, :] = held_ref[pl.ds(source, PIECE), :]
        out_ref[per * PIECE:, :] = grad_ref[...]


def compacted(shard_blocks, held, grad, slot_rows, n_tp, width):
    n_blocks = width // BLOCK
    slot_blocks = slot_rows // BLOCK
    rows = n_blocks // n_tp * PIECE + grad.shape[0]
    vmem = pl.BlockSpec(memory_space=pltpu.VMEM)
    return pl.pallas_call(
        functools.partial(compact_kernel, slot_blocks, n_tp),
        in_specs=[pl.BlockSpec(memory_space=pltpu.SMEM), vmem, vmem],
        out_specs=[vmem] * n_tp,
        out_shape=[jax.ShapeDtypeStruct((rows, grad.shape[1]), grad.dtype)] * n_tp,
        scratch_shapes=[pltpu.SMEM((n_blocks + slot_blocks,), jnp.int32)],
        compiler_params=SMALL,
        cost_estimate=pl.CostEstimate(flops=0, bytes_accessed=2 * rows * grad.shape[1], transcendentals=0),
        name="compact_rows",
    )(shard_blocks, held.reshape(-1, held.shape[-1]), grad)


def input_kernel(heads, counts_ref, *refs):
    own, (before_ref, after_ref), grads = refs[:heads], refs[heads:heads + 2], refs[heads + 2:2 * heads + 2]
    out_ref, masked, weight = refs[2 * heads + 2:]
    step = pl.program_id(0)
    turn = lax.rem(lax.axis_index("rep"), SPLIT)
    blocks = before_ref.shape[1] // PIECE

    @pl.when(step == 0)
    def _():
        for h in range(heads):
            grad = grads[h][...].astype(jnp.float32)
            live = lax.broadcasted_iota(jnp.int32, grad.shape, 0) < counts_ref[0]
            masked[:, h * BLOCK:(h + 1) * BLOCK] = jnp.where(live, grad, 0.0).astype(masked.dtype)

    for piece_here in range(SPLIT):
        @pl.when(turn == piece_here)
        def _():
            for shift in range(SPLIT):
                first = PIECE_AT[(piece_here + shift) % SPLIT]
                for h in range(heads):
                    ref = (own[h], after_ref.at[h], before_ref.at[h])[shift]
                    for b in range(blocks):
                        weight[b * BLOCK + first:b * BLOCK + first + PIECE, h * BLOCK:(h + 1) * BLOCK] = ref[
                            b * PIECE:(b + 1) * PIECE, :
                        ]

    out_ref[...] = lax.dot_general(
        masked[...], weight[...], (((1,), (1,)), ((), ())), preferred_element_type=jnp.float32
    ).astype(out_ref.dtype)


def input_product(counts, own, before, after, rows_dev):
    n_tp, pieces, head = before.shape
    steps = 4
    blocks = pieces // PIECE // steps
    chunk = blocks * BLOCK
    return pl.pallas_call(
        functools.partial(input_kernel, n_tp),
        grid=(steps,),
        in_specs=[pl.BlockSpec(memory_space=pltpu.SMEM)]
        + [pl.BlockSpec((blocks * PIECE, head), lambda i: (i, 0))] * n_tp
        + [pl.BlockSpec((n_tp, blocks * PIECE, head), lambda i: (0, i, 0))] * 2
        + [pl.BlockSpec((rows_dev, head), lambda i: (pieces // rows_dev, 0))] * n_tp,
        out_specs=pl.BlockSpec((rows_dev, chunk), lambda i: (0, i)),
        out_shape=jax.ShapeDtypeStruct((rows_dev, steps * chunk), jnp.bfloat16),
        scratch_shapes=[
            pltpu.VMEM((rows_dev, head * n_tp), jnp.bfloat16),
            pltpu.VMEM((chunk, head * n_tp), jnp.bfloat16),
        ],
        compiler_params=pltpu.CompilerParams(vmem_limit_bytes=16 * 1024 * 1024),
        cost_estimate=pl.CostEstimate(
            flops=2 * rows_dev * steps * chunk * head * n_tp,
            bytes_accessed=2 * steps * chunk * (head * n_tp + rows_dev),
            transcendentals=0,
        ),
        name="input_grad",
    )(counts, *own, before, after, *own)


def ordered(array, other):
    return lax.optimization_barrier((array, other))[0]


def on_device(hidden_in, value_grad, weight_shards, shard_blocks, token_counts):
    rows_dev, width = hidden_in.shape
    slot_rows, head = weight_shards.shape
    n_dp, n_tp, n_rep = lax.axis_size("dp"), lax.axis_size("tp"), lax.axis_size("rep")
    n_y = n_dp // 2
    slot_blocks = slot_rows // BLOCK
    core_swap = [(i, i ^ 1) for i in range(n_dp)]
    along_y = [[c + 2 * y for y in range(n_y)] for c in range(2)]
    up = [(i, (i + 1) % n_rep) for i in range(n_rep)]
    down = [(i, (i - 1) % n_rep) for i in range(n_rep)]

    turn = lax.rem(lax.axis_index("rep"), SPLIT)
    first = turn * PIECE_AT[1] - jnp.where(turn == 2, 2 * PIECE_AT[1] - PIECE_AT[2], 0)
    piece = lax.dynamic_slice_in_dim(weight_shards.reshape(slot_blocks, BLOCK, head), first, PIECE, 1)
    piece = piece.reshape(1, slot_blocks * PIECE, head)
    held = lax.all_to_all(
        jnp.broadcast_to(piece, (n_y,) + piece.shape[1:]), "dp", 0, 0, axis_index_groups=along_y
    ).reshape(n_y * slot_blocks * PIECE, head)
    send, keep = grad_products(token_counts, shard_blocks, hidden_in, value_grad, slot_rows)
    received = lax.ppermute(send, "dp", core_swap)
    stay, to_next, to_last = paired_parts(keep, received)

    pair = [[2 * y, 2 * y + 1] for y in range(n_y)]
    held = lax.all_to_all(jnp.broadcast_to(held[None], (2,) + held.shape), "dp", 0, 0, axis_index_groups=pair)
    sent = compacted(shard_blocks, held, value_grad, slot_rows, n_tp, width)
    own = [sent[0]] + [
        lax.ppermute(sent[k], "tp", [(i, (i + k) % n_tp) for i in range(n_tp)]) for k in range(1, n_tp)
    ]
    pieces = jnp.stack([part[: part.shape[0] - rows_dev] for part in own])
    before = lax.ppermute(pieces, "rep", up)
    after = lax.ppermute(pieces, "rep", down)
    input_grad = input_product(token_counts, own, before, after, rows_dev)

    stay = ordered(stay, sent[0])
    part = summed([stay, lax.ppermute(to_next, "rep", up), lax.ppermute(to_last, "rep", down)])
    spread = lax.all_to_all(part.reshape(n_y, slot_rows // SPLIT, head), "dp", 0, 0, axis_index_groups=along_y)
    owned = summed([spread[y] for y in range(n_y)])
    fellows = [[k + SPLIT * q for q in range(n_rep // SPLIT)] for k in range(SPLIT)]
    share_rows = slot_rows // n_rep
    shares = lax.all_to_all(
        owned.reshape(n_rep // SPLIT, share_rows, head), "rep", 0, 0, axis_index_groups=fellows
    )
    share = summed([shares[q] for q in range(n_rep // SPLIT)])
    total = lax.all_to_all(jnp.broadcast_to(share[None], (n_rep,) + share.shape), "rep", 0, 0)
    weight_grad = finished(total.reshape(slot_rows, head), share_rows)
    return (input_grad, weight_grad)


def solution(mesh):
    placed = (P(("rep", "dp"), None), P(("rep", "dp"), "tp"), P("dp", "tp"), P(), P(("rep", "dp")))
    return jax.shard_map(
        on_device,
        mesh=mesh,
        in_specs=placed,
        out_specs=(P(("rep", "dp"), "tp"), P("dp", "tp")),
        check_vma=False,
    )
```

time: 139 us -> 131 us (0.942)
  waiting for transfers between devices: 49.6 us -> 35.3 us
  starting transfers between devices: 61.5 us -> 68.5 us
  Pallas kernels: 20.3 us -> 13.5 us
  blocking collectives: 0 us -> 4.81 us
    all_to_all x1 -> x0, waiting for transfers between devices: 11.9 us -> none  [on_device(): own = lax.all_to_all(sent, 'tp', 0, 0)]
    ppermute x1 -> x3, starting transfers between devices: 1.91 us -> 13.3 us  [on_device(): lax.ppermute(sent[k], 'tp', [(i, (i + k) % n_tp) for i in range(n_tp)])]
    ppermute x1, waiting for transfers between devices: 10.4 us -> 0.01 us  [on_device(): lax.ppermute(to_next, 'rep', up)]
    ppermute x1 -> x3, waiting for transfers between devices: 1.97 us -> 9.18 us  [on_device(): lax.ppermute(sent[k], 'tp', [(i, (i + k) % n_tp) for i in range(n_tp)])]
    pallas_call x3, Pallas kernels: 17.6 us -> 11.3 us  [the longest x1 7.27 us: grad_products(): pl.pallas_call(functools.partial(grad_kernel, chunk, slot_blocks), in_spe...]
    all_to_all x1, starting transfers between devices: 5.56 us -> 10.4 us  [on_device(): lax.all_to_all(owned.reshape(n_rep // SPLIT, share_rows, head), 'rep', 0,...]
    all_to_all x0 -> x1, blocking collectives: none -> 4.81 us  [on_device(): lax.all_to_all(jnp.broadcast_to(held[None], (2,) + held.shape), 'dp', 0,...]
    all_to_all x1 -> x0, starting transfers between devices: 4.76 us -> none  [on_device(): own = lax.all_to_all(sent, 'tp', 0, 0)]
  transfers between devices with their start and end apart: 11 -> 12, of which waited for: 9 -> 8; matrix products, arithmetic and copies ran while one was open for 3% -> 4% of each run, Pallas kernels for 7% -> 4%
where the time goes in v2:
time: 131 us; the launch traced here: 130 us
  starting transfers between devices  68.5 us (52%)
  waiting for transfers between devices  35.3 us (27%)
  Pallas kernels  13.5 us (10%)
  blocking collectives  4.81 us (4%)
  local copies, waits for them, and re-layouts  3.75 us (3%)
  other arithmetic  2.7 us (2%)
  between operations  1.57 us (1%)
    ppermute x3, starting transfers between devices, on_device(): lax.ppermute(sent[k], 'tp', [(i, (i + k) % n_tp) for i in range(n_tp)])  13.3 us
    ppermute x1, starting transfers between devices, on_device(): lax.ppermute(to_last, 'rep', down)  12.2 us
    ppermute x1, waiting for transfers between devices, on_device(): after = lax.ppermute(pieces, 'rep', down)  10.5 us
    all_to_all x1, starting transfers between devices, on_device(): lax.all_to_all(owned.reshape(n_rep // SPLIT, share_rows, head), 'rep', 0,...  10.4 us
    ppermute x3, waiting for transfers between devices, on_device(): lax.ppermute(sent[k], 'tp', [(i, (i + k) % n_tp) for i in range(n_tp)])  9.18 us
    all_to_all x1, starting transfers between devices, on_device(): lax.all_to_all(jnp.broadcast_to(share[None], (n_rep,) + share.shape), 're...  7.35 us
    pallas_call x1, Pallas kernels, grad_products(): pl.pallas_call(functools.partial(grad_kernel, chunk, slot_blocks), in_spe...  7.27 us
    all_to_all x1, starting transfers between devices, on_device(): lax.all_to_all(jnp.broadcast_to(piece, (n_y,) + piece.shape[1:]), 'dp', 0...  7.08 us
  transfers between devices with their start and end apart: 12, of which 8 were waited for; matrix products, arithmetic and copies ran while one was open for 4% of the time, Pallas kernels for 4%

profile of v2, /device:TPU:6, one launch (start us, length us, event | category | flops | bytes accessed | tf_op | source)
XLA Modules:
  0.0 130.1 jit_solution(4444493653833834509)
XLA Ops:
  1.3 7.3 %grad_products.1 = (bf16[6144,128]{1,0:T(8,128)(2,1)}, bf16[6144,128]{1,0:T(8,128)(2,1)}) custom-call(s32[1]{0:T(128)S(6)} %copy.7.counts_ref, s32[16]{0:T(128)} %blocks_ref.3, bf16[384,8192]{1,0:T(8,128)(2,1)} %hidden_ref.1, bf16[384,128]{1,0:T(8,128)(2,1)} %grad_ref.3), custom_call_target="tpu_custom_call" | custom-call | flops 805306368 | bytes 9437184 | tf_op jit(solution)/shard_map/grad_products/pallas_call | solution.py:84
  8.6 2.1 %collective-permute-start.5 = (bf16[6144,128]{1,0:T(8,128)(2,1)}, bf16[6144,128]{1,0:T(8,128)(2,1)S(1)}, u32[]{:S(2)}, u32[]{:S(2)}) collective-permute-start(bf16[6144,128]{1,0:T(8,128)(2,1)} %get-tuple-element.17), channel_id=1, source_target_pairs={{0,4},{4,0},{8,12},{12,8},{16,20},{20,16},{24,28},{28,24},{32,36},... | collective-permute-start | bytes 4718600 | tf_op jit(solution)/shard_map/ppermute | solution.py:265
  11.6 7.1 %all-to-all-start = ((bf16[8,288,128]{2,1,0:T(8,128)(2,1)}), bf16[8,288,128]{2,1,0:T(8,128)(2,1)}, u32[]{:S(2)}, u32[]{:S(2)}) async-start(bf16[8,288,128]{2,1,0:T(8,128)(2,1)} %broadcast_in_dim.23), calls=%async_computation | async-start | bytes 1179648 | tf_op jit(solution)/shard_map/all_to_all | solution.py:261
  18.7 1.3 pair_parts.1
  20.8 4.3 %collective-permute-start.6 = (bf16[2048,128]{1,0:T(8,128)(2,1)}, bf16[2048,128]{1,0:T(8,128)(2,1)S(1)}, u32[]{:S(2)}, u32[]{:S(2)}) collective-permute-start(bf16[2048,128]{1,0:T(8,128)(2,1)} %get-tuple-element.20), channel_id=1, source_target_pairs={{0,64},{64,128},{128,192},{192,256},{256,320},{320,384},{384,448},... | collective-permute-start | bytes 1572872 | tf_op jit(solution)/shard_map/ppermute | solution.py:280
  25.1 12.2 %collective-permute-start.7 = (bf16[2048,128]{1,0:T(8,128)(2,1)}, bf16[2048,128]{1,0:T(8,128)(2,1)S(1)}, u32[]{:S(2)}, u32[]{:S(2)}) collective-permute-start(bf16[2048,128]{1,0:T(8,128)(2,1)} %get-tuple-element.21), channel_id=1, source_target_pairs={{0,704},{64,0},{128,64},{192,128},{256,192},{320,256},{384,320},{4... | collective-permute-start | bytes 1572872 | tf_op jit(solution)/shard_map/ppermute | solution.py:280
  38.4 1.2 broadcast_in_dim.25
  39.7 4.8 %all_to_all.25 = bf16[2,2304,128]{2,1,0:T(8,128)(2,1)S(1)} all-to-all(bf16[2,2304,128]{2,1,0:T(8,128)(2,1)S(1)} %broadcast_in_dim.25), channel_id=1, replica_groups={{0,4},{8,12},{16,20},{24,28},{32,36},{40,44},{48,52},{56,60},{1,5},{9,1..., dimensions={0} | all-to-all | bytes 2359296 | tf_op jit(solution)/shard_map/all_to_all | solution.py:269
  45.2 8.7 %collective-permute-start = (bf16[1152,128]{1,0:T(8,128)(2,1)S(1)}, bf16[1152,128]{1,0:T(8,128)(2,1)S(1)}, u32[]{:S(2)}, u32[]{:S(2)}) collective-permute-start(bf16[1152,128]{1,0:T(8,128)(2,1)S(1)} %get-tuple-element.13), channel_id=1, source_target_pairs={{0,1},{1,2},{2,3},{3,0},{4,5},{5,6},{6,7},{7,4},{8,9},{9,10},{10,1... | collective-permute-start | bytes 884744 | tf_op jit(solution)/shard_map/ppermute | solution.py:272
  53.9 1.9 %collective-permute-start.1 = (bf16[1152,128]{1,0:T(8,128)(2,1)S(1)}, bf16[1152,128]{1,0:T(8,128)(2,1)S(1)}, u32[]{:S(2)}, u32[]{:S(2)}) collective-permute-start(bf16[1152,128]{1,0:T(8,128)(2,1)S(1)} %get-tuple-element.14), channel_id=1, source_target_pairs={{0,2},{1,3},{2,0},{3,1},{4,6},{5,7},{6,4},{7,5},{8,10},{9,11},{10,... | collective-permute-start | bytes 884744 | tf_op jit(solution)/shard_map/ppermute | solution.py:272
  56.9 3.5 %all-to-all-start.2 = ((bf16[8,256,128]{2,1,0:T(8,128)(2,1)}), bf16[8,256,128]{2,1,0:T(8,128)(2,1)S(1)}, u32[]{:S(2)}, u32[]{:S(2)}) async-start(bf16[8,256,128]{2,1,0:T(8,128)(2,1)} %bitcast.8), calls=%async_computation.2 | async-start | bytes 1048576 | tf_op jit(solution)/shard_map/all_to_all | solution.py:281
  60.4 2.8 %collective-permute-start.2 = (bf16[1152,128]{1,0:T(8,128)(2,1)S(1)}, bf16[1152,128]{1,0:T(8,128)(2,1)S(1)}, u32[]{:S(2)}, u32[]{:S(2)}) collective-permute-start(bf16[1152,128]{1,0:T(8,128)(2,1)S(1)} %get-tuple-element.15), channel_id=1, source_target_pairs={{0,3},{1,0},{2,1},{3,2},{4,7},{5,4},{6,5},{7,6},{8,11},{9,8},{10,9... | collective-permute-start | bytes 884744 | tf_op jit(solution)/shard_map/ppermute | solution.py:272
  63.2 3.6 %collective-permute-done.refs_1_.refs_7_ = bf16[1152,128]{1,0:T(8,128)(2,1)S(1)} collective-permute-done((bf16[1152,128]{1,0:T(8,128)(2,1)S(1)}, bf16[1152,128]{1,0:T(8,128)(2,1)S(1)}, u32[]{:S(2)}, u32[]{:S(2)}) %collective-permute-start) | collective-permute-done | bytes 294944 | tf_op jit(solution)/shard_map/ppermute | solution.py:272
  66.8 5.6 %collective-permute-done.2.refs_3_.refs_9_ = bf16[1152,128]{1,0:T(8,128)(2,1)S(1)} collective-permute-done((bf16[1152,128]{1,0:T(8,128)(2,1)S(1)}, bf16[1152,128]{1,0:T(8,128)(2,1)S(1)}, u32[]{:S(2)}, u32[]{:S(2)}) %collective-permute-start.2) | collective-permute-done | bytes 294944 | tf_op jit(solution)/shard_map/ppermute | solution.py:272
  72.4 5.7 %all-to-all-done.2 = bf16[8,256,128]{2,1,0:T(8,128)(2,1)S(1)} async-done(((bf16[8,256,128]{2,1,0:T(8,128)(2,1)}), bf16[8,256,128]{2,1,0:T(8,128)(2,1)S(1)}, u32[]{:S(2)}, u32[]{:S(2)}) %all-to-all-start.2) | async-done | bytes 524320 | tf_op jit(solution)/shard_map/all_to_all | solution.py:281
  78.8 10.4 %all-to-all-start.3 = ((bf16[4,64,128]{2,1,0:T(8,128)(2,1)}), bf16[4,64,128]{2,1,0:T(8,128)(2,1)S(1)}, u32[]{:S(2)}, u32[]{:S(2)}) async-start(bf16[4,64,128]{2,1,0:T(8,128)(2,1)} %bitcast.9), calls=%async_computation.3 | async-start | bytes 131072 | tf_op jit(solution)/shard_map/all_to_all | solution.py:285
  90.1 6.3 %collective-permute-start.4 = (bf16[4,768,128]{2,1,0:T(8,128)(2,1)}, bf16[4,768,128]{2,1,0:T(8,128)(2,1)S(1)}, u32[]{:S(2)}, u32[]{:S(2)}) collective-permute-start(bf16[4,768,128]{2,1,0:T(8,128)(2,1)} %pad_maximum_fusion), channel_id=1, source_target_pairs={{0,704},{64,0},{128,64},{192,128},{256,192},{320,256},{384,320},{4... | collective-permute-start | bytes 2359304 | tf_op jit(solution)/shard_map/ppermute | solution.py:276
  96.5 1.9 %collective-permute-start.3 = (bf16[4,768,128]{2,1,0:T(8,128)(2,1)}, bf16[4,768,128]{2,1,0:T(8,128)(2,1)S(1)}, u32[]{:S(2)}, u32[]{:S(2)}) collective-permute-start(bf16[4,768,128]{2,1,0:T(8,128)(2,1)} %pad_maximum_fusion), channel_id=1, source_target_pairs={{0,64},{64,128},{128,192},{192,256},{256,320},{320,384},{384,448},... | collective-permute-start | bytes 2359304 | tf_op jit(solution)/shard_map/ppermute | solution.py:275
  98.4 1.7 %all-to-all-done.3 = bf16[4,64,128]{2,1,0:T(8,128)(2,1)S(1)} async-done(((bf16[4,64,128]{2,1,0:T(8,128)(2,1)}), bf16[4,64,128]{2,1,0:T(8,128)(2,1)S(1)}, u32[]{:S(2)}, u32[]{:S(2)}) %all-to-all-start.3) | async-done | bytes 65568 | tf_op jit(solution)/shard_map/all_to_all | solution.py:285
  100.8 7.3 %all-to-all-start.4 = ((bf16[12,64,128]{2,1,0:T(8,128)(2,1)}), bf16[12,64,128]{2,1,0:T(8,128)(2,1)S(1)}, u32[]{:S(2)}, u32[]{:S(2)}) async-start(bf16[12,64,128]{2,1,0:T(8,128)(2,1)} %broadcast_in_dim.27), calls=%async_computation.4 | async-start | bytes 393216 | tf_op jit(solution)/shard_map/all_to_all | solution.py:289
  108.2 10.5 %collective-permute-done.4.refs_5_ = bf16[4,768,128]{2,1,0:T(8,128)(2,1)S(1)} collective-permute-done((bf16[4,768,128]{2,1,0:T(8,128)(2,1)}, bf16[4,768,128]{2,1,0:T(8,128)(2,1)S(1)}, u32[]{:S(2)}, u32[]{:S(2)}) %collective-permute-start.4) | collective-permute-done | bytes 786464 | tf_op jit(solution)/shard_map/ppermute | solution.py:276
  118.7 4.0 %collective-permute-done.3.refs_4_ = bf16[4,768,128]{2,1,0:T(8,128)(2,1)S(1)} collective-permute-done((bf16[4,768,128]{2,1,0:T(8,128)(2,1)}, bf16[4,768,128]{2,1,0:T(8,128)(2,1)S(1)}, u32[]{:S(2)}, u32[]{:S(2)}) %collective-permute-start.3) | collective-permute-done | bytes 786464 | tf_op jit(solution)/shard_map/ppermute | solution.py:275
  122.6 3.4 %input_grad.1 = bf16[384,2048]{1,0:T(8,128)(2,1)} custom-call(s32[1]{0:T(128)S(6)} %copy.7.counts_ref, bf16[1152,128]{1,0:T(8,128)(2,1)S(1)} %get-tuple-element.12.refs_0_.refs_6_, bf16[1152,128]{1,0:T(8,128)(2,1)S(1)} %collective-permute-done.refs_1_.refs_7_, bf16[1152,128]{1,0:T(8,128)(2,1)S(1)} %collective-permute-done.1.refs_2_.refs_8_, ...), custom_call_target="tpu_custom_call" | custom-call | flops 805306368 | bytes 3670016 | tf_op jit(solution)/shard_map/input_grad/pallas_call | solution.py:219
  126.0 3.2 %all-to-all-done.4 = bf16[12,64,128]{2,1,0:T(8,128)(2,1)S(1)} async-done(((bf16[12,64,128]{2,1,0:T(8,128)(2,1)}), bf16[12,64,128]{2,1,0:T(8,128)(2,1)S(1)}, u32[]{:S(2)}, u32[]{:S(2)}) %all-to-all-start.4) | async-done | bytes 196640 | tf_op jit(solution)/shard_map/all_to_all | solution.py:289
  (30 shorter events, 7.9 us)
Async XLA Ops:
  0.6 10.1 %copy-start = (bf16[768,128]{1,0:T(8,128)(2,1)S(1)}, bf16[768,128]{1,0:T(8,128)(2,1)}, u32[]{:S(2)}) copy-start(bf16[768,128]{1,0:T(8,128)(2,1)} %param.7) | copy-start | bytes 589828
  8.6 10.1 %copy-start.1 = (bf16[6144,128]{1,0:T(8,128)(2,1)S(1)}, bf16[6144,128]{1,0:T(8,128)(2,1)}, u32[]{:S(2)}) copy-start(bf16[6144,128]{1,0:T(8,128)(2,1)} %get-tuple-element.16.keep_ref) | copy-start | bytes 4718596
  8.6 10.1 %collective-permute-start.5 = (bf16[6144,128]{1,0:T(8,128)(2,1)}, bf16[6144,128]{1,0:T(8,128)(2,1)S(1)}, u32[]{:S(2)}, u32[]{:S(2)}) collective-permute-start(bf16[6144,128]{1,0:T(8,128)(2,1)} %get-tuple-element.17), channel_id=1, source_target_pairs={{0,4},{4,0},{8,12},{12,8},{16,20},{20,16},{24,28},{28,24},{32,36},... | collective-permute-start | bytes 4718600 | tf_op jit(solution)/shard_map/ppermute | solution.py:265
  11.6 26.8 %all-to-all-start = ((bf16[8,288,128]{2,1,0:T(8,128)(2,1)}), bf16[8,288,128]{2,1,0:T(8,128)(2,1)}, u32[]{:S(2)}, u32[]{:S(2)}) async-start(bf16[8,288,128]{2,1,0:T(8,128)(2,1)} %broadcast_in_dim.23), calls=%async_computation | async-start | bytes 1179648 | tf_op jit(solution)/shard_map/all_to_all | solution.py:261
  20.0 0.8 copy-start.2
  20.8 35.0 %collective-permute-start.6 = (bf16[2048,128]{1,0:T(8,128)(2,1)}, bf16[2048,128]{1,0:T(8,128)(2,1)S(1)}, u32[]{:S(2)}, u32[]{:S(2)}) collective-permute-start(bf16[2048,128]{1,0:T(8,128)(2,1)} %get-tuple-element.20), channel_id=1, source_target_pairs={{0,64},{64,128},{128,192},{192,256},{256,320},{320,384},{384,448},... | collective-permute-start | bytes 1572872 | tf_op jit(solution)/shard_map/ppermute | solution.py:280
  25.1 30.7 %collective-permute-start.7 = (bf16[2048,128]{1,0:T(8,128)(2,1)}, bf16[2048,128]{1,0:T(8,128)(2,1)S(1)}, u32[]{:S(2)}, u32[]{:S(2)}) collective-permute-start(bf16[2048,128]{1,0:T(8,128)(2,1)} %get-tuple-element.21), channel_id=1, source_target_pairs={{0,704},{64,0},{128,64},{192,128},{256,192},{320,256},{384,320},{4... | collective-permute-start | bytes 1572872 | tf_op jit(solution)/shard_map/ppermute | solution.py:280
  39.7 4.8 %copy-start.4 = (bf16[384,128]{1,0:T(8,128)(2,1)S(1)}, bf16[384,128]{1,0:T(8,128)(2,1)}, u32[]{:S(2)}) copy-start(bf16[384,128]{1,0:T(8,128)(2,1)} %grad_ref.3) | copy-start | bytes 294916
  39.7 4.8 %copy-start.5 = (s32[16]{0:T(128)S(1)}, s32[16]{0:T(128)}, u32[]{:S(2)}) copy-start(s32[16]{0:T(128)} %blocks_ref.3) | copy-start | bytes 196
  39.7 16.2 %copy-start.3 = (bf16[2048,128]{1,0:T(8,128)(2,1)S(1)}, bf16[2048,128]{1,0:T(8,128)(2,1)}, u32[]{:S(2)}) copy-start(bf16[2048,128]{1,0:T(8,128)(2,1)} %copy-done.2) | copy-start | bytes 1572868
  45.2 21.5 %collective-permute-start = (bf16[1152,128]{1,0:T(8,128)(2,1)S(1)}, bf16[1152,128]{1,0:T(8,128)(2,1)S(1)}, u32[]{:S(2)}, u32[]{:S(2)}) collective-permute-start(bf16[1152,128]{1,0:T(8,128)(2,1)S(1)} %get-tuple-element.13), channel_id=1, source_target_pairs={{0,1},{1,2},{2,3},{3,0},{4,5},{5,6},{6,7},{7,4},{8,9},{9,10},{10,1... | collective-permute-start | bytes 884744 | tf_op jit(solution)/shard_map/ppermute | solution.py:272
  53.9 12.9 %collective-permute-start.1 = (bf16[1152,128]{1,0:T(8,128)(2,1)S(1)}, bf16[1152,128]{1,0:T(8,128)(2,1)S(1)}, u32[]{:S(2)}, u32[]{:S(2)}) collective-permute-start(bf16[1152,128]{1,0:T(8,128)(2,1)S(1)} %get-tuple-element.14), channel_id=1, source_target_pairs={{0,2},{1,3},{2,0},{3,1},{4,6},{5,7},{6,4},{7,5},{8,10},{9,11},{10,... | collective-permute-start | bytes 884744 | tf_op jit(solution)/shard_map/ppermute | solution.py:272
  56.9 21.2 %all-to-all-start.2 = ((bf16[8,256,128]{2,1,0:T(8,128)(2,1)}), bf16[8,256,128]{2,1,0:T(8,128)(2,1)S(1)}, u32[]{:S(2)}, u32[]{:S(2)}) async-start(bf16[8,256,128]{2,1,0:T(8,128)(2,1)} %bitcast.8), calls=%async_computation.2 | async-start | bytes 1048576 | tf_op jit(solution)/shard_map/all_to_all | solution.py:281
  60.4 12.0 %collective-permute-start.2 = (bf16[1152,128]{1,0:T(8,128)(2,1)S(1)}, bf16[1152,128]{1,0:T(8,128)(2,1)S(1)}, u32[]{:S(2)}, u32[]{:S(2)}) collective-permute-start(bf16[1152,128]{1,0:T(8,128)(2,1)S(1)} %get-tuple-element.15), channel_id=1, source_target_pairs={{0,3},{1,0},{2,1},{3,2},{4,7},{5,4},{6,5},{7,6},{8,11},{9,8},{10,9... | collective-permute-start | bytes 884744 | tf_op jit(solution)/shard_map/ppermute | solution.py:272
  78.8 21.3 %all-to-all-start.3 = ((bf16[4,64,128]{2,1,0:T(8,128)(2,1)}), bf16[4,64,128]{2,1,0:T(8,128)(2,1)S(1)}, u32[]{:S(2)}, u32[]{:S(2)}) async-start(bf16[4,64,128]{2,1,0:T(8,128)(2,1)} %bitcast.9), calls=%async_computation.3 | async-start | bytes 131072 | tf_op jit(solution)/shard_map/all_to_all | solution.py:285
  90.1 28.5 %collective-permute-start.4 = (bf16[4,768,128]{2,1,0:T(8,128)(2,1)}, bf16[4,768,128]{2,1,0:T(8,128)(2,1)S(1)}, u32[]{:S(2)}, u32[]{:S(2)}) collective-permute-start(bf16[4,768,128]{2,1,0:T(8,128)(2,1)} %pad_maximum_fusion), channel_id=1, source_target_pairs={{0,704},{64,0},{128,64},{192,128},{256,192},{320,256},{384,320},{4... | collective-permute-start | bytes 2359304 | tf_op jit(solution)/shard_map/ppermute | solution.py:276
  96.5 26.2 %collective-permute-start.3 = (bf16[4,768,128]{2,1,0:T(8,128)(2,1)}, bf16[4,768,128]{2,1,0:T(8,128)(2,1)S(1)}, u32[]{:S(2)}, u32[]{:S(2)}) collective-permute-start(bf16[4,768,128]{2,1,0:T(8,128)(2,1)} %pad_maximum_fusion), channel_id=1, source_target_pairs={{0,64},{64,128},{128,192},{192,256},{256,320},{320,384},{384,448},... | collective-permute-start | bytes 2359304 | tf_op jit(solution)/shard_map/ppermute | solution.py:275
  100.8 28.4 %all-to-all-start.4 = ((bf16[12,64,128]{2,1,0:T(8,128)(2,1)}), bf16[12,64,128]{2,1,0:T(8,128)(2,1)S(1)}, u32[]{:S(2)}, u32[]{:S(2)}) async-start(bf16[12,64,128]{2,1,0:T(8,128)(2,1)} %broadcast_in_dim.27), calls=%async_computation.4 | async-start | bytes 393216 | tf_op jit(solution)/shard_map/all_to_all | solution.py:289

commit v3 on v2

--- a/solution.py
+++ b/solution.py
@@ -9,8 +9,6 @@
 
 BLOCK = 128
 SPLIT = 3
-PIECE = 48
-PIECE_AT = (0, 48, 80)
 SMALL = pltpu.CompilerParams(vmem_limit_bytes=12 * 1024 * 1024)
 
 
@@ -146,101 +144,71 @@
     )(total)
 
 
-def compact_kernel(slot_blocks, n_tp, blocks_ref, held_ref, grad_ref, *rest):
+def compact_kernel(slot_blocks, n_tp, blocks_ref, gathered_ref, grad_ref, *rest):
     outs, place = rest[:n_tp], rest[n_tp]
     index = lax.axis_index("tp")
-    half = held_ref.shape[0] // 2
-    fill_places(
-        blocks_ref, place, slot_blocks,
-        lambda owner, at: (owner % 2) * half + ((owner // 2) * slot_blocks + at) * PIECE,
-    )
-    per = (outs[0].shape[0] - grad_ref.shape[0]) // PIECE
+    fill_places(blocks_ref, place, slot_blocks, lambda owner, at: (owner * slot_blocks + at) * BLOCK)
+    per = (outs[0].shape[0] - grad_ref.shape[0]) // BLOCK
     for k, out_ref in enumerate(outs):
         first = lax.rem(index + k, n_tp) * per
         for at in range(per):
-            source = pl.multiple_of(place[first + at], 16)
-            out_ref[at * PIECE:(at + 1) * PIECE, :] = held_ref[pl.ds(source, PIECE), :]
-        out_ref[per * PIECE:, :] = grad_ref[...]
-
-
-def compacted(shard_blocks, held, grad, slot_rows, n_tp, width):
-    n_blocks = width // BLOCK
+            source = pl.multiple_of(place[first + at], BLOCK)
+            out_ref[at * BLOCK:(at + 1) * BLOCK, :] = gathered_ref[pl.ds(source, BLOCK), :]
+        out_ref[per * BLOCK:, :] = grad_ref[...]
+
+
+def compacted(shard_blocks, gathered, grad, slot_rows, n_tp, width):
     slot_blocks = slot_rows // BLOCK
-    rows = n_blocks // n_tp * PIECE + grad.shape[0]
+    rows = width // n_tp + grad.shape[0]
     vmem = pl.BlockSpec(memory_space=pltpu.VMEM)
     return pl.pallas_call(
         functools.partial(compact_kernel, slot_blocks, n_tp),
         in_specs=[pl.BlockSpec(memory_space=pltpu.SMEM), vmem, vmem],
         out_specs=[vmem] * n_tp,
         out_shape=[jax.ShapeDtypeStruct((rows, grad.shape[1]), grad.dtype)] * n_tp,
-        scratch_shapes=[pltpu.SMEM((n_blocks + slot_blocks,), jnp.int32)],
+        scratch_shapes=[pltpu.SMEM((width // BLOCK + slot_blocks,), jnp.int32)],
         compiler_params=SMALL,
-        cost_estimate=pl.CostEstimate(flops=0, bytes_accessed=2 * rows * grad.shape[1], transcendentals=0),
+        cost_estimate=pl.CostEstimate(flops=0, bytes_accessed=4 * width * grad.shape[1], transcendentals=0),
         name="compact_rows",
-    )(shard_blocks, held.reshape(-1, held.shape[-1]), grad)
+    )(shard_blocks, gathered, grad)
 
 
 def input_kernel(heads, counts_ref, *refs):
-    own, (before_ref, after_ref), grads = refs[:heads], refs[heads:heads + 2], refs[heads + 2:2 * heads + 2]
-    out_ref, masked, weight = refs[2 * heads + 2:]
-    step = pl.program_id(0)
-    turn = lax.rem(lax.axis_index("rep"), SPLIT)
-    blocks = before_ref.shape[1] // PIECE
-
-    @pl.when(step == 0)
+    weights, grads = refs[:heads], refs[heads:2 * heads]
+    out_ref, masked = refs[2 * heads:]
+
+    @pl.when(pl.program_id(0) == 0)
     def _():
         for h in range(heads):
             grad = grads[h][...].astype(jnp.float32)
             live = lax.broadcasted_iota(jnp.int32, grad.shape, 0) < counts_ref[0]
             masked[:, h * BLOCK:(h + 1) * BLOCK] = jnp.where(live, grad, 0.0).astype(masked.dtype)
 
-    for piece_here in range(SPLIT):
-        @pl.when(turn == piece_here)
-        def _():
-            for shift in range(SPLIT):
-                first = PIECE_AT[(piece_here + shift) % SPLIT]
-                for h in range(heads):
-                    ref = (own[h], after_ref.at[h], before_ref.at[h])[shift]
-                    for b in range(blocks):
-                        weight[b * BLOCK + first:b * BLOCK + first + PIECE, h * BLOCK:(h + 1) * BLOCK] = ref[
-                            b * PIECE:(b + 1) * PIECE, :
-                        ]
-
+    weight = jnp.concatenate([w[...] for w in weights], axis=1)
     out_ref[...] = lax.dot_general(
-        masked[...], weight[...], (((1,), (1,)), ((), ())), preferred_element_type=jnp.float32
+        masked[...], weight, (((1,), (1,)), ((), ())), preferred_element_type=jnp.float32
     ).astype(out_ref.dtype)
 
 
-def input_product(counts, own, before, after, rows_dev):
-    n_tp, pieces, head = before.shape
-    steps = 4
-    blocks = pieces // PIECE // steps
-    chunk = blocks * BLOCK
-    return pl.pallas_call(
-        functools.partial(input_kernel, n_tp),
-        grid=(steps,),
+def input_product(counts, parts, rows_dev):
+    n = len(parts)
+    rows, head = parts[0].shape[0] - rows_dev, parts[0].shape[1]
+    chunk = 512
+    return pl.pallas_call(
+        functools.partial(input_kernel, n),
+        grid=(rows // chunk,),
         in_specs=[pl.BlockSpec(memory_space=pltpu.SMEM)]
-        + [pl.BlockSpec((blocks * PIECE, head), lambda i: (i, 0))] * n_tp
-        + [pl.BlockSpec((n_tp, blocks * PIECE, head), lambda i: (0, i, 0))] * 2
-        + [pl.BlockSpec((rows_dev, head), lambda i: (pieces // rows_dev, 0))] * n_tp,
+        + [pl.BlockSpec((chunk, head), lambda i: (i, 0))] * n
+        + [pl.BlockSpec((pl.Element(rows_dev), pl.Element(head)), lambda i: (rows, 0))] * n,
         out_specs=pl.BlockSpec((rows_dev, chunk), lambda i: (0, i)),
-        out_shape=jax.ShapeDtypeStruct((rows_dev, steps * chunk), jnp.bfloat16),
-        scratch_shapes=[
-            pltpu.VMEM((rows_dev, head * n_tp), jnp.bfloat16),
-            pltpu.VMEM((chunk, head * n_tp), jnp.bfloat16),
-        ],
+        out_shape=jax.ShapeDtypeStruct((rows_dev, rows), jnp.bfloat16),
+        scratch_shapes=[pltpu.VMEM((rows_dev, head * n), jnp.bfloat16)],
         compiler_params=pltpu.CompilerParams(vmem_limit_bytes=16 * 1024 * 1024),
         cost_estimate=pl.CostEstimate(
-            flops=2 * rows_dev * steps * chunk * head * n_tp,
-            bytes_accessed=2 * steps * chunk * (head * n_tp + rows_dev),
-            transcendentals=0,
+            flops=2 * rows_dev * rows * head * n, bytes_accessed=2 * rows * (head * n + rows_dev), transcendentals=0
         ),
         name="input_grad",
-    )(counts, *own, before, after, *own)
-
-
-def ordered(array, other):
-    return lax.optimization_barrier((array, other))[0]
+    )(counts, *parts, *parts)
 
 
 def on_device(hidden_in, value_grad, weight_shards, shard_blocks, token_counts):
@@ -248,35 +216,22 @@
     slot_rows, head = weight_shards.shape
     n_dp, n_tp, n_rep = lax.axis_size("dp"), lax.axis_size("tp"), lax.axis_size("rep")
     n_y = n_dp // 2
-    slot_blocks = slot_rows // BLOCK
     core_swap = [(i, i ^ 1) for i in range(n_dp)]
     along_y = [[c + 2 * y for y in range(n_y)] for c in range(2)]
     up = [(i, (i + 1) % n_rep) for i in range(n_rep)]
     down = [(i, (i - 1) % n_rep) for i in range(n_rep)]
 
-    turn = lax.rem(lax.axis_index("rep"), SPLIT)
-    first = turn * PIECE_AT[1] - jnp.where(turn == 2, 2 * PIECE_AT[1] - PIECE_AT[2], 0)
-    piece = lax.dynamic_slice_in_dim(weight_shards.reshape(slot_blocks, BLOCK, head), first, PIECE, 1)
-    piece = piece.reshape(1, slot_blocks * PIECE, head)
-    held = lax.all_to_all(
-        jnp.broadcast_to(piece, (n_y,) + piece.shape[1:]), "dp", 0, 0, axis_index_groups=along_y
-    ).reshape(n_y * slot_blocks * PIECE, head)
+    gathered = lax.all_gather(weight_shards, "dp", axis=0, tiled=True)
     send, keep = grad_products(token_counts, shard_blocks, hidden_in, value_grad, slot_rows)
     received = lax.ppermute(send, "dp", core_swap)
     stay, to_next, to_last = paired_parts(keep, received)
 
-    pair = [[2 * y, 2 * y + 1] for y in range(n_y)]
-    held = lax.all_to_all(jnp.broadcast_to(held[None], (2,) + held.shape), "dp", 0, 0, axis_index_groups=pair)
-    sent = compacted(shard_blocks, held, value_grad, slot_rows, n_tp, width)
-    own = [sent[0]] + [
+    sent = compacted(shard_blocks, gathered, value_grad, slot_rows, n_tp, width)
+    parts = [sent[0]] + [
         lax.ppermute(sent[k], "tp", [(i, (i + k) % n_tp) for i in range(n_tp)]) for k in range(1, n_tp)
     ]
-    pieces = jnp.stack([part[: part.shape[0] - rows_dev] for part in own])
-    before = lax.ppermute(pieces, "rep", up)
-    after = lax.ppermute(pieces, "rep", down)
-    input_grad = input_product(token_counts, own, before, after, rows_dev)
-
-    stay = ordered(stay, sent[0])
+    input_grad = input_product(token_counts, parts, rows_dev)
+
     part = summed([stay, lax.ppermute(to_next, "rep", up), lax.ppermute(to_last, "rep", down)])
     spread = lax.all_to_all(part.reshape(n_y, slot_rows // SPLIT, head), "dp", 0, 0, axis_index_groups=along_y)
     owned = summed([spread[y] for y in range(n_y)])

time: 131 us -> 131 us (level); the launches traced: 130 us -> 129 us
  blocking collectives: 4.81 us -> 47.5 us
  starting transfers between devices: 68.5 us -> 33.1 us
  waiting for transfers between devices: 35.3 us -> 15.7 us
  between operations: 1.57 us -> 14.8 us
  other arithmetic: 2.7 us -> 0.92 us
    all_to_all x1 -> x2, blocking collectives: 4.81 us -> 47.5 us  [the longest x1 24.2 us: on_device(): lax.all_to_all(part.reshape(n_y, slot_rows // SPLIT, head), 'dp', 0, 0, a...]
    all_to_all x3 -> x0, starting transfers between devices: 17.9 us -> none  [the longest x1 7.35 us: on_device(): lax.all_to_all(jnp.broadcast_to(share[None], (n_rep,) + share.shape), 're...]
    ppermute x2 -> x0, waiting for transfers between devices: 14.5 us -> none  [the longest x1 10.5 us: on_device(): after = lax.ppermute(pieces, 'rep', down)]
    ppermute x1, waiting for transfers between devices: 0.01 us -> 10.3 us  [on_device(): lax.ppermute(to_next, 'rep', up)]
    all_to_all x3 -> x0, waiting for transfers between devices: 10 us -> none  [the longest x1 5.66 us: on_device(): lax.all_to_all(part.reshape(n_y, slot_rows // SPLIT, head), 'dp', 0, 0, a...]
    ppermute x3, waiting for transfers between devices: 9.18 us -> 0.01 us  [on_device(): lax.ppermute(sent[k], 'tp', [(i, (i + k) % n_tp) for i in range(n_tp)])]
    ppermute x2 -> x0, starting transfers between devices: 8.27 us -> none  [the longest x1 6.35 us: on_device(): after = lax.ppermute(pieces, 'rep', down)]
    ppermute x3, starting transfers between devices: 13.3 us -> 8.63 us  [on_device(): lax.ppermute(sent[k], 'tp', [(i, (i + k) % n_tp) for i in range(n_tp)])]
  transfers between devices with their start and end apart: 12 -> 8, of which waited for: 8 -> 3; matrix products, arithmetic and copies ran while one was open for 4% -> 1% of each run, Pallas kernels for 4% -> 8%
where the time goes in v3:
time: 131 us; the launch traced here: 129 us
  blocking collectives  47.5 us (36%)
  starting transfers between devices  33.1 us (25%)
  waiting for transfers between devices  15.7 us (12%)
  between operations  14.8 us (11%)
  Pallas kernels  13.2 us (10%)
  local copies, waits for them, and re-layouts  3.33 us (3%)
    all_to_all x1, blocking collectives, on_device(): lax.all_to_all(part.reshape(n_y, slot_rows // SPLIT, head), 'dp', 0, 0, a...  24.2 us
    all_to_all x1, blocking collectives, on_device(): lax.all_to_all(jnp.broadcast_to(share[None], (n_rep,) + share.shape), 're...  23.4 us
    ppermute x1, starting transfers between devices, on_device(): lax.ppermute(to_last, 'rep', down)  12.2 us
    ppermute x1, waiting for transfers between devices, on_device(): lax.ppermute(to_next, 'rep', up)  10.3 us
    ppermute x3, starting transfers between devices, on_device(): lax.ppermute(sent[k], 'tp', [(i, (i + k) % n_tp) for i in range(n_tp)])  8.63 us
    pallas_call x1, Pallas kernels, grad_products(): pl.pallas_call(functools.partial(grad_kernel, chunk, slot_blocks), in_spe...  7.27 us
    all_to_all x1, starting transfers between devices, on_device(): lax.all_to_all(owned.reshape(n_rep // SPLIT, share_rows, head), 'rep', 0,...  6.04 us
    ppermute x1, starting transfers between devices, on_device(): lax.ppermute(to_next, 'rep', up)  4.27 us
  transfers between devices with their start and end apart: 8, of which 3 were waited for; matrix products, arithmetic and copies ran while one was open for 1% of the time, Pallas kernels for 8%

profile of v3, /device:TPU:6, one launch (start us, length us, event | category | flops | bytes accessed | tf_op | source)
XLA Modules:
  0.0 128.6 jit_solution(6501371303356335211)
XLA Ops:
  7.2 0.0 all-gather.2.cloned.1.call-start
  7.2 0.7 all-gather.2.cloned.1.call-update
  8.5 7.3 %grad_products.1 = (bf16[6144,128]{1,0:T(8,128)(2,1)}, bf16[6144,128]{1,0:T(8,128)(2,1)}) custom-call(s32[1]{0:T(128)S(6)} %copy.7.counts_ref, s32[16]{0:T(128)} %blocks_ref.3, bf16[384,8192]{1,0:T(8,128)(2,1)} %hidden_ref.1, bf16[384,128]{1,0:T(8,128)(2,1)} %grad_ref.3), custom_call_target="tpu_custom_call" | custom-call | flops 805306368 | bytes 9437184 | tf_op jit(solution)/shard_map/grad_products/pallas_call | solution.py:82
  15.8 1.9 %collective-permute-start.3 = (bf16[6144,128]{1,0:T(8,128)(2,1)}, bf16[6144,128]{1,0:T(8,128)(2,1)S(1)}, u32[]{:S(2)}, u32[]{:S(2)}) collective-permute-start(bf16[6144,128]{1,0:T(8,128)(2,1)} %get-tuple-element.16), channel_id=1, source_target_pairs={{0,4},{4,0},{8,12},{12,8},{16,20},{20,16},{24,28},{28,24},{32,36},... | collective-permute-start | bytes 4718600 | tf_op jit(solution)/shard_map/ppermute | solution.py:226
  17.7 3.6 %collective-permute-done.3.received_ref = bf16[6144,128]{1,0:T(8,128)(2,1)S(1)} collective-permute-done((bf16[6144,128]{1,0:T(8,128)(2,1)}, bf16[6144,128]{1,0:T(8,128)(2,1)S(1)}, u32[]{:S(2)}, u32[]{:S(2)}) %collective-permute-start.3) | collective-permute-done | bytes 1572896 | tf_op jit(solution)/shard_map/ppermute | solution.py:226
  21.3 1.4 %copy-done.1 = bf16[6144,128]{1,0:T(8,128)(2,1)S(1)} copy-done((bf16[6144,128]{1,0:T(8,128)(2,1)S(1)}, bf16[6144,128]{1,0:T(8,128)(2,1)}, u32[]{:S(2)}) %copy-start.1) | copy-done | bytes 1572888
  22.7 0.4 pair_parts.1
  23.1 4.3 %collective-permute-start.4 = (bf16[2048,128]{1,0:T(8,128)(2,1)S(1)}, bf16[2048,128]{1,0:T(8,128)(2,1)S(1)}, u32[]{:S(2)}, u32[]{:S(2)}) collective-permute-start(bf16[2048,128]{1,0:T(8,128)(2,1)S(1)} %get-tuple-element.18), channel_id=1, source_target_pairs={{0,64},{64,128},{128,192},{192,256},{256,320},{320,384},{384,448},... | collective-permute-start | bytes 1572872 | tf_op jit(solution)/shard_map/ppermute | solution.py:235
  27.4 12.2 %collective-permute-start.5 = (bf16[2048,128]{1,0:T(8,128)(2,1)S(1)}, bf16[2048,128]{1,0:T(8,128)(2,1)S(1)}, u32[]{:S(2)}, u32[]{:S(2)}) collective-permute-start(bf16[2048,128]{1,0:T(8,128)(2,1)S(1)} %get-tuple-element.19), channel_id=1, source_target_pairs={{0,704},{64,0},{128,64},{192,128},{256,192},{320,256},{384,320},{4... | collective-permute-start | bytes 1572872 | tf_op jit(solution)/shard_map/ppermute | solution.py:235
  39.6 10.3 %collective-permute-done.4 = bf16[2048,128]{1,0:T(8,128)(2,1)S(1)} collective-permute-done((bf16[2048,128]{1,0:T(8,128)(2,1)S(1)}, bf16[2048,128]{1,0:T(8,128)(2,1)S(1)}, u32[]{:S(2)}, u32[]{:S(2)}) %collective-permute-start.4) | collective-permute-done | bytes 524320 | tf_op jit(solution)/shard_map/ppermute | solution.py:235
  49.9 1.2 collective-permute-done.5
  51.1 0.2 add_convert_fusion
  51.3 24.2 %all_to_all.15 = bf16[8,256,128]{2,1,0:T(8,128)(2,1)S(1)} all-to-all(bf16[8,256,128]{2,1,0:T(8,128)(2,1)S(1)} %bitcast.6), channel_id=1, replica_groups={{0,8,16,24,32,40,48,56},{4,12,20,28,36,44,52,60},{1,9,17,25,33,41,49,57..., dimensions={0} | all-to-all | bytes 1048576 | tf_op jit(solution)/shard_map/all_to_all | solution.py:236
  75.4 0.7 add_convert_fusion.1
  76.1 6.0 %all-to-all-start.1 = ((bf16[4,64,128]{2,1,0:T(8,128)(2,1)}), bf16[4,64,128]{2,1,0:T(8,128)(2,1)S(1)}, u32[]{:S(2)}, u32[]{:S(2)}) async-start(bf16[4,64,128]{2,1,0:T(8,128)(2,1)} %bitcast.1), calls=%async_computation.1 | async-start | bytes 131072 | tf_op jit(solution)/shard_map/all_to_all | solution.py:240
  82.2 1.9 %copy-done = bf16[12288,128]{1,0:T(8,128)(2,1)S(1)} copy-done((bf16[12288,128]{1,0:T(8,128)(2,1)S(1)}, bf16[12288,128]{1,0:T(8,128)(2,1)}, u32[]{:S(2)}) %copy-start) | copy-done | bytes 3145752
  84.1 1.8 %compact_rows.1 = (bf16[2432,128]{1,0:T(8,128)(2,1)S(1)}, bf16[2432,128]{1,0:T(8,128)(2,1)}, bf16[2432,128]{1,0:T(8,128)(2,1)}, bf16[2432,128]{1,0:T(8,128)(2,1)S(1)}) custom-call(s32[16]{0:T(128)S(1)} %copy-done.3, bf16[12288,128]{1,0:T(8,128)(2,1)S(1)} %copy-done, bf16[384,128]{1,0:T(8,128)(2,1)S(1)} %copy-done.2), custom_call_target="tpu_custom_call" | custom-call | bytes 4194304 | tf_op jit(solution)/shard_map/compact_rows/pallas_call | solution.py:164
  85.9 2.3 %collective-permute-start = (bf16[2432,128]{1,0:T(8,128)(2,1)}, bf16[2432,128]{1,0:T(8,128)(2,1)S(1)}, u32[]{:S(2)}, u32[]{:S(2)}) collective-permute-start(bf16[2432,128]{1,0:T(8,128)(2,1)} %get-tuple-element.12), channel_id=1, source_target_pairs={{0,1},{1,2},{2,3},{3,0},{4,5},{5,6},{6,7},{7,4},{8,9},{9,10},{10,1... | collective-permute-start | bytes 1867784 | tf_op jit(solution)/shard_map/ppermute | solution.py:231
  88.2 4.4 %collective-permute-start.1 = (bf16[2432,128]{1,0:T(8,128)(2,1)}, bf16[2432,128]{1,0:T(8,128)(2,1)S(1)}, u32[]{:S(2)}, u32[]{:S(2)}) collective-permute-start(bf16[2432,128]{1,0:T(8,128)(2,1)} %get-tuple-element.13), channel_id=1, source_target_pairs={{0,2},{1,3},{2,0},{3,1},{4,6},{5,7},{6,4},{7,5},{8,10},{9,11},{10,... | collective-permute-start | bytes 1867784 | tf_op jit(solution)/shard_map/ppermute | solution.py:231
  92.6 1.9 %collective-permute-start.2 = (bf16[2432,128]{1,0:T(8,128)(2,1)S(1)}, bf16[2432,128]{1,0:T(8,128)(2,1)S(1)}, u32[]{:S(2)}, u32[]{:S(2)}) collective-permute-start(bf16[2432,128]{1,0:T(8,128)(2,1)S(1)} %get-tuple-element.14), channel_id=1, source_target_pairs={{0,3},{1,0},{2,1},{3,2},{4,7},{5,4},{6,5},{7,6},{8,11},{9,8},{10,9... | collective-permute-start | bytes 1867784 | tf_op jit(solution)/shard_map/ppermute | solution.py:231
  94.6 23.4 %all_to_all.16 = bf16[12,64,128]{2,1,0:T(8,128)(2,1)S(1)} all-to-all(bf16[12,64,128]{2,1,0:T(8,128)(2,1)S(1)} %broadcast_in_dim.9), channel_id=1, replica_groups=mesh['rep'=12,'dp'=16,'tp'=4] {'rep'}, dimensions={0} | all-to-all | bytes 393216 | tf_op jit(solution)/shard_map/all_to_all | solution.py:244
  118.0 0.9 finish_weight_grad.1
  118.9 0.0 collective-permute-done.refs_1_.refs_5_
  118.9 2.9 %input_grad.1 = bf16[384,2048]{1,0:T(8,128)(2,1)} custom-call(s32[1]{0:T(128)S(6)} %copy.7.counts_ref, bf16[2432,128]{1,0:T(8,128)(2,1)S(1)} %get-tuple-element.11.refs_0_.refs_4_, bf16[2432,128]{1,0:T(8,128)(2,1)S(1)} %collective-permute-done.refs_1_.refs_5_, bf16[2432,128]{1,0:T(8,128)(2,1)S(1)} %collective-permute-done.1.refs_2_.refs_6_, ...), custom_call_target="tpu_custom_call" | custom-call | flops 805306368 | bytes 3670016 | tf_op jit(solution)/shard_map/input_grad/pallas_call | solution.py:197
  (12 shorter events, 0.1 us)
Async XLA Ops:
  7.2 75.0 %all-gather.2.cloned.1.call-start = ((), (), s32[]{:S(2)}) async-start(), calls=%async_computation.3 | async-start | bytes 3342336 | tf_op jit(solution)/shard_map/all_gather | solution.py:224
  15.8 5.5 %collective-permute-start.3 = (bf16[6144,128]{1,0:T(8,128)(2,1)}, bf16[6144,128]{1,0:T(8,128)(2,1)S(1)}, u32[]{:S(2)}, u32[]{:S(2)}) collective-permute-start(bf16[6144,128]{1,0:T(8,128)(2,1)} %get-tuple-element.16), channel_id=1, source_target_pairs={{0,4},{4,0},{8,12},{12,8},{16,20},{20,16},{24,28},{28,24},{32,36},... | collective-permute-start | bytes 4718600 | tf_op jit(solution)/shard_map/ppermute | solution.py:226
  21.3 1.4 %copy-start.1 = (bf16[6144,128]{1,0:T(8,128)(2,1)S(1)}, bf16[6144,128]{1,0:T(8,128)(2,1)}, u32[]{:S(2)}) copy-start(bf16[6144,128]{1,0:T(8,128)(2,1)} %get-tuple-element.15.keep_ref) | copy-start | bytes 4718596
  23.1 26.8 %collective-permute-start.4 = (bf16[2048,128]{1,0:T(8,128)(2,1)S(1)}, bf16[2048,128]{1,0:T(8,128)(2,1)S(1)}, u32[]{:S(2)}, u32[]{:S(2)}) collective-permute-start(bf16[2048,128]{1,0:T(8,128)(2,1)S(1)} %get-tuple-element.18), channel_id=1, source_target_pairs={{0,64},{64,128},{128,192},{192,256},{256,320},{320,384},{384,448},... | collective-permute-start | bytes 1572872 | tf_op jit(solution)/shard_map/ppermute | solution.py:235
  27.4 23.7 %collective-permute-start.5 = (bf16[2048,128]{1,0:T(8,128)(2,1)S(1)}, bf16[2048,128]{1,0:T(8,128)(2,1)S(1)}, u32[]{:S(2)}, u32[]{:S(2)}) collective-permute-start(bf16[2048,128]{1,0:T(8,128)(2,1)S(1)} %get-tuple-element.19), channel_id=1, source_target_pairs={{0,704},{64,0},{128,64},{192,128},{256,192},{320,256},{384,320},{4... | collective-permute-start | bytes 1572872 | tf_op jit(solution)/shard_map/ppermute | solution.py:235
  51.1 31.1 %copy-start.2 = (bf16[384,128]{1,0:T(8,128)(2,1)S(1)}, bf16[384,128]{1,0:T(8,128)(2,1)}, u32[]{:S(2)}) copy-start(bf16[384,128]{1,0:T(8,128)(2,1)} %grad_ref.3) | copy-start | bytes 294916
  51.1 31.1 %copy-start.3 = (s32[16]{0:T(128)S(1)}, s32[16]{0:T(128)}, u32[]{:S(2)}) copy-start(s32[16]{0:T(128)} %blocks_ref.3) | copy-start | bytes 196
  76.1 18.4 %all-to-all-start.1 = ((bf16[4,64,128]{2,1,0:T(8,128)(2,1)}), bf16[4,64,128]{2,1,0:T(8,128)(2,1)S(1)}, u32[]{:S(2)}, u32[]{:S(2)}) async-start(bf16[4,64,128]{2,1,0:T(8,128)(2,1)} %bitcast.1), calls=%async_computation.1 | async-start | bytes 131072 | tf_op jit(solution)/shard_map/all_to_all | solution.py:240
  82.2 1.9 %copy-start = (bf16[12288,128]{1,0:T(8,128)(2,1)S(1)}, bf16[12288,128]{1,0:T(8,128)(2,1)}, u32[]{:S(2)}) copy-start(bf16[12288,128]{1,0:T(8,128)(2,1)} %all-gather.2.cloned.1.call-done.gathered_ref) | copy-start | bytes 9437188
  85.9 33.0 %collective-permute-start = (bf16[2432,128]{1,0:T(8,128)(2,1)}, bf16[2432,128]{1,0:T(8,128)(2,1)S(1)}, u32[]{:S(2)}, u32[]{:S(2)}) collective-permute-start(bf16[2432,128]{1,0:T(8,128)(2,1)} %get-tuple-element.12), channel_id=1, source_target_pairs={{0,1},{1,2},{2,3},{3,0},{4,5},{5,6},{6,7},{7,4},{8,9},{9,10},{10,1... | collective-permute-start | bytes 1867784 | tf_op jit(solution)/shard_map/ppermute | solution.py:231
  88.2 30.7 %collective-permute-start.1 = (bf16[2432,128]{1,0:T(8,128)(2,1)}, bf16[2432,128]{1,0:T(8,128)(2,1)S(1)}, u32[]{:S(2)}, u32[]{:S(2)}) collective-permute-start(bf16[2432,128]{1,0:T(8,128)(2,1)} %get-tuple-element.13), channel_id=1, source_target_pairs={{0,2},{1,3},{2,0},{3,1},{4,6},{5,7},{6,4},{7,5},{8,10},{9,11},{10,... | collective-permute-start | bytes 1867784 | tf_op jit(solution)/shard_map/ppermute | solution.py:231
  92.6 26.3 %collective-permute-start.2 = (bf16[2432,128]{1,0:T(8,128)(2,1)S(1)}, bf16[2432,128]{1,0:T(8,128)(2,1)S(1)}, u32[]{:S(2)}, u32[]{:S(2)}) collective-permute-start(bf16[2432,128]{1,0:T(8,128)(2,1)S(1)} %get-tuple-element.14), channel_id=1, source_target_pairs={{0,3},{1,0},{2,1},{3,2},{4,7},{5,4},{6,5},{7,6},{8,11},{9,8},{10,9... | collective-permute-start | bytes 1867784 | tf_op jit(solution)/shard_map/ppermute | solution.py:231
Sparse Core Ops, SparseCore 0:
  10.4 53.1 all-gather.1

commit v4 on v3

--- a/solution.py
+++ b/solution.py
@@ -144,33 +144,49 @@
     )(total)
 
 
-def compact_kernel(slot_blocks, n_tp, blocks_ref, gathered_ref, grad_ref, *rest):
+def compact_kernel(slot_blocks, n_tp, blocks_ref, mine_ref, other_ref, grad_ref, *rest):
     outs, place = rest[:n_tp], rest[n_tp]
+    core = lax.rem(lax.axis_index("dp"), 2)
     index = lax.axis_index("tp")
-    fill_places(blocks_ref, place, slot_blocks, lambda owner, at: (owner * slot_blocks + at) * BLOCK)
+    half = mine_ref.shape[0]
+    side = [jnp.where(core == parity, 0, half) for parity in range(2)]
+    fill_places(
+        blocks_ref, place, slot_blocks,
+        lambda owner, at: side[owner % 2] + ((owner // 2) * slot_blocks + at) * BLOCK,
+    )
     per = (outs[0].shape[0] - grad_ref.shape[0]) // BLOCK
     for k, out_ref in enumerate(outs):
         first = lax.rem(index + k, n_tp) * per
         for at in range(per):
-            source = pl.multiple_of(place[first + at], BLOCK)
-            out_ref[at * BLOCK:(at + 1) * BLOCK, :] = gathered_ref[pl.ds(source, BLOCK), :]
+            source = place[first + at]
+
+            @pl.when(source < half)
+            def _():
+                out_ref[at * BLOCK:(at + 1) * BLOCK, :] = mine_ref[pl.ds(pl.multiple_of(source, BLOCK), BLOCK), :]
+
+            @pl.when(source >= half)
+            def _():
+                out_ref[at * BLOCK:(at + 1) * BLOCK, :] = other_ref[
+                    pl.ds(pl.multiple_of(source - half, BLOCK), BLOCK), :
+                ]
+
         out_ref[per * BLOCK:, :] = grad_ref[...]
 
 
-def compacted(shard_blocks, gathered, grad, slot_rows, n_tp, width):
+def compacted(shard_blocks, mine, other, grad, slot_rows, n_tp, width):
     slot_blocks = slot_rows // BLOCK
     rows = width // n_tp + grad.shape[0]
     vmem = pl.BlockSpec(memory_space=pltpu.VMEM)
     return pl.pallas_call(
         functools.partial(compact_kernel, slot_blocks, n_tp),
-        in_specs=[pl.BlockSpec(memory_space=pltpu.SMEM), vmem, vmem],
+        in_specs=[pl.BlockSpec(memory_space=pltpu.SMEM), vmem, vmem, vmem],
         out_specs=[vmem] * n_tp,
         out_shape=[jax.ShapeDtypeStruct((rows, grad.shape[1]), grad.dtype)] * n_tp,
         scratch_shapes=[pltpu.SMEM((width // BLOCK + slot_blocks,), jnp.int32)],
         compiler_params=SMALL,
         cost_estimate=pl.CostEstimate(flops=0, bytes_accessed=4 * width * grad.shape[1], transcendentals=0),
         name="compact_rows",
-    )(shard_blocks, gathered, grad)
+    )(shard_blocks, mine, other, grad)
 
 
 def input_kernel(heads, counts_ref, *refs):
@@ -211,6 +227,10 @@
     )(counts, *parts, *parts)
 
 
+def ordered(array, other):
+    return lax.optimization_barrier((array, other))[0]
+
+
 def on_device(hidden_in, value_grad, weight_shards, shard_blocks, token_counts):
     rows_dev, width = hidden_in.shape
     slot_rows, head = weight_shards.shape
@@ -221,12 +241,15 @@
     up = [(i, (i + 1) % n_rep) for i in range(n_rep)]
     down = [(i, (i - 1) % n_rep) for i in range(n_rep)]
 
-    gathered = lax.all_gather(weight_shards, "dp", axis=0, tiled=True)
+    held = lax.all_to_all(
+        jnp.broadcast_to(weight_shards[None], (n_y,) + weight_shards.shape), "dp", 0, 0, axis_index_groups=along_y
+    ).reshape(n_y * slot_rows, head)
     send, keep = grad_products(token_counts, shard_blocks, hidden_in, value_grad, slot_rows)
     received = lax.ppermute(send, "dp", core_swap)
     stay, to_next, to_last = paired_parts(keep, received)
 
-    sent = compacted(shard_blocks, gathered, value_grad, slot_rows, n_tp, width)
+    other = lax.ppermute(held, "dp", core_swap)
+    sent = compacted(shard_blocks, held, other, value_grad, slot_rows, n_tp, width)
     parts = [sent[0]] + [
         lax.ppermute(sent[k], "tp", [(i, (i + k) % n_tp) for i in range(n_tp)]) for k in range(1, n_tp)
     ]
@@ -234,6 +257,7 @@
 
     part = summed([stay, lax.ppermute(to_next, "rep", up), lax.ppermute(to_last, "rep", down)])
     spread = lax.all_to_all(part.reshape(n_y, slot_rows // SPLIT, head), "dp", 0, 0, axis_index_groups=along_y)
+    spread = ordered(spread, sent[0])
     owned = summed([spread[y] for y in range(n_y)])
     fellows = [[k + SPLIT * q for q in range(n_rep // SPLIT)] for k in range(SPLIT)]
     share_rows = slot_rows // n_rep

time: 131 us -> 134 us (1.023)
  blocking collectives: 47.5 us -> 0 us
  starting transfers between devices: 33.1 us -> 60.9 us
  waiting for transfers between devices: 15.7 us -> 41.2 us
  between operations: 14.8 us -> 1.39 us
  local copies, waits for them, and re-layouts: 3.33 us -> 9.43 us
  other arithmetic: 0.92 us -> 4.16 us
  Pallas kernels: 13.2 us -> 14.6 us
    all_to_all x2 -> x0, blocking collectives: 47.5 us -> none  [the longest x1 24.2 us: on_device(): lax.all_to_all(part.reshape(n_y, slot_rows // SPLIT, head), 'dp', 0, 0, a...]
    all_to_all x0 -> x3, starting transfers between devices: none -> 22.3 us  [the longest x1 7.99 us: on_device(): lax.all_to_all(jnp.broadcast_to(share[None], (n_rep,) + share.shape), 're...]
    all_to_all x0 -> x3, waiting for transfers between devices: none -> 17 us  [the longest x1 10.4 us: on_device(): lax.all_to_all(part.reshape(n_y, slot_rows // SPLIT, head), 'dp', 0, 0, a...]
    ppermute x3, waiting for transfers between devices: 0.01 us -> 15.1 us  [on_device(): lax.ppermute(sent[k], 'tp', [(i, (i + k) % n_tp) for i in range(n_tp)])]
    ppermute x1, waiting for transfers between devices: 10.3 us -> 2.08 us  [on_device(): lax.ppermute(to_next, 'rep', up)]
    all_to_all x1, starting transfers between devices: 6.04 us -> 9.62 us  [on_device(): lax.all_to_all(owned.reshape(n_rep // SPLIT, share_rows, head), 'rep', 0,...]
    convert_element_type x2, other arithmetic: 0.91 us -> 4.15 us  [summed(): return total.astype(parts[0].dtype)]
    unnamed x8 -> x16, local copies, waits for them, and re-layouts: 3.3 us -> 6.44 us
  transfers between devices with their start and end apart: 8 -> 11, of which waited for: 3 -> 8; matrix products, arithmetic and copies ran while one was open for 1% -> 2% of each run, Pallas kernels for 8% -> 10%
where the time goes in v4:
time: 134 us; the launch traced here: 132 us
  starting transfers between devices  60.9 us (45%)
  waiting for transfers between devices  41.2 us (31%)
  Pallas kernels  14.6 us (11%)
  local copies, waits for them, and re-layouts  9.43 us (7%)
  other arithmetic  4.16 us (3%)
  between operations  1.39 us (1%)
    ppermute x3, waiting for transfers between devices, on_device(): lax.ppermute(sent[k], 'tp', [(i, (i + k) % n_tp) for i in range(n_tp)])  15.1 us
    ppermute x1, starting transfers between devices, on_device(): lax.ppermute(to_last, 'rep', down)  12.2 us
    all_to_all x1, waiting for transfers between devices, on_device(): lax.all_to_all(part.reshape(n_y, slot_rows // SPLIT, head), 'dp', 0, 0, a...  10.4 us
    all_to_all x1, starting transfers between devices, on_device(): lax.all_to_all(owned.reshape(n_rep // SPLIT, share_rows, head), 'rep', 0,...  9.62 us
    ppermute x3, starting transfers between devices, on_device(): lax.ppermute(sent[k], 'tp', [(i, (i + k) % n_tp) for i in range(n_tp)])  8.62 us
    all_to_all x1, starting transfers between devices, on_device(): lax.all_to_all(jnp.broadcast_to(share[None], (n_rep,) + share.shape), 're...  7.99 us
    all_to_all x1, starting transfers between devices, on_device(): lax.all_to_all(part.reshape(n_y, slot_rows // SPLIT, head), 'dp', 0, 0, a...  7.21 us
    pallas_call x1, Pallas kernels, grad_products(): pl.pallas_call(functools.partial(grad_kernel, chunk, slot_blocks), in_spe...  7.2 us
  transfers between devices with their start and end apart: 11, of which 8 were waited for; matrix products, arithmetic and copies ran while one was open for 2% of the time, Pallas kernels for 10%

profile of v4, /device:TPU:6, one launch (start us, length us, event | category | flops | bytes accessed | tf_op | source)
XLA Modules:
  0.0 131.7 jit_solution(5872530070549952762)
XLA Ops:
  0.6 2.3 %broadcast_in_dim.6 = bf16[8,768,128]{2,1,0:T(8,128)(2,1)} broadcast(bf16[768,128]{1,0:T(8,128)(2,1)} %param.7), dimensions={1,2} | broadcast | bytes 1769472 | tf_op jit(solution)/shard_map/broadcast_in_dim | solution.py:245
  2.9 7.1 %all-to-all-start = ((bf16[8,768,128]{2,1,0:T(8,128)(2,1)}), bf16[8,768,128]{2,1,0:T(8,128)(2,1)S(1)}, u32[]{:S(2)}, u32[]{:S(2)}) async-start(bf16[8,768,128]{2,1,0:T(8,128)(2,1)} %broadcast_in_dim.6), calls=%async_computation | async-start | bytes 3145728 | tf_op jit(solution)/shard_map/all_to_all | solution.py:244
  10.7 7.2 %grad_products.1 = (bf16[6144,128]{1,0:T(8,128)(2,1)}, bf16[6144,128]{1,0:T(8,128)(2,1)}) custom-call(s32[1]{0:T(128)S(6)} %copy.7.counts_ref, s32[16]{0:T(128)} %blocks_ref.3, bf16[384,8192]{1,0:T(8,128)(2,1)} %hidden_ref.1, bf16[384,128]{1,0:T(8,128)(2,1)} %grad_ref.3), custom_call_target="tpu_custom_call" | custom-call | flops 805306368 | bytes 9437184 | tf_op jit(solution)/shard_map/grad_products/pallas_call | solution.py:82
  17.9 1.9 %collective-permute-start.4 = (bf16[6144,128]{1,0:T(8,128)(2,1)}, bf16[6144,128]{1,0:T(8,128)(2,1)S(1)}, u32[]{:S(2)}, u32[]{:S(2)}) collective-permute-start(bf16[6144,128]{1,0:T(8,128)(2,1)} %get-tuple-element.17), channel_id=1, source_target_pairs={{0,4},{4,0},{8,12},{12,8},{16,20},{20,16},{24,28},{28,24},{32,36},... | collective-permute-start | bytes 4718600 | tf_op jit(solution)/shard_map/ppermute | solution.py:248
  19.8 3.6 %collective-permute-done.4.received_ref = bf16[6144,128]{1,0:T(8,128)(2,1)S(1)} collective-permute-done((bf16[6144,128]{1,0:T(8,128)(2,1)}, bf16[6144,128]{1,0:T(8,128)(2,1)S(1)}, u32[]{:S(2)}, u32[]{:S(2)}) %collective-permute-start.4) | collective-permute-done | bytes 1572896 | tf_op jit(solution)/shard_map/ppermute | solution.py:248
  26.9 4.3 %collective-permute-start.5 = (bf16[2048,128]{1,0:T(8,128)(2,1)}, bf16[2048,128]{1,0:T(8,128)(2,1)}, u32[]{:S(2)}, u32[]{:S(2)}) collective-permute-start(bf16[2048,128]{1,0:T(8,128)(2,1)} %get-tuple-element.19), channel_id=1, source_target_pairs={{0,64},{64,128},{128,192},{192,256},{256,320},{320,384},{384,448},... | collective-permute-start | bytes 1572872 | tf_op jit(solution)/shard_map/ppermute | solution.py:258
  31.1 12.2 %collective-permute-start.6 = (bf16[2048,128]{1,0:T(8,128)(2,1)}, bf16[2048,128]{1,0:T(8,128)(2,1)}, u32[]{:S(2)}, u32[]{:S(2)}) collective-permute-start(bf16[2048,128]{1,0:T(8,128)(2,1)} %get-tuple-element.20), channel_id=1, source_target_pairs={{0,704},{64,0},{128,64},{192,128},{256,192},{320,256},{384,320},{4... | collective-permute-start | bytes 1572872 | tf_op jit(solution)/shard_map/ppermute | solution.py:258
  43.4 6.6 %all-to-all-done = bf16[8,768,128]{2,1,0:T(8,128)(2,1)S(1)} async-done(((bf16[8,768,128]{2,1,0:T(8,128)(2,1)}), bf16[8,768,128]{2,1,0:T(8,128)(2,1)S(1)}, u32[]{:S(2)}, u32[]{:S(2)}) %all-to-all-start) | async-done | bytes 1572896 | tf_op jit(solution)/shard_map/all_to_all | solution.py:244
  50.0 1.9 %collective-permute-start = (bf16[6144,128]{1,0:T(8,128)(2,1)S(1)}, bf16[6144,128]{1,0:T(8,128)(2,1)S(1)}, u32[]{:S(2)}, u32[]{:S(2)}) collective-permute-start(bf16[6144,128]{1,0:T(8,128)(2,1)S(1)} %bitcast.6), channel_id=1, source_target_pairs={{0,4},{4,0},{8,12},{12,8},{16,20},{20,16},{24,28},{28,24},{32,36},... | collective-permute-start | bytes 4718600 | tf_op jit(solution)/shard_map/ppermute | solution.py:251
  51.9 2.1 %collective-permute-done.5 = bf16[2048,128]{1,0:T(8,128)(2,1)} collective-permute-done((bf16[2048,128]{1,0:T(8,128)(2,1)}, bf16[2048,128]{1,0:T(8,128)(2,1)}, u32[]{:S(2)}, u32[]{:S(2)}) %collective-permute-start.5) | collective-permute-done | bytes 524320 | tf_op jit(solution)/shard_map/ppermute | solution.py:258
  55.2 2.4 %add_convert_fusion = bf16[2048,128]{1,0:T(8,128)(2,1)} fusion(bf16[2048,128]{1,0:T(8,128)(2,1)} %collective-permute-done.6, bf16[2048,128]{1,0:T(8,128)(2,1)} %collective-permute-done.5, bf16[2048,128]{1,0:T(8,128)(2,1)} %copy-done.3), kind=kLoop, calls=%fused_computation | loop fusion | flops 1572864 | bytes 2097152 | tf_op jit(solution)/shard_map/convert_element_type | solution.py:123
  57.5 7.2 %all-to-all-start.1 = ((bf16[8,256,128]{2,1,0:T(8,128)(2,1)}), bf16[8,256,128]{2,1,0:T(8,128)(2,1)}, u32[]{:S(2)}, u32[]{:S(2)}) async-start(bf16[8,256,128]{2,1,0:T(8,128)(2,1)} %bitcast.9), calls=%async_computation.1 | async-start | bytes 1048576 | tf_op jit(solution)/shard_map/all_to_all | solution.py:259
  67.3 2.4 %compact_rows.1 = (bf16[2432,128]{1,0:T(8,128)(2,1)S(1)}, bf16[2432,128]{1,0:T(8,128)(2,1)}, bf16[2432,128]{1,0:T(8,128)(2,1)S(1)}, bf16[2432,128]{1,0:T(8,128)(2,1)S(1)}) custom-call(s32[16]{0:T(128)S(1)} %copy-done.5, bf16[6144,128]{1,0:T(8,128)(2,1)S(1)} %bitcast.7, bf16[6144,128]{1,0:T(8,128)(2,1)S(1)} %copy-done.2, bf16[384,128]{1,0:T(8,128)(2,1)S(1)} %copy-done.4), custom_call_target="tpu_custom_call" | custom-call | bytes 4194304 | tf_op jit(solution)/shard_map/compact_rows/pallas_call | solution.py:180
  71.4 10.4 %all-to-all-done.1 = bf16[8,256,128]{2,1,0:T(8,128)(2,1)} async-done(((bf16[8,256,128]{2,1,0:T(8,128)(2,1)}), bf16[8,256,128]{2,1,0:T(8,128)(2,1)}, u32[]{:S(2)}, u32[]{:S(2)}) %all-to-all-start.1) | async-done | bytes 524320 | tf_op jit(solution)/shard_map/all_to_all | solution.py:259
  81.8 1.8 %add_convert_fusion.1 = bf16[1,256,128]{2,1,0:T(8,128)(2,1)} fusion(bf16[8,256,128]{2,1,0:T(8,128)(2,1)} %all-to-all-done.1), kind=kLoop, calls=%fused_computation.1 | loop fusion | flops 524288 | bytes 589824 | tf_op jit(solution)/shard_map/convert_element_type | solution.py:123
  83.6 9.6 %all-to-all-start.2 = ((bf16[4,64,128]{2,1,0:T(8,128)(2,1)}), bf16[4,64,128]{2,1,0:T(8,128)(2,1)S(1)}, u32[]{:S(2)}, u32[]{:S(2)}) async-start(bf16[4,64,128]{2,1,0:T(8,128)(2,1)} %bitcast.2), calls=%async_computation.2 | async-start | bytes 131072 | tf_op jit(solution)/shard_map/all_to_all | solution.py:264
  93.2 2.4 %collective-permute-start.1 = (bf16[2432,128]{1,0:T(8,128)(2,1)}, bf16[2432,128]{1,0:T(8,128)(2,1)S(1)}, u32[]{:S(2)}, u32[]{:S(2)}) collective-permute-start(bf16[2432,128]{1,0:T(8,128)(2,1)} %get-tuple-element.13), channel_id=1, source_target_pairs={{0,1},{1,2},{2,3},{3,0},{4,5},{5,6},{6,7},{7,4},{8,9},{9,10},{10,1... | collective-permute-start | bytes 1867784 | tf_op jit(solution)/shard_map/ppermute | solution.py:254
  95.6 4.3 %collective-permute-start.2 = (bf16[2432,128]{1,0:T(8,128)(2,1)}, bf16[2432,128]{1,0:T(8,128)(2,1)S(1)}, u32[]{:S(2)}, u32[]{:S(2)}) collective-permute-start(bf16[2432,128]{1,0:T(8,128)(2,1)} %copy-done.7), channel_id=1, source_target_pairs={{0,2},{1,3},{2,0},{3,1},{4,6},{5,7},{6,4},{7,5},{8,10},{9,11},{10,... | collective-permute-start | bytes 1867784 | tf_op jit(solution)/shard_map/ppermute | solution.py:254
  99.9 1.9 %collective-permute-start.3 = (bf16[2432,128]{1,0:T(8,128)(2,1)}, bf16[2432,128]{1,0:T(8,128)(2,1)S(1)}, u32[]{:S(2)}, u32[]{:S(2)}) collective-permute-start(bf16[2432,128]{1,0:T(8,128)(2,1)} %copy-done.6), channel_id=1, source_target_pairs={{0,3},{1,0},{2,1},{3,2},{4,7},{5,4},{6,5},{7,6},{8,11},{9,8},{10,9... | collective-permute-start | bytes 1867784 | tf_op jit(solution)/shard_map/ppermute | solution.py:254
  101.8 2.3 %all-to-all-done.2 = bf16[4,64,128]{2,1,0:T(8,128)(2,1)S(1)} async-done(((bf16[4,64,128]{2,1,0:T(8,128)(2,1)}), bf16[4,64,128]{2,1,0:T(8,128)(2,1)S(1)}, u32[]{:S(2)}, u32[]{:S(2)}) %all-to-all-start.2) | async-done | bytes 65568 | tf_op jit(solution)/shard_map/all_to_all | solution.py:264
  104.9 8.0 %all-to-all-start.3 = ((bf16[12,64,128]{2,1,0:T(8,128)(2,1)}), bf16[12,64,128]{2,1,0:T(8,128)(2,1)S(1)}, u32[]{:S(2)}, u32[]{:S(2)}) async-start(bf16[12,64,128]{2,1,0:T(8,128)(2,1)} %broadcast_in_dim.16), calls=%async_computation.3 | async-start | bytes 393216 | tf_op jit(solution)/shard_map/all_to_all | solution.py:268
  112.9 3.3 %collective-permute-done.2.refs_2_.refs_6_ = bf16[2432,128]{1,0:T(8,128)(2,1)S(1)} collective-permute-done((bf16[2432,128]{1,0:T(8,128)(2,1)}, bf16[2432,128]{1,0:T(8,128)(2,1)S(1)}, u32[]{:S(2)}, u32[]{:S(2)}) %collective-permute-start.2) | collective-permute-done | bytes 622624 | tf_op jit(solution)/shard_map/ppermute | solution.py:254
  116.2 11.8 %collective-permute-done.3.refs_3_.refs_7_ = bf16[2432,128]{1,0:T(8,128)(2,1)S(1)} collective-permute-done((bf16[2432,128]{1,0:T(8,128)(2,1)}, bf16[2432,128]{1,0:T(8,128)(2,1)S(1)}, u32[]{:S(2)}, u32[]{:S(2)}) %collective-permute-start.3) | collective-permute-done | bytes 622624 | tf_op jit(solution)/shard_map/ppermute | solution.py:254
  128.0 2.8 %input_grad.1 = bf16[384,2048]{1,0:T(8,128)(2,1)} custom-call(s32[1]{0:T(128)S(6)} %copy.7.counts_ref, bf16[2432,128]{1,0:T(8,128)(2,1)S(1)} %get-tuple-element.12.refs_0_.refs_4_, bf16[2432,128]{1,0:T(8,128)(2,1)S(1)} %collective-permute-done.1.refs_1_.refs_5_, bf16[2432,128]{1,0:T(8,128)(2,1)S(1)} %collective-permute-done.2.refs_2_.refs_6_, ...), custom_call_target="tpu_custom_call" | custom-call | flops 805306368 | bytes 3670016 | tf_op jit(solution)/shard_map/input_grad/pallas_call | solution.py:213
  (24 shorter events, 10.5 us)
Async XLA Ops:
  2.9 47.1 %all-to-all-start = ((bf16[8,768,128]{2,1,0:T(8,128)(2,1)}), bf16[8,768,128]{2,1,0:T(8,128)(2,1)S(1)}, u32[]{:S(2)}, u32[]{:S(2)}) async-start(bf16[8,768,128]{2,1,0:T(8,128)(2,1)} %broadcast_in_dim.6), calls=%async_computation | async-start | bytes 3145728 | tf_op jit(solution)/shard_map/all_to_all | solution.py:244
  17.9 5.5 %collective-permute-start.4 = (bf16[6144,128]{1,0:T(8,128)(2,1)}, bf16[6144,128]{1,0:T(8,128)(2,1)S(1)}, u32[]{:S(2)}, u32[]{:S(2)}) collective-permute-start(bf16[6144,128]{1,0:T(8,128)(2,1)} %get-tuple-element.17), channel_id=1, source_target_pairs={{0,4},{4,0},{8,12},{12,8},{16,20},{20,16},{24,28},{28,24},{32,36},... | collective-permute-start | bytes 4718600 | tf_op jit(solution)/shard_map/ppermute | solution.py:248
  23.4 1.4 %copy-start = (bf16[6144,128]{1,0:T(8,128)(2,1)S(1)}, bf16[6144,128]{1,0:T(8,128)(2,1)}, u32[]{:S(2)}) copy-start(bf16[6144,128]{1,0:T(8,128)(2,1)} %get-tuple-element.16.keep_ref) | copy-start | bytes 4718596
  26.1 0.8 copy-start.3
  26.9 27.1 %collective-permute-start.5 = (bf16[2048,128]{1,0:T(8,128)(2,1)}, bf16[2048,128]{1,0:T(8,128)(2,1)}, u32[]{:S(2)}, u32[]{:S(2)}) collective-permute-start(bf16[2048,128]{1,0:T(8,128)(2,1)} %get-tuple-element.19), channel_id=1, source_target_pairs={{0,64},{64,128},{128,192},{192,256},{256,320},{320,384},{384,448},... | collective-permute-start | bytes 1572872 | tf_op jit(solution)/shard_map/ppermute | solution.py:258
  31.1 24.0 %collective-permute-start.6 = (bf16[2048,128]{1,0:T(8,128)(2,1)}, bf16[2048,128]{1,0:T(8,128)(2,1)}, u32[]{:S(2)}, u32[]{:S(2)}) collective-permute-start(bf16[2048,128]{1,0:T(8,128)(2,1)} %get-tuple-element.20), channel_id=1, source_target_pairs={{0,704},{64,0},{128,64},{192,128},{256,192},{320,256},{384,320},{4... | collective-permute-start | bytes 1572872 | tf_op jit(solution)/shard_map/ppermute | solution.py:258
  50.0 14.8 %collective-permute-start = (bf16[6144,128]{1,0:T(8,128)(2,1)S(1)}, bf16[6144,128]{1,0:T(8,128)(2,1)S(1)}, u32[]{:S(2)}, u32[]{:S(2)}) collective-permute-start(bf16[6144,128]{1,0:T(8,128)(2,1)S(1)} %bitcast.6), channel_id=1, source_target_pairs={{0,4},{4,0},{8,12},{12,8},{16,20},{20,16},{24,28},{28,24},{32,36},... | collective-permute-start | bytes 4718600 | tf_op jit(solution)/shard_map/ppermute | solution.py:251
  55.1 10.7 %copy-start.4 = (bf16[384,128]{1,0:T(8,128)(2,1)S(1)}, bf16[384,128]{1,0:T(8,128)(2,1)}, u32[]{:S(2)}) copy-start(bf16[384,128]{1,0:T(8,128)(2,1)} %grad_ref.3) | copy-start | bytes 294916
  55.1 10.7 %copy-start.5 = (s32[16]{0:T(128)S(1)}, s32[16]{0:T(128)}, u32[]{:S(2)}) copy-start(s32[16]{0:T(128)} %blocks_ref.3) | copy-start | bytes 196
  57.5 24.3 %all-to-all-start.1 = ((bf16[8,256,128]{2,1,0:T(8,128)(2,1)}), bf16[8,256,128]{2,1,0:T(8,128)(2,1)}, u32[]{:S(2)}, u32[]{:S(2)}) async-start(bf16[8,256,128]{2,1,0:T(8,128)(2,1)} %bitcast.9), calls=%async_computation.1 | async-start | bytes 1048576 | tf_op jit(solution)/shard_map/all_to_all | solution.py:259
  64.7 1.1 copy-start.1
  65.9 1.4 %copy-start.2 = (bf16[6144,128]{1,0:T(8,128)(2,1)S(1)}, bf16[6144,128]{1,0:T(8,128)(2,1)}, u32[]{:S(2)}) copy-start(bf16[6144,128]{1,0:T(8,128)(2,1)} %copy-done.1) | copy-start | bytes 4718596
  69.7 0.9 copy-start.6
  70.6 0.8 copy-start.7
  83.6 20.6 %all-to-all-start.2 = ((bf16[4,64,128]{2,1,0:T(8,128)(2,1)}), bf16[4,64,128]{2,1,0:T(8,128)(2,1)S(1)}, u32[]{:S(2)}, u32[]{:S(2)}) async-start(bf16[4,64,128]{2,1,0:T(8,128)(2,1)} %bitcast.2), calls=%async_computation.2 | async-start | bytes 131072 | tf_op jit(solution)/shard_map/all_to_all | solution.py:264
  93.2 19.7 %collective-permute-start.1 = (bf16[2432,128]{1,0:T(8,128)(2,1)}, bf16[2432,128]{1,0:T(8,128)(2,1)S(1)}, u32[]{:S(2)}, u32[]{:S(2)}) collective-permute-start(bf16[2432,128]{1,0:T(8,128)(2,1)} %get-tuple-element.13), channel_id=1, source_target_pairs={{0,1},{1,2},{2,3},{3,0},{4,5},{5,6},{6,7},{7,4},{8,9},{9,10},{10,1... | collective-permute-start | bytes 1867784 | tf_op jit(solution)/shard_map/ppermute | solution.py:254
  95.6 20.6 %collective-permute-start.2 = (bf16[2432,128]{1,0:T(8,128)(2,1)}, bf16[2432,128]{1,0:T(8,128)(2,1)S(1)}, u32[]{:S(2)}, u32[]{:S(2)}) collective-permute-start(bf16[2432,128]{1,0:T(8,128)(2,1)} %copy-done.7), channel_id=1, source_target_pairs={{0,2},{1,3},{2,0},{3,1},{4,6},{5,7},{6,4},{7,5},{8,10},{9,11},{10,... | collective-permute-start | bytes 1867784 | tf_op jit(solution)/shard_map/ppermute | solution.py:254
  99.9 28.1 %collective-permute-start.3 = (bf16[2432,128]{1,0:T(8,128)(2,1)}, bf16[2432,128]{1,0:T(8,128)(2,1)S(1)}, u32[]{:S(2)}, u32[]{:S(2)}) collective-permute-start(bf16[2432,128]{1,0:T(8,128)(2,1)} %copy-done.6), channel_id=1, source_target_pairs={{0,3},{1,0},{2,1},{3,2},{4,7},{5,4},{6,5},{7,6},{8,11},{9,8},{10,9... | collective-permute-start | bytes 1867784 | tf_op jit(solution)/shard_map/ppermute | solution.py:254
  104.9 26.0 %all-to-all-start.3 = ((bf16[12,64,128]{2,1,0:T(8,128)(2,1)}), bf16[12,64,128]{2,1,0:T(8,128)(2,1)S(1)}, u32[]{:S(2)}, u32[]{:S(2)}) async-start(bf16[12,64,128]{2,1,0:T(8,128)(2,1)} %broadcast_in_dim.16), calls=%async_computation.3 | async-start | bytes 393216 | tf_op jit(solution)/shard_map/all_to_all | solution.py:268

commit v5 on v2

--- a/solution.py
+++ b/solution.py
@@ -9,8 +9,7 @@
 
 BLOCK = 128
 SPLIT = 3
-PIECE = 48
-PIECE_AT = (0, 48, 80)
+PIECE = 32
 SMALL = pltpu.CompilerParams(vmem_limit_bytes=12 * 1024 * 1024)
 
 
@@ -148,17 +147,18 @@
 
 def compact_kernel(slot_blocks, n_tp, blocks_ref, held_ref, grad_ref, *rest):
     outs, place = rest[:n_tp], rest[n_tp]
+    core = lax.rem(lax.axis_index("dp"), 2)
     index = lax.axis_index("tp")
-    half = held_ref.shape[0] // 2
+    side = [jnp.where(core == parity, 0, slot_blocks) for parity in range(2)]
     fill_places(
         blocks_ref, place, slot_blocks,
-        lambda owner, at: (owner % 2) * half + ((owner // 2) * slot_blocks + at) * PIECE,
+        lambda owner, at: (side[owner % 2] + (owner // 2) * 2 * slot_blocks + at) * PIECE,
     )
     per = (outs[0].shape[0] - grad_ref.shape[0]) // PIECE
     for k, out_ref in enumerate(outs):
         first = lax.rem(index + k, n_tp) * per
         for at in range(per):
-            source = pl.multiple_of(place[first + at], 16)
+            source = pl.multiple_of(place[first + at], PIECE)
             out_ref[at * PIECE:(at + 1) * PIECE, :] = held_ref[pl.ds(source, PIECE), :]
         out_ref[per * PIECE:, :] = grad_ref[...]
 
@@ -177,52 +177,81 @@
         compiler_params=SMALL,
         cost_estimate=pl.CostEstimate(flops=0, bytes_accessed=2 * rows * grad.shape[1], transcendentals=0),
         name="compact_rows",
-    )(shard_blocks, held.reshape(-1, held.shape[-1]), grad)
+    )(shard_blocks, held, grad)
+
+
+def stack_kernel(heads, *refs):
+    own, far, out_ref = refs[:heads], refs[heads:heads + 2], refs[-1]
+    half = heads // 2
+    for h in range(heads):
+        out_ref[h] = own[h][: out_ref.shape[1], :]
+        out_ref[heads + h] = far[h // half][h % half]
+
+
+def stacked(own, far, other):
+    n = len(own)
+    _, pieces, head = far[0].shape
+    vmem = pl.BlockSpec(memory_space=pltpu.VMEM)
+    return pl.pallas_call(
+        functools.partial(stack_kernel, n),
+        in_specs=[vmem] * (n + 2) + [pl.BlockSpec(memory_space=pl.ANY)],
+        out_specs=vmem,
+        out_shape=jax.ShapeDtypeStruct((2 * n, pieces, head), own[0].dtype),
+        compiler_params=SMALL,
+        cost_estimate=pl.CostEstimate(flops=0, bytes_accessed=8 * n * pieces * head, transcendentals=0),
+        name="stack_rows",
+    )(*own, *far, other)
 
 
 def input_kernel(heads, counts_ref, *refs):
-    own, (before_ref, after_ref), grads = refs[:heads], refs[heads:heads + 2], refs[heads + 2:2 * heads + 2]
-    out_ref, masked, weight = refs[2 * heads + 2:]
-    step = pl.program_id(0)
-    turn = lax.rem(lax.axis_index("rep"), SPLIT)
-    blocks = before_ref.shape[1] // PIECE
-
-    @pl.when(step == 0)
+    own, far, other_ref = refs[:heads], refs[heads:heads + 2], refs[heads + 2]
+    grads = refs[heads + 3:2 * heads + 3]
+    out_ref, masked, weight = refs[2 * heads + 3:]
+    turn = lax.rem(lax.axis_index("rep"), 2)
+    core = lax.rem(lax.axis_index("dp"), 2)
+    blocks = own[0].shape[0] // PIECE
+    half = heads // 2
+
+    @pl.when(pl.program_id(0) == 0)
     def _():
         for h in range(heads):
             grad = grads[h][...].astype(jnp.float32)
             live = lax.broadcasted_iota(jnp.int32, grad.shape, 0) < counts_ref[0]
             masked[:, h * BLOCK:(h + 1) * BLOCK] = jnp.where(live, grad, 0.0).astype(masked.dtype)
 
-    for piece_here in range(SPLIT):
-        @pl.when(turn == piece_here)
-        def _():
-            for shift in range(SPLIT):
-                first = PIECE_AT[(piece_here + shift) % SPLIT]
-                for h in range(heads):
-                    ref = (own[h], after_ref.at[h], before_ref.at[h])[shift]
-                    for b in range(blocks):
-                        weight[b * BLOCK + first:b * BLOCK + first + PIECE, h * BLOCK:(h + 1) * BLOCK] = ref[
-                            b * PIECE:(b + 1) * PIECE, :
-                        ]
+    for h in range(heads):
+        sources = (
+            (own[h], turn, core),
+            (far[h // half].at[h % half], 1 - turn, core),
+            (other_ref.at[h], turn, 1 - core),
+            (other_ref.at[heads + h], 1 - turn, 1 - core),
+        )
+        for ref, its_turn, its_core in sources:
+            first = (2 * its_turn + its_core) * PIECE
+            for b in range(blocks):
+                rows = pl.ds(pl.multiple_of(b * BLOCK + first, PIECE), PIECE)
+                weight[rows, h * BLOCK:(h + 1) * BLOCK] = ref[b * PIECE:(b + 1) * PIECE, :]
 
     out_ref[...] = lax.dot_general(
         masked[...], weight[...], (((1,), (1,)), ((), ())), preferred_element_type=jnp.float32
     ).astype(out_ref.dtype)
 
 
-def input_product(counts, own, before, after, rows_dev):
-    n_tp, pieces, head = before.shape
+def input_product(counts, own, far, other, rows_dev):
+    n_tp = len(own)
+    _, pieces, head = other.shape
     steps = 4
     blocks = pieces // PIECE // steps
     chunk = blocks * BLOCK
+    rows = blocks * PIECE
     return pl.pallas_call(
         functools.partial(input_kernel, n_tp),
         grid=(steps,),
         in_specs=[pl.BlockSpec(memory_space=pltpu.SMEM)]
-        + [pl.BlockSpec((blocks * PIECE, head), lambda i: (i, 0))] * n_tp
-        + [pl.BlockSpec((n_tp, blocks * PIECE, head), lambda i: (0, i, 0))] * 2
-        + [pl.BlockSpec((rows_dev, head), lambda i: (pieces // rows_dev, 0))] * n_tp,
+        + [pl.BlockSpec((rows, head), lambda i: (i, 0))] * n_tp
+        + [pl.BlockSpec((n_tp // 2, rows, head), lambda i: (0, i, 0))] * 2
+        + [pl.BlockSpec((2 * n_tp, rows, head), lambda i: (0, i, 0))]
+        + [pl.BlockSpec((pl.Element(rows_dev), pl.Element(head)), lambda i: (pieces, 0))] * n_tp,
         out_specs=pl.BlockSpec((rows_dev, chunk), lambda i: (0, i)),
         out_shape=jax.ShapeDtypeStruct((rows_dev, steps * chunk), jnp.bfloat16),
         scratch_shapes=[
@@ -236,7 +265,7 @@
             transcendentals=0,
         ),
         name="input_grad",
-    )(counts, *own, before, after, *own)
+    )(counts, *own, *far, other, *own)
 
 
 def ordered(array, other):
@@ -254,31 +283,36 @@
     up = [(i, (i + 1) % n_rep) for i in range(n_rep)]
     down = [(i, (i - 1) % n_rep) for i in range(n_rep)]
 
-    turn = lax.rem(lax.axis_index("rep"), SPLIT)
-    first = turn * PIECE_AT[1] - jnp.where(turn == 2, 2 * PIECE_AT[1] - PIECE_AT[2], 0)
-    piece = lax.dynamic_slice_in_dim(weight_shards.reshape(slot_blocks, BLOCK, head), first, PIECE, 1)
-    piece = piece.reshape(1, slot_blocks * PIECE, head)
+    core = lax.rem(lax.axis_index("dp"), 2)
+    turn = lax.rem(lax.axis_index("rep"), 2)
+    slot = weight_shards.reshape(slot_blocks, BLOCK, head)
+
+    def quarter(of_core):
+        rows = lax.dynamic_slice_in_dim(slot, (2 * turn + of_core) * PIECE, PIECE, 1)
+        return rows.reshape(slot_blocks * PIECE, head)
+
+    both = jnp.concatenate([quarter(core), lax.ppermute(quarter(1 - core), "dp", core_swap)])
     held = lax.all_to_all(
-        jnp.broadcast_to(piece, (n_y,) + piece.shape[1:]), "dp", 0, 0, axis_index_groups=along_y
-    ).reshape(n_y * slot_blocks * PIECE, head)
+        jnp.broadcast_to(both[None], (n_y,) + both.shape), "dp", 0, 0, axis_index_groups=along_y
+    ).reshape(n_y * both.shape[0], head)
     send, keep = grad_products(token_counts, shard_blocks, hidden_in, value_grad, slot_rows)
     received = lax.ppermute(send, "dp", core_swap)
     stay, to_next, to_last = paired_parts(keep, received)
 
-    pair = [[2 * y, 2 * y + 1] for y in range(n_y)]
-    held = lax.all_to_all(jnp.broadcast_to(held[None], (2,) + held.shape), "dp", 0, 0, axis_index_groups=pair)
+    part = summed([stay, lax.ppermute(to_next, "rep", up), lax.ppermute(to_last, "rep", down)])
+    held = ordered(held, part)
     sent = compacted(shard_blocks, held, value_grad, slot_rows, n_tp, width)
     own = [sent[0]] + [
         lax.ppermute(sent[k], "tp", [(i, (i + k) % n_tp) for i in range(n_tp)]) for k in range(1, n_tp)
     ]
-    pieces = jnp.stack([part[: part.shape[0] - rows_dev] for part in own])
-    before = lax.ppermute(pieces, "rep", up)
-    after = lax.ppermute(pieces, "rep", down)
-    input_grad = input_product(token_counts, own, before, after, rows_dev)
-
-    stay = ordered(stay, sent[0])
-    part = summed([stay, lax.ppermute(to_next, "rep", up), lax.ppermute(to_last, "rep", down)])
+    pieces = [part[: part.shape[0] - rows_dev] for part in own]
+    far = [
+        lax.ppermute(jnp.stack(pieces[: n_tp // 2]), "rep", up),
+        lax.ppermute(jnp.stack(pieces[n_tp // 2:]), "rep", down),
+    ]
+
     spread = lax.all_to_all(part.reshape(n_y, slot_rows // SPLIT, head), "dp", 0, 0, axis_index_groups=along_y)
+    spread = ordered(spread, pieces)
     owned = summed([spread[y] for y in range(n_y)])
     fellows = [[k + SPLIT * q for q in range(n_rep // SPLIT)] for k in range(SPLIT)]
     share_rows = slot_rows // n_rep
@@ -286,6 +320,8 @@
         owned.reshape(n_rep // SPLIT, share_rows, head), "rep", 0, 0, axis_index_groups=fellows
     )
     share = summed([shares[q] for q in range(n_rep // SPLIT)])
+    other = lax.ppermute(stacked(own, far, share), "dp", core_swap)
+    input_grad = input_product(token_counts, own, far, other, rows_dev)
     total = lax.all_to_all(jnp.broadcast_to(share[None], (n_rep,) + share.shape), "rep", 0, 0)
     weight_grad = finished(total.reshape(slot_rows, head), share_rows)
     return (input_grad, weight_grad)

time: 131 us -> 129 us (0.985)
  blocking collectives: 4.81 us -> 22.2 us
  starting transfers between devices: 68.5 us -> 58.1 us
  waiting for transfers between devices: 35.3 us -> 28.8 us
  local copies, waits for them, and re-layouts: 3.75 us -> 1.09 us
    all_to_all x1, blocking collectives: 4.81 us -> 22.2 us  [on_device(): lax.all_to_all(jnp.broadcast_to(share[None], (n_rep,) + share.shape), 're...]
    ppermute x2 -> x4, waiting for transfers between devices: 14.5 us -> 2.23 us  [the longest x1 1.25 us: on_device(): lax.ppermute(jnp.stack(pieces[:n_tp // 2]), 'rep', up)]
    ppermute x1, waiting for transfers between devices: 0.01 us -> 10.1 us  [on_device(): lax.ppermute(to_next, 'rep', up)]
    all_to_all x2 -> x1, starting transfers between devices: 14.4 us -> 7.11 us  [on_device(): lax.all_to_all(jnp.broadcast_to(both[None], (n_y,) + both.shape), 'dp', 0...]
    all_to_all x1, starting transfers between devices: 10.4 us -> 3.28 us  [on_device(): lax.all_to_all(owned.reshape(n_rep // SPLIT, share_rows, head), 'rep', 0,...]
    all_to_all x1, waiting for transfers between devices: 1.69 us -> 8.14 us  [on_device(): lax.all_to_all(owned.reshape(n_rep // SPLIT, share_rows, head), 'rep', 0,...]
    all_to_all x1, waiting for transfers between devices: 5.66 us -> 0.01 us  [on_device(): lax.all_to_all(part.reshape(n_y, slot_rows // SPLIT, head), 'dp', 0, 0, a...]
    ppermute x2 -> x4, starting transfers between devices: 8.27 us -> 13 us  [the longest x1 5.6 us: on_device(): lax.ppermute(jnp.stack(pieces[n_tp // 2:]), 'rep', down)]
  transfers between devices with their start and end apart: 12 -> 13, of which waited for: 8 -> 7; matrix products, arithmetic and copies ran while one was open for 4% -> 2% of each run, Pallas kernels for 4% -> 3%
where the time goes in v5:
time: 129 us; the launch traced here: 128 us
  starting transfers between devices  58.1 us (45%)
  waiting for transfers between devices  28.8 us (22%)
  blocking collectives  22.2 us (17%)
  Pallas kernels  14 us (11%)
  other arithmetic  1.78 us (1%)
  between operations  1.55 us (1%)
    all_to_all x1, blocking collectives, on_device(): lax.all_to_all(jnp.broadcast_to(share[None], (n_rep,) + share.shape), 're...  22.2 us
    ppermute x1, starting transfers between devices, on_device(): lax.ppermute(to_last, 'rep', down)  12.2 us
    ppermute x1, waiting for transfers between devices, on_device(): lax.ppermute(to_next, 'rep', up)  10.1 us
    ppermute x3, starting transfers between devices, on_device(): lax.ppermute(sent[k], 'tp', [(i, (i + k) % n_tp) for i in range(n_tp)])  9.23 us
    all_to_all x1, waiting for transfers between devices, on_device(): lax.all_to_all(owned.reshape(n_rep // SPLIT, share_rows, head), 'rep', 0,...  8.14 us
    pallas_call x1, Pallas kernels, grad_products(): pl.pallas_call(functools.partial(grad_kernel, chunk, slot_blocks), in_spe...  7.28 us
    ppermute x3, waiting for transfers between devices, on_device(): lax.ppermute(sent[k], 'tp', [(i, (i + k) % n_tp) for i in range(n_tp)])  7.19 us
    all_to_all x1, starting transfers between devices, on_device(): lax.all_to_all(jnp.broadcast_to(both[None], (n_y,) + both.shape), 'dp', 0...  7.11 us
  transfers between devices with their start and end apart: 13, of which 7 were waited for; matrix products, arithmetic and copies ran while one was open for 2% of the time, Pallas kernels for 3%

profile of v5, /device:TPU:6, one launch (start us, length us, event | category | flops | bytes accessed | tf_op | source)
XLA Modules:
  0.0 127.6 jit_solution(9413098753287074100)
XLA Ops:
  1.3 7.3 %grad_products.1 = (bf16[6144,128]{1,0:T(8,128)(2,1)}, bf16[6144,128]{1,0:T(8,128)(2,1)}) custom-call(s32[1]{0:T(128)S(6)} %copy.7.counts_ref, s32[16]{0:T(128)} %blocks_ref.3, bf16[384,8192]{1,0:T(8,128)(2,1)} %hidden_ref.1, bf16[384,128]{1,0:T(8,128)(2,1)} %grad_ref.3), custom_call_target="tpu_custom_call" | custom-call | flops 805306368 | bytes 9437184 | tf_op jit(solution)/shard_map/grad_products/pallas_call | solution.py:83
  8.6 2.1 %collective-permute-start.1 = (bf16[6144,128]{1,0:T(8,128)(2,1)}, bf16[6144,128]{1,0:T(8,128)(2,1)}, u32[]{:S(2)}, u32[]{:S(2)}) collective-permute-start(bf16[6144,128]{1,0:T(8,128)(2,1)} %get-tuple-element.14), channel_id=1, source_target_pairs={{0,4},{4,0},{8,12},{12,8},{16,20},{20,16},{24,28},{28,24},{32,36},... | collective-permute-start | bytes 4718600 | tf_op jit(solution)/shard_map/ppermute | solution.py:299
  10.7 2.4 %collective-permute-start = (bf16[192,128]{1,0:T(8,128)(2,1)S(1)}, bf16[192,128]{1,0:T(8,128)(2,1)S(1)}, u32[]{:S(2)}, u32[]{:S(2)}) collective-permute-start(bf16[192,128]{1,0:T(8,128)(2,1)S(1)} %bitcast.21), channel_id=1, source_target_pairs={{0,4},{4,0},{8,12},{12,8},{16,20},{20,16},{24,28},{28,24},{32,36},... | collective-permute-start | bytes 147464 | tf_op jit(solution)/shard_map/ppermute | solution.py:294
  14.1 1.0 broadcast_in_dim.4
  15.1 7.1 %all-to-all-start = ((bf16[8,384,128]{2,1,0:T(8,128)(2,1)}), bf16[8,384,128]{2,1,0:T(8,128)(2,1)S(1)}, u32[]{:S(2)}, u32[]{:S(2)}) async-start(bf16[8,384,128]{2,1,0:T(8,128)(2,1)} %broadcast_in_dim.4), calls=%async_computation | async-start | bytes 1572864 | tf_op jit(solution)/shard_map/all_to_all | solution.py:295
  22.2 1.8 %pair_parts.1 = (bf16[2048,128]{1,0:T(8,128)(2,1)S(1)}, bf16[2048,128]{1,0:T(8,128)(2,1)S(1)}, bf16[2048,128]{1,0:T(8,128)(2,1)S(1)}) custom-call(bf16[6144,128]{1,0:T(8,128)(2,1)S(1)} %copy-done, bf16[6144,128]{1,0:T(8,128)(2,1)} %collective-permute-done.1.received_ref), custom_call_target="tpu_custom_call" | custom-call | tf_op jit(solution)/shard_map/pair_parts/pallas_call | solution.py:117
  24.0 4.3 %collective-permute-start.2 = (bf16[2048,128]{1,0:T(8,128)(2,1)S(1)}, bf16[2048,128]{1,0:T(8,128)(2,1)S(1)}, u32[]{:S(2)}, u32[]{:S(2)}) collective-permute-start(bf16[2048,128]{1,0:T(8,128)(2,1)S(1)} %get-tuple-element.16), channel_id=1, source_target_pairs={{0,64},{64,128},{128,192},{192,256},{256,320},{320,384},{384,448},... | collective-permute-start | bytes 1572872 | tf_op jit(solution)/shard_map/ppermute | solution.py:302
  28.3 12.2 %collective-permute-start.3 = (bf16[2048,128]{1,0:T(8,128)(2,1)S(1)}, bf16[2048,128]{1,0:T(8,128)(2,1)S(1)}, u32[]{:S(2)}, u32[]{:S(2)}) collective-permute-start(bf16[2048,128]{1,0:T(8,128)(2,1)S(1)} %get-tuple-element.17), channel_id=1, source_target_pairs={{0,704},{64,0},{128,64},{192,128},{256,192},{320,256},{384,320},{4... | collective-permute-start | bytes 1572872 | tf_op jit(solution)/shard_map/ppermute | solution.py:302
  40.5 10.1 %collective-permute-done.2 = bf16[2048,128]{1,0:T(8,128)(2,1)S(1)} collective-permute-done((bf16[2048,128]{1,0:T(8,128)(2,1)S(1)}, bf16[2048,128]{1,0:T(8,128)(2,1)S(1)}, u32[]{:S(2)}, u32[]{:S(2)}) %collective-permute-start.2) | collective-permute-done | bytes 524320 | tf_op jit(solution)/shard_map/ppermute | solution.py:302
  50.6 1.2 collective-permute-done.3
  51.8 1.0 add_convert_fusion
  52.8 6.9 %all-to-all-start.1 = ((bf16[8,256,128]{2,1,0:T(8,128)(2,1)}), bf16[8,256,128]{2,1,0:T(8,128)(2,1)S(1)}, u32[]{:S(2)}, u32[]{:S(2)}) async-start(bf16[8,256,128]{2,1,0:T(8,128)(2,1)} %bitcast.8), calls=%async_computation.1 | async-start | bytes 1048576 | tf_op jit(solution)/shard_map/all_to_all | solution.py:314
  60.5 3.3 %collective-permute-start.5 = (bf16[896,128]{1,0:T(8,128)(2,1)S(1)}, bf16[896,128]{1,0:T(8,128)(2,1)S(1)}, u32[]{:S(2)}, u32[]{:S(2)}) collective-permute-start(bf16[896,128]{1,0:T(8,128)(2,1)S(1)} %get-tuple-element.21), channel_id=1, source_target_pairs={{0,2},{1,3},{2,0},{3,1},{4,6},{5,7},{6,4},{7,5},{8,10},{9,11},{10,... | collective-permute-start | bytes 688136 | tf_op jit(solution)/shard_map/ppermute | solution.py:306
  63.8 4.0 %collective-permute-start.4 = (bf16[896,128]{1,0:T(8,128)(2,1)S(1)}, bf16[896,128]{1,0:T(8,128)(2,1)S(1)}, u32[]{:S(2)}, u32[]{:S(2)}) collective-permute-start(bf16[896,128]{1,0:T(8,128)(2,1)S(1)} %get-tuple-element.20), channel_id=1, source_target_pairs={{0,1},{1,2},{2,3},{3,0},{4,5},{5,6},{6,7},{7,4},{8,9},{9,10},{10,1... | collective-permute-start | bytes 688136 | tf_op jit(solution)/shard_map/ppermute | solution.py:306
  67.8 1.9 %collective-permute-start.6 = (bf16[896,128]{1,0:T(8,128)(2,1)S(1)}, bf16[896,128]{1,0:T(8,128)(2,1)S(1)}, u32[]{:S(2)}, u32[]{:S(2)}) collective-permute-start(bf16[896,128]{1,0:T(8,128)(2,1)S(1)} %get-tuple-element.22), channel_id=1, source_target_pairs={{0,3},{1,0},{2,1},{3,2},{4,7},{5,4},{6,5},{7,6},{8,11},{9,8},{10,9... | collective-permute-start | bytes 688136 | tf_op jit(solution)/shard_map/ppermute | solution.py:306
  69.9 7.0 %collective-permute-done.6.refs_3_.refs_10_ = bf16[896,128]{1,0:T(8,128)(2,1)S(1)} collective-permute-done((bf16[896,128]{1,0:T(8,128)(2,1)S(1)}, bf16[896,128]{1,0:T(8,128)(2,1)S(1)}, u32[]{:S(2)}, u32[]{:S(2)}) %collective-permute-start.6) | collective-permute-done | bytes 229408 | tf_op jit(solution)/shard_map/ppermute | solution.py:306
  77.0 5.6 %collective-permute-start.8 = (bf16[2,512,128]{2,1,0:T(8,128)(2,1)S(1)}, bf16[2,512,128]{2,1,0:T(8,128)(2,1)S(1)}, u32[]{:S(2)}, u32[]{:S(2)}) collective-permute-start(bf16[2,512,128]{2,1,0:T(8,128)(2,1)S(1)} %pad_maximum_fusion.1), channel_id=1, source_target_pairs={{0,704},{64,0},{128,64},{192,128},{256,192},{320,256},{384,320},{4... | collective-permute-start | bytes 786440 | tf_op jit(solution)/shard_map/ppermute | solution.py:311
  83.3 3.3 %all-to-all-start.2 = ((bf16[4,64,128]{2,1,0:T(8,128)(2,1)}), bf16[4,64,128]{2,1,0:T(8,128)(2,1)S(1)}, u32[]{:S(2)}, u32[]{:S(2)}) async-start(bf16[4,64,128]{2,1,0:T(8,128)(2,1)} %bitcast.9), calls=%async_computation.2 | async-start | bytes 131072 | tf_op jit(solution)/shard_map/all_to_all | solution.py:319
  86.7 3.1 %collective-permute-start.7 = (bf16[2,512,128]{2,1,0:T(8,128)(2,1)S(1)}, bf16[2,512,128]{2,1,0:T(8,128)(2,1)S(1)}, u32[]{:S(2)}, u32[]{:S(2)}) collective-permute-start(bf16[2,512,128]{2,1,0:T(8,128)(2,1)S(1)} %pad_maximum_fusion), channel_id=1, source_target_pairs={{0,64},{64,128},{128,192},{192,256},{256,320},{320,384},{384,448},... | collective-permute-start | bytes 786440 | tf_op jit(solution)/shard_map/ppermute | solution.py:310
  89.8 8.1 %all-to-all-done.2 = bf16[4,64,128]{2,1,0:T(8,128)(2,1)S(1)} async-done(((bf16[4,64,128]{2,1,0:T(8,128)(2,1)}), bf16[4,64,128]{2,1,0:T(8,128)(2,1)S(1)}, u32[]{:S(2)}, u32[]{:S(2)}) %all-to-all-start.2) | async-done | bytes 65568 | tf_op jit(solution)/shard_map/all_to_all | solution.py:319
  97.9 1.3 collective-permute-done.7.refs_4_
  99.3 1.9 %collective-permute-start.9 = (bf16[8,512,128]{2,1,0:T(8,128)(2,1)S(1)}, bf16[8,512,128]{2,1,0:T(8,128)(2,1)S(1)}, u32[]{:S(2)}, u32[]{:S(2)}) collective-permute-start(bf16[8,512,128]{2,1,0:T(8,128)(2,1)S(1)} %stack_rows.1), channel_id=1, source_target_pairs={{0,4},{4,0},{8,12},{12,8},{16,20},{20,16},{24,28},{28,24},{32,36},... | collective-permute-start | bytes 3145736 | tf_op jit(solution)/shard_map/ppermute | solution.py:323
  101.2 22.2 %all_to_all.20 = bf16[12,64,128]{2,1,0:T(8,128)(2,1)S(1)} all-to-all(bf16[12,64,128]{2,1,0:T(8,128)(2,1)S(1)} %broadcast_in_dim.5), channel_id=1, replica_groups=mesh['rep'=12,'dp'=16,'tp'=4] {'rep'}, dimensions={0} | all-to-all | bytes 393216 | tf_op jit(solution)/shard_map/all_to_all | solution.py:325
  124.3 3.3 %input_grad.1 = bf16[384,2048]{1,0:T(8,128)(2,1)} custom-call(s32[1]{0:T(128)S(6)} %copy.7.counts_ref, bf16[896,128]{1,0:T(8,128)(2,1)S(1)} %get-tuple-element.19.refs_0_.refs_7_, bf16[896,128]{1,0:T(8,128)(2,1)S(1)} %collective-permute-done.4.refs_1_.refs_8_, bf16[896,128]{1,0:T(8,128)(2,1)S(1)} %collective-permute-done.5.refs_2_.refs_9_, ...), custom_call_target="tpu_custom_call" | custom-call | flops 805306368 | bytes 3670016 | tf_op jit(solution)/shard_map/input_grad/pallas_call | solution.py:247
  (30 shorter events, 3.7 us)
Async XLA Ops:
  1.3 9.4 %copy-start.3 = (bf16[768,128]{1,0:T(8,128)(2,1)S(1)}, bf16[768,128]{1,0:T(8,128)(2,1)}, u32[]{:S(2)}) copy-start(bf16[768,128]{1,0:T(8,128)(2,1)} %param.7) | copy-start | bytes 589828
  8.6 13.6 %copy-start = (bf16[6144,128]{1,0:T(8,128)(2,1)S(1)}, bf16[6144,128]{1,0:T(8,128)(2,1)}, u32[]{:S(2)}) copy-start(bf16[6144,128]{1,0:T(8,128)(2,1)} %get-tuple-element.13.keep_ref) | copy-start | bytes 4718596
  8.6 13.6 %collective-permute-start.1 = (bf16[6144,128]{1,0:T(8,128)(2,1)}, bf16[6144,128]{1,0:T(8,128)(2,1)}, u32[]{:S(2)}, u32[]{:S(2)}) collective-permute-start(bf16[6144,128]{1,0:T(8,128)(2,1)} %get-tuple-element.14), channel_id=1, source_target_pairs={{0,4},{4,0},{8,12},{12,8},{16,20},{20,16},{24,28},{28,24},{32,36},... | collective-permute-start | bytes 4718600 | tf_op jit(solution)/shard_map/ppermute | solution.py:299
  10.7 3.4 %collective-permute-start = (bf16[192,128]{1,0:T(8,128)(2,1)S(1)}, bf16[192,128]{1,0:T(8,128)(2,1)S(1)}, u32[]{:S(2)}, u32[]{:S(2)}) collective-permute-start(bf16[192,128]{1,0:T(8,128)(2,1)S(1)} %bitcast.21), channel_id=1, source_target_pairs={{0,4},{4,0},{8,12},{12,8},{16,20},{20,16},{24,28},{28,24},{32,36},... | collective-permute-start | bytes 147464 | tf_op jit(solution)/shard_map/ppermute | solution.py:294
  15.1 37.7 %all-to-all-start = ((bf16[8,384,128]{2,1,0:T(8,128)(2,1)}), bf16[8,384,128]{2,1,0:T(8,128)(2,1)S(1)}, u32[]{:S(2)}, u32[]{:S(2)}) async-start(bf16[8,384,128]{2,1,0:T(8,128)(2,1)} %broadcast_in_dim.4), calls=%async_computation | async-start | bytes 1572864 | tf_op jit(solution)/shard_map/all_to_all | solution.py:295
  24.0 26.6 %collective-permute-start.2 = (bf16[2048,128]{1,0:T(8,128)(2,1)S(1)}, bf16[2048,128]{1,0:T(8,128)(2,1)S(1)}, u32[]{:S(2)}, u32[]{:S(2)}) collective-permute-start(bf16[2048,128]{1,0:T(8,128)(2,1)S(1)} %get-tuple-element.16), channel_id=1, source_target_pairs={{0,64},{64,128},{128,192},{192,256},{256,320},{320,384},{384,448},... | collective-permute-start | bytes 1572872 | tf_op jit(solution)/shard_map/ppermute | solution.py:302
  28.3 23.5 %collective-permute-start.3 = (bf16[2048,128]{1,0:T(8,128)(2,1)S(1)}, bf16[2048,128]{1,0:T(8,128)(2,1)S(1)}, u32[]{:S(2)}, u32[]{:S(2)}) collective-permute-start(bf16[2048,128]{1,0:T(8,128)(2,1)S(1)} %get-tuple-element.17), channel_id=1, source_target_pairs={{0,704},{64,0},{128,64},{192,128},{256,192},{320,256},{384,320},{4... | collective-permute-start | bytes 1572872 | tf_op jit(solution)/shard_map/ppermute | solution.py:302
  51.8 7.9 %copy-start.1 = (bf16[384,128]{1,0:T(8,128)(2,1)S(1)}, bf16[384,128]{1,0:T(8,128)(2,1)}, u32[]{:S(2)}) copy-start(bf16[384,128]{1,0:T(8,128)(2,1)} %grad_ref.3) | copy-start | bytes 294916
  51.8 7.9 %copy-start.2 = (s32[16]{0:T(128)S(1)}, s32[16]{0:T(128)}, u32[]{:S(2)}) copy-start(s32[16]{0:T(128)} %blocks_ref.3) | copy-start | bytes 196
  52.8 29.8 %all-to-all-start.1 = ((bf16[8,256,128]{2,1,0:T(8,128)(2,1)}), bf16[8,256,128]{2,1,0:T(8,128)(2,1)S(1)}, u32[]{:S(2)}, u32[]{:S(2)}) async-start(bf16[8,256,128]{2,1,0:T(8,128)(2,1)} %bitcast.8), calls=%async_computation.1 | async-start | bytes 1048576 | tf_op jit(solution)/shard_map/all_to_all | solution.py:314
  60.5 9.4 %collective-permute-start.5 = (bf16[896,128]{1,0:T(8,128)(2,1)S(1)}, bf16[896,128]{1,0:T(8,128)(2,1)S(1)}, u32[]{:S(2)}, u32[]{:S(2)}) collective-permute-start(bf16[896,128]{1,0:T(8,128)(2,1)S(1)} %get-tuple-element.21), channel_id=1, source_target_pairs={{0,2},{1,3},{2,0},{3,1},{4,6},{5,7},{6,4},{7,5},{8,10},{9,11},{10,... | collective-permute-start | bytes 688136 | tf_op jit(solution)/shard_map/ppermute | solution.py:306
  63.8 18.8 %collective-permute-start.4 = (bf16[896,128]{1,0:T(8,128)(2,1)S(1)}, bf16[896,128]{1,0:T(8,128)(2,1)S(1)}, u32[]{:S(2)}, u32[]{:S(2)}) collective-permute-start(bf16[896,128]{1,0:T(8,128)(2,1)S(1)} %get-tuple-element.20), channel_id=1, source_target_pairs={{0,1},{1,2},{2,3},{3,0},{4,5},{5,6},{6,7},{7,4},{8,9},{9,10},{10,1... | collective-permute-start | bytes 688136 | tf_op jit(solution)/shard_map/ppermute | solution.py:306
  67.8 9.1 %collective-permute-start.6 = (bf16[896,128]{1,0:T(8,128)(2,1)S(1)}, bf16[896,128]{1,0:T(8,128)(2,1)S(1)}, u32[]{:S(2)}, u32[]{:S(2)}) collective-permute-start(bf16[896,128]{1,0:T(8,128)(2,1)S(1)} %get-tuple-element.22), channel_id=1, source_target_pairs={{0,3},{1,0},{2,1},{3,2},{4,7},{5,4},{6,5},{7,6},{8,11},{9,8},{10,9... | collective-permute-start | bytes 688136 | tf_op jit(solution)/shard_map/ppermute | solution.py:306
  77.0 20.9 %collective-permute-start.8 = (bf16[2,512,128]{2,1,0:T(8,128)(2,1)S(1)}, bf16[2,512,128]{2,1,0:T(8,128)(2,1)S(1)}, u32[]{:S(2)}, u32[]{:S(2)}) collective-permute-start(bf16[2,512,128]{2,1,0:T(8,128)(2,1)S(1)} %pad_maximum_fusion.1), channel_id=1, source_target_pairs={{0,704},{64,0},{128,64},{192,128},{256,192},{320,256},{384,320},{4... | collective-permute-start | bytes 786440 | tf_op jit(solution)/shard_map/ppermute | solution.py:311
  83.3 14.6 %all-to-all-start.2 = ((bf16[4,64,128]{2,1,0:T(8,128)(2,1)}), bf16[4,64,128]{2,1,0:T(8,128)(2,1)S(1)}, u32[]{:S(2)}, u32[]{:S(2)}) async-start(bf16[4,64,128]{2,1,0:T(8,128)(2,1)} %bitcast.9), calls=%async_computation.2 | async-start | bytes 131072 | tf_op jit(solution)/shard_map/all_to_all | solution.py:319
  86.7 12.5 %collective-permute-start.7 = (bf16[2,512,128]{2,1,0:T(8,128)(2,1)S(1)}, bf16[2,512,128]{2,1,0:T(8,128)(2,1)S(1)}, u32[]{:S(2)}, u32[]{:S(2)}) collective-permute-start(bf16[2,512,128]{2,1,0:T(8,128)(2,1)S(1)} %pad_maximum_fusion), channel_id=1, source_target_pairs={{0,64},{64,128},{128,192},{192,256},{256,320},{320,384},{384,448},... | collective-permute-start | bytes 786440 | tf_op jit(solution)/shard_map/ppermute | solution.py:310
  99.3 25.0 %collective-permute-start.9 = (bf16[8,512,128]{2,1,0:T(8,128)(2,1)S(1)}, bf16[8,512,128]{2,1,0:T(8,128)(2,1)S(1)}, u32[]{:S(2)}, u32[]{:S(2)}) collective-permute-start(bf16[8,512,128]{2,1,0:T(8,128)(2,1)S(1)} %stack_rows.1), channel_id=1, source_target_pairs={{0,4},{4,0},{8,12},{12,8},{16,20},{20,16},{24,28},{28,24},{32,36},... | collective-permute-start | bytes 3145736 | tf_op jit(solution)/shard_map/ppermute | solution.py:323

commit v6 on v5

--- a/solution.py
+++ b/solution.py
@@ -124,7 +124,7 @@
     return total.astype(parts[0].dtype)
 
 
-def finish_kernel(share, total_ref, out_ref):
+def finish_kernel(share, total_ref, done_ref, out_ref):
     n_rep = total_ref.shape[0] // share
     per = out_ref.shape[0] // SPLIT
     rows = [None] * (out_ref.shape[0] // share)
@@ -136,24 +136,20 @@
         out_ref[at * BLOCK:(at + 1) * BLOCK, :] = slot[at * BLOCK:(at + 1) * BLOCK, :].T
 
 
-def finished(total, share):
+def finished(total, share, done):
     return pl.pallas_call(
         functools.partial(finish_kernel, share),
+        in_specs=[pl.BlockSpec(memory_space=pltpu.VMEM), pl.BlockSpec(memory_space=pl.ANY)],
         out_shape=jax.ShapeDtypeStruct(total.shape, jnp.float32),
         compiler_params=SMALL,
         name="finish_weight_grad",
-    )(total)
+    )(total, done)
 
 
 def compact_kernel(slot_blocks, n_tp, blocks_ref, held_ref, grad_ref, *rest):
     outs, place = rest[:n_tp], rest[n_tp]
-    core = lax.rem(lax.axis_index("dp"), 2)
     index = lax.axis_index("tp")
-    side = [jnp.where(core == parity, 0, slot_blocks) for parity in range(2)]
-    fill_places(
-        blocks_ref, place, slot_blocks,
-        lambda owner, at: (side[owner % 2] + (owner // 2) * 2 * slot_blocks + at) * PIECE,
-    )
+    fill_places(blocks_ref, place, slot_blocks, lambda owner, at: (owner * slot_blocks + at) * PIECE)
     per = (outs[0].shape[0] - grad_ref.shape[0]) // PIECE
     for k, out_ref in enumerate(outs):
         first = lax.rem(index + k, n_tp) * per
@@ -181,39 +177,56 @@
 
 
 def stack_kernel(heads, *refs):
-    own, far, out_ref = refs[:heads], refs[heads:heads + 2], refs[-1]
-    half = heads // 2
+    own, out_ref = refs[:heads], refs[-1]
     for h in range(heads):
         out_ref[h] = own[h][: out_ref.shape[1], :]
-        out_ref[heads + h] = far[h // half][h % half]
-
-
-def stacked(own, far, other):
-    n = len(own)
-    _, pieces, head = far[0].shape
+
+
+def stacked(own, pieces, done):
+    n, head = len(own), own[0].shape[1]
     vmem = pl.BlockSpec(memory_space=pltpu.VMEM)
     return pl.pallas_call(
         functools.partial(stack_kernel, n),
-        in_specs=[vmem] * (n + 2) + [pl.BlockSpec(memory_space=pl.ANY)],
+        in_specs=[vmem] * n + [pl.BlockSpec(memory_space=pl.ANY)],
         out_specs=vmem,
-        out_shape=jax.ShapeDtypeStruct((2 * n, pieces, head), own[0].dtype),
+        out_shape=jax.ShapeDtypeStruct((n, pieces, head), own[0].dtype),
         compiler_params=SMALL,
-        cost_estimate=pl.CostEstimate(flops=0, bytes_accessed=8 * n * pieces * head, transcendentals=0),
+        cost_estimate=pl.CostEstimate(flops=0, bytes_accessed=4 * n * pieces * head, transcendentals=0),
         name="stack_rows",
-    )(*own, *far, other)
-
-
-def input_kernel(heads, counts_ref, *refs):
-    own, far, other_ref = refs[:heads], refs[heads:heads + 2], refs[heads + 2]
-    grads = refs[heads + 3:2 * heads + 3]
-    out_ref, masked, weight = refs[2 * heads + 3:]
+    )(*own, done)
+
+
+def halve_kernel(own_ref, other_ref, *outs):
+    half = own_ref.shape[0] // 2
+    for k, out_ref in enumerate(outs):
+        out_ref[:half] = own_ref[k * half:(k + 1) * half]
+        out_ref[half:] = other_ref[k * half:(k + 1) * half]
+
+
+def halved(own, other):
+    vmem = pl.BlockSpec(memory_space=pltpu.VMEM)
+    return pl.pallas_call(
+        halve_kernel,
+        in_specs=[vmem] * 2,
+        out_specs=[vmem] * 2,
+        out_shape=[jax.ShapeDtypeStruct(own.shape, own.dtype)] * 2,
+        compiler_params=SMALL,
+        cost_estimate=pl.CostEstimate(flops=0, bytes_accessed=8 * own.size, transcendentals=0),
+        name="halve_heads",
+    )(own, other)
+
+
+def input_kernel(heads, counts_ref, own_ref, other_ref, *refs):
+    far, grads = refs[:2], refs[2:heads + 2]
+    out_ref, done_ref, masked, weight = refs[heads + 2:]
     turn = lax.rem(lax.axis_index("rep"), 2)
     core = lax.rem(lax.axis_index("dp"), 2)
-    blocks = own[0].shape[0] // PIECE
+    blocks = own_ref.shape[1] // PIECE
     half = heads // 2
 
     @pl.when(pl.program_id(0) == 0)
     def _():
+        done_ref[...] = jnp.zeros_like(done_ref)
         for h in range(heads):
             grad = grads[h][...].astype(jnp.float32)
             live = lax.broadcasted_iota(jnp.int32, grad.shape, 0) < counts_ref[0]
@@ -221,10 +234,10 @@
 
     for h in range(heads):
         sources = (
-            (own[h], turn, core),
+            (own_ref.at[h], turn, core),
+            (other_ref.at[h], turn, 1 - core),
             (far[h // half].at[h % half], 1 - turn, core),
-            (other_ref.at[h], turn, 1 - core),
-            (other_ref.at[heads + h], 1 - turn, 1 - core),
+            (far[h // half].at[half + h % half], 1 - turn, 1 - core),
         )
         for ref, its_turn, its_core in sources:
             first = (2 * its_turn + its_core) * PIECE
@@ -237,23 +250,26 @@
     ).astype(out_ref.dtype)
 
 
-def input_product(counts, own, far, other, rows_dev):
-    n_tp = len(own)
-    _, pieces, head = other.shape
+def input_product(counts, parts, own, other, far, rows_dev):
+    n_tp, pieces, head = own.shape
     steps = 4
     blocks = pieces // PIECE // steps
     chunk = blocks * BLOCK
-    rows = blocks * PIECE
+    piece = pl.BlockSpec((n_tp, blocks * PIECE, head), lambda i: (0, i, 0))
     return pl.pallas_call(
         functools.partial(input_kernel, n_tp),
         grid=(steps,),
         in_specs=[pl.BlockSpec(memory_space=pltpu.SMEM)]
-        + [pl.BlockSpec((rows, head), lambda i: (i, 0))] * n_tp
-        + [pl.BlockSpec((n_tp // 2, rows, head), lambda i: (0, i, 0))] * 2
-        + [pl.BlockSpec((2 * n_tp, rows, head), lambda i: (0, i, 0))]
+        + [piece] * 4
         + [pl.BlockSpec((pl.Element(rows_dev), pl.Element(head)), lambda i: (pieces, 0))] * n_tp,
-        out_specs=pl.BlockSpec((rows_dev, chunk), lambda i: (0, i)),
-        out_shape=jax.ShapeDtypeStruct((rows_dev, steps * chunk), jnp.bfloat16),
+        out_specs=[
+            pl.BlockSpec((rows_dev, chunk), lambda i: (0, i)),
+            pl.BlockSpec((8, 128), lambda i: (0, 0)),
+        ],
+        out_shape=[
+            jax.ShapeDtypeStruct((rows_dev, steps * chunk), jnp.bfloat16),
+            jax.ShapeDtypeStruct((8, 128), jnp.float32),
+        ],
         scratch_shapes=[
             pltpu.VMEM((rows_dev, head * n_tp), jnp.bfloat16),
             pltpu.VMEM((chunk, head * n_tp), jnp.bfloat16),
@@ -265,7 +281,7 @@
             transcendentals=0,
         ),
         name="input_grad",
-    )(counts, *own, *far, other, *own)
+    )(counts, own, other, *far, *parts)
 
 
 def ordered(array, other):
@@ -283,18 +299,14 @@
     up = [(i, (i + 1) % n_rep) for i in range(n_rep)]
     down = [(i, (i - 1) % n_rep) for i in range(n_rep)]
 
-    core = lax.rem(lax.axis_index("dp"), 2)
     turn = lax.rem(lax.axis_index("rep"), 2)
-    slot = weight_shards.reshape(slot_blocks, BLOCK, head)
-
-    def quarter(of_core):
-        rows = lax.dynamic_slice_in_dim(slot, (2 * turn + of_core) * PIECE, PIECE, 1)
-        return rows.reshape(slot_blocks * PIECE, head)
-
-    both = jnp.concatenate([quarter(core), lax.ppermute(quarter(1 - core), "dp", core_swap)])
+    halves = lax.dynamic_slice_in_dim(
+        weight_shards.reshape(slot_blocks, BLOCK, head), 2 * turn * PIECE, 2 * PIECE, 1
+    )
+    quarters = halves.reshape(slot_blocks, 2, PIECE, head).swapaxes(0, 1).reshape(1, 2, slot_blocks * PIECE, head)
     held = lax.all_to_all(
-        jnp.broadcast_to(both[None], (n_y,) + both.shape), "dp", 0, 0, axis_index_groups=along_y
-    ).reshape(n_y * both.shape[0], head)
+        jnp.broadcast_to(quarters, (n_y,) + quarters.shape[1:]).reshape(n_dp, slot_blocks * PIECE, head), "dp", 0, 0
+    ).reshape(n_dp * slot_blocks * PIECE, head)
     send, keep = grad_products(token_counts, shard_blocks, hidden_in, value_grad, slot_rows)
     received = lax.ppermute(send, "dp", core_swap)
     stay, to_next, to_last = paired_parts(keep, received)
@@ -302,28 +314,26 @@
     part = summed([stay, lax.ppermute(to_next, "rep", up), lax.ppermute(to_last, "rep", down)])
     held = ordered(held, part)
     sent = compacted(shard_blocks, held, value_grad, slot_rows, n_tp, width)
-    own = [sent[0]] + [
+    parts = [sent[0]] + [
         lax.ppermute(sent[k], "tp", [(i, (i + k) % n_tp) for i in range(n_tp)]) for k in range(1, n_tp)
     ]
-    pieces = [part[: part.shape[0] - rows_dev] for part in own]
-    far = [
-        lax.ppermute(jnp.stack(pieces[: n_tp // 2]), "rep", up),
-        lax.ppermute(jnp.stack(pieces[n_tp // 2:]), "rep", down),
-    ]
 
     spread = lax.all_to_all(part.reshape(n_y, slot_rows // SPLIT, head), "dp", 0, 0, axis_index_groups=along_y)
-    spread = ordered(spread, pieces)
     owned = summed([spread[y] for y in range(n_y)])
+    own = stacked(parts, parts[0].shape[0] - rows_dev, spread)
+    other = lax.ppermute(own, "dp", core_swap)
+    first, second = halved(own, other)
+    far = [lax.ppermute(first, "rep", up), lax.ppermute(second, "rep", down)]
+    input_grad, done = input_product(token_counts, parts, own, other, far, rows_dev)
+
     fellows = [[k + SPLIT * q for q in range(n_rep // SPLIT)] for k in range(SPLIT)]
     share_rows = slot_rows // n_rep
     shares = lax.all_to_all(
         owned.reshape(n_rep // SPLIT, share_rows, head), "rep", 0, 0, axis_index_groups=fellows
     )
     share = summed([shares[q] for q in range(n_rep // SPLIT)])
-    other = lax.ppermute(stacked(own, far, share), "dp", core_swap)
-    input_grad = input_product(token_counts, own, far, other, rows_dev)
     total = lax.all_to_all(jnp.broadcast_to(share[None], (n_rep,) + share.shape), "rep", 0, 0)
-    weight_grad = finished(total.reshape(slot_rows, head), share_rows)
+    weight_grad = finished(total.reshape(slot_rows, head), share_rows, done)
     return (input_grad, weight_grad)
 
 

time: 129 us -> 119 us (0.922)
  blocking collectives: 22.2 us -> 0 us
  starting transfers between devices: 58.1 us -> 63.9 us
  Pallas kernels: 14 us -> 16.2 us
  local copies, waits for them, and re-layouts: 1.09 us -> 3.2 us
  waiting for transfers between devices: 28.8 us -> 30.8 us
    all_to_all x1 -> x0, blocking collectives: 22.2 us -> none  [on_device(): lax.all_to_all(jnp.broadcast_to(share[None], (n_rep,) + share.shape), 're...]
    all_to_all x1 -> x2, starting transfers between devices: 7.11 us -> 14.3 us  [the longest x1 7.27 us: on_device(): lax.all_to_all(jnp.broadcast_to(quarters, (n_y,) + quarters.shape[1:]).re...]
    all_to_all x1, waiting for transfers between devices: 8.14 us -> 1.72 us  [on_device(): lax.all_to_all(owned.reshape(n_rep // SPLIT, share_rows, head), 'rep', 0,...]
    ppermute x4 -> x3, waiting for transfers between devices: 2.23 us -> 7.03 us  [the longest x2 7.03 us: on_device(): far = [lax.ppermute(first, 'rep', up), lax.ppermute(second, 'rep', down)]]
    ppermute x4 -> x3, starting transfers between devices: 13 us -> 9.88 us  [the longest x2 7.96 us: on_device(): far = [lax.ppermute(first, 'rep', up), lax.ppermute(second, 'rep', down)]]
    all_to_all x1, starting transfers between devices: 3.28 us -> 5.85 us  [on_device(): lax.all_to_all(owned.reshape(n_rep // SPLIT, share_rows, head), 'rep', 0,...]
    all_to_all x1 -> x2, waiting for transfers between devices: 0.01 us -> 1.98 us  [the longest x1 1.98 us: on_device(): lax.all_to_all(jnp.broadcast_to(share[None], (n_rep,) + share.shape), 're...]
    unnamed x8, local copies, waits for them, and re-layouts: 0.02 us -> 1.42 us
  transfers between devices with their start and end apart: 13 -> 13, of which waited for: 7 -> 9; matrix products, arithmetic and copies ran while one was open for 2% -> 3% of each run, Pallas kernels for 3% -> 7%
where the time goes in v6:
time: 119 us; the launch traced here: 117 us
  starting transfers between devices  63.9 us (54%)
  waiting for transfers between devices  30.8 us (26%)
  Pallas kernels  16.2 us (14%)
  local copies, waits for them, and re-layouts  3.2 us (3%)
  other arithmetic  1.72 us (1%)
  between operations  1.51 us (1%)
    ppermute x1, starting transfers between devices, on_device(): lax.ppermute(to_last, 'rep', down)  12.2 us
    ppermute x1, waiting for transfers between devices, on_device(): lax.ppermute(to_next, 'rep', up)  10.5 us
    ppermute x3, starting transfers between devices, on_device(): lax.ppermute(sent[k], 'tp', [(i, (i + k) % n_tp) for i in range(n_tp)])  8.62 us
    ppermute x3, waiting for transfers between devices, on_device(): lax.ppermute(sent[k], 'tp', [(i, (i + k) % n_tp) for i in range(n_tp)])  8.34 us
    ppermute x2, starting transfers between devices, on_device(): far = [lax.ppermute(first, 'rep', up), lax.ppermute(second, 'rep', down)]  7.96 us
    pallas_call x1, Pallas kernels, grad_products(): pl.pallas_call(functools.partial(grad_kernel, chunk, slot_blocks), in_spe...  7.3 us
    all_to_all x1, starting transfers between devices, on_device(): lax.all_to_all(jnp.broadcast_to(quarters, (n_y,) + quarters.shape[1:]).re...  7.27 us
    ppermute x2, waiting for transfers between devices, on_device(): far = [lax.ppermute(first, 'rep', up), lax.ppermute(second, 'rep', down)]  7.03 us
  transfers between devices with their start and end apart: 13, of which 9 were waited for; matrix products, arithmetic and copies ran while one was open for 3% of the time, Pallas kernels for 7%

profile of v6, /device:TPU:6, one launch (start us, length us, event | category | flops | bytes accessed | tf_op | source)
XLA Modules:
  0.0 117.4 jit_solution(203528949544762794)
XLA Ops:
  1.3 7.3 %grad_products.1 = (bf16[6144,128]{1,0:T(8,128)(2,1)}, bf16[6144,128]{1,0:T(8,128)(2,1)}) custom-call(s32[1]{0:T(128)S(6)} %copy.8.counts_ref, s32[16]{0:T(128)} %blocks_ref.3, bf16[384,8192]{1,0:T(8,128)(2,1)} %hidden_ref.1, bf16[384,128]{1,0:T(8,128)(2,1)} %grad_ref.3), custom_call_target="tpu_custom_call" | custom-call | flops 805306368 | bytes 9437184 | tf_op jit(solution)/shard_map/grad_products/pallas_call | solution.py:83
  8.6 1.9 %collective-permute-start = (bf16[6144,128]{1,0:T(8,128)(2,1)}, bf16[6144,128]{1,0:T(8,128)(2,1)}, u32[]{:S(2)}, u32[]{:S(2)}) collective-permute-start(bf16[6144,128]{1,0:T(8,128)(2,1)} %get-tuple-element.17), channel_id=1, source_target_pairs={{0,4},{4,0},{8,12},{12,8},{16,20},{20,16},{24,28},{28,24},{32,36},... | collective-permute-start | bytes 4718600 | tf_op jit(solution)/shard_map/ppermute | solution.py:311
  11.7 7.3 %all-to-all-start = ((bf16[16,192,128]{2,1,0:T(8,128)(2,1)}), bf16[16,192,128]{2,1,0:T(8,128)(2,1)S(1)}, u32[]{:S(2)}, u32[]{:S(2)}) async-start(bf16[16,192,128]{2,1,0:T(8,128)(2,1)} %bitcast.4), calls=%async_computation | async-start | bytes 1572864 | tf_op jit(solution)/shard_map/all_to_all | solution.py:307
  20.4 1.8 %pair_parts.1 = (bf16[2048,128]{1,0:T(8,128)(2,1)S(1)}, bf16[2048,128]{1,0:T(8,128)(2,1)S(1)}, bf16[2048,128]{1,0:T(8,128)(2,1)S(1)}) custom-call(bf16[6144,128]{1,0:T(8,128)(2,1)S(1)} %copy-done.1, bf16[6144,128]{1,0:T(8,128)(2,1)} %collective-permute-done.received_ref), custom_call_target="tpu_custom_call" | custom-call | tf_op jit(solution)/shard_map/pair_parts/pallas_call | solution.py:117
  22.1 4.3 %collective-permute-start.1 = (bf16[2048,128]{1,0:T(8,128)(2,1)S(1)}, bf16[2048,128]{1,0:T(8,128)(2,1)S(1)}, u32[]{:S(2)}, u32[]{:S(2)}) collective-permute-start(bf16[2048,128]{1,0:T(8,128)(2,1)S(1)} %get-tuple-element.19), channel_id=1, source_target_pairs={{0,64},{64,128},{128,192},{192,256},{256,320},{320,384},{384,448},... | collective-permute-start | bytes 1572872 | tf_op jit(solution)/shard_map/ppermute | solution.py:314
  26.5 12.2 %collective-permute-start.2 = (bf16[2048,128]{1,0:T(8,128)(2,1)S(1)}, bf16[2048,128]{1,0:T(8,128)(2,1)S(1)}, u32[]{:S(2)}, u32[]{:S(2)}) collective-permute-start(bf16[2048,128]{1,0:T(8,128)(2,1)S(1)} %get-tuple-element.20), channel_id=1, source_target_pairs={{0,704},{64,0},{128,64},{192,128},{256,192},{320,256},{384,320},{4... | collective-permute-start | bytes 1572872 | tf_op jit(solution)/shard_map/ppermute | solution.py:314
  38.7 10.5 %collective-permute-done.1 = bf16[2048,128]{1,0:T(8,128)(2,1)S(1)} collective-permute-done((bf16[2048,128]{1,0:T(8,128)(2,1)S(1)}, bf16[2048,128]{1,0:T(8,128)(2,1)S(1)}, u32[]{:S(2)}, u32[]{:S(2)}) %collective-permute-start.1) | collective-permute-done | bytes 524320 | tf_op jit(solution)/shard_map/ppermute | solution.py:314
  51.4 6.8 %all-to-all-start.1 = ((bf16[8,256,128]{2,1,0:T(8,128)(2,1)}), bf16[8,256,128]{2,1,0:T(8,128)(2,1)S(1)}, u32[]{:S(2)}, u32[]{:S(2)}) async-start(bf16[8,256,128]{2,1,0:T(8,128)(2,1)} %bitcast.6), calls=%async_computation.1 | async-start | bytes 1048576 | tf_op jit(solution)/shard_map/all_to_all | solution.py:321
  59.0 2.4 %collective-permute-start.3 = (bf16[896,128]{1,0:T(8,128)(2,1)S(1)}, bf16[896,128]{1,0:T(8,128)(2,1)S(1)}, u32[]{:S(2)}, u32[]{:S(2)}) collective-permute-start(bf16[896,128]{1,0:T(8,128)(2,1)S(1)} %get-tuple-element.23), channel_id=1, source_target_pairs={{0,1},{1,2},{2,3},{3,0},{4,5},{5,6},{6,7},{7,4},{8,9},{9,10},{10,1... | collective-permute-start | bytes 688136 | tf_op jit(solution)/shard_map/ppermute | solution.py:318
  61.4 4.3 %collective-permute-start.4 = (bf16[896,128]{1,0:T(8,128)(2,1)S(1)}, bf16[896,128]{1,0:T(8,128)(2,1)S(1)}, u32[]{:S(2)}, u32[]{:S(2)}) collective-permute-start(bf16[896,128]{1,0:T(8,128)(2,1)S(1)} %get-tuple-element.24), channel_id=1, source_target_pairs={{0,2},{1,3},{2,0},{3,1},{4,6},{5,7},{6,4},{7,5},{8,10},{9,11},{10,... | collective-permute-start | bytes 688136 | tf_op jit(solution)/shard_map/ppermute | solution.py:318
  65.7 1.9 %collective-permute-start.5 = (bf16[896,128]{1,0:T(8,128)(2,1)S(1)}, bf16[896,128]{1,0:T(8,128)(2,1)S(1)}, u32[]{:S(2)}, u32[]{:S(2)}) collective-permute-start(bf16[896,128]{1,0:T(8,128)(2,1)S(1)} %get-tuple-element.25), channel_id=1, source_target_pairs={{0,3},{1,0},{2,1},{3,2},{4,7},{5,4},{6,5},{7,6},{8,11},{9,8},{10,9... | collective-permute-start | bytes 688136 | tf_op jit(solution)/shard_map/ppermute | solution.py:318
  67.7 1.8 %collective-permute-done.3.refs_1_.refs_3_ = bf16[896,128]{1,0:T(8,128)(2,1)S(1)} collective-permute-done((bf16[896,128]{1,0:T(8,128)(2,1)S(1)}, bf16[896,128]{1,0:T(8,128)(2,1)S(1)}, u32[]{:S(2)}, u32[]{:S(2)}) %collective-permute-start.3) | collective-permute-done | bytes 229408 | tf_op jit(solution)/shard_map/ppermute | solution.py:318
  69.5 2.7 %collective-permute-done.4.refs_2_.refs_4_ = bf16[896,128]{1,0:T(8,128)(2,1)S(1)} collective-permute-done((bf16[896,128]{1,0:T(8,128)(2,1)S(1)}, bf16[896,128]{1,0:T(8,128)(2,1)S(1)}, u32[]{:S(2)}, u32[]{:S(2)}) %collective-permute-start.4) | collective-permute-done | bytes 229408 | tf_op jit(solution)/shard_map/ppermute | solution.py:318
  72.2 3.9 %collective-permute-done.5.refs_3_.refs_5_ = bf16[896,128]{1,0:T(8,128)(2,1)S(1)} collective-permute-done((bf16[896,128]{1,0:T(8,128)(2,1)S(1)}, bf16[896,128]{1,0:T(8,128)(2,1)S(1)}, u32[]{:S(2)}, u32[]{:S(2)}) %collective-permute-start.5) | collective-permute-done | bytes 229408 | tf_op jit(solution)/shard_map/ppermute | solution.py:318
  76.0 1.9 %collective-permute-start.6 = (bf16[4,512,128]{2,1,0:T(8,128)(2,1)S(1)}, bf16[4,512,128]{2,1,0:T(8,128)(2,1)S(1)}, u32[]{:S(2)}, u32[]{:S(2)}) collective-permute-start(bf16[4,512,128]{2,1,0:T(8,128)(2,1)S(1)} %stack_rows.1.own_ref), channel_id=1, source_target_pairs={{0,4},{4,0},{8,12},{12,8},{16,20},{20,16},{24,28},{28,24},{32,36},... | collective-permute-start | bytes 1572872 | tf_op jit(solution)/shard_map/ppermute | solution.py:324
  78.7 5.8 %all-to-all-start.2 = ((bf16[4,64,128]{2,1,0:T(8,128)(2,1)}), bf16[4,64,128]{2,1,0:T(8,128)(2,1)S(1)}, u32[]{:S(2)}, u32[]{:S(2)}) async-start(bf16[4,64,128]{2,1,0:T(8,128)(2,1)} %bitcast.7), calls=%async_computation.2 | async-start | bytes 131072 | tf_op jit(solution)/shard_map/all_to_all | solution.py:331
  85.6 4.0 %collective-permute-start.7 = (bf16[4,512,128]{2,1,0:T(8,128)(2,1)}, bf16[4,512,128]{2,1,0:T(8,128)(2,1)S(1)}, u32[]{:S(2)}, u32[]{:S(2)}) collective-permute-start(bf16[4,512,128]{2,1,0:T(8,128)(2,1)} %get-tuple-element.26), channel_id=1, source_target_pairs={{0,64},{64,128},{128,192},{192,256},{256,320},{320,384},{384,448},... | collective-permute-start | bytes 1572872 | tf_op jit(solution)/shard_map/ppermute | solution.py:326
  89.5 4.0 %collective-permute-start.8 = (bf16[4,512,128]{2,1,0:T(8,128)(2,1)}, bf16[4,512,128]{2,1,0:T(8,128)(2,1)}, u32[]{:S(2)}, u32[]{:S(2)}) collective-permute-start(bf16[4,512,128]{2,1,0:T(8,128)(2,1)} %get-tuple-element.27), channel_id=1, source_target_pairs={{0,704},{64,0},{128,64},{192,128},{256,192},{320,256},{384,320},{4... | collective-permute-start | bytes 1572872 | tf_op jit(solution)/shard_map/ppermute | solution.py:326
  93.6 1.7 %all-to-all-done.2 = bf16[4,64,128]{2,1,0:T(8,128)(2,1)S(1)} async-done(((bf16[4,64,128]{2,1,0:T(8,128)(2,1)}), bf16[4,64,128]{2,1,0:T(8,128)(2,1)S(1)}, u32[]{:S(2)}, u32[]{:S(2)}) %all-to-all-start.2) | async-done | bytes 65568 | tf_op jit(solution)/shard_map/all_to_all | solution.py:331
  96.0 7.0 %all-to-all-start.3 = ((bf16[12,64,128]{2,1,0:T(8,128)(2,1)}), bf16[12,64,128]{2,1,0:T(8,128)(2,1)S(1)}, u32[]{:S(2)}, u32[]{:S(2)}) async-start(bf16[12,64,128]{2,1,0:T(8,128)(2,1)} %broadcast_in_dim.18), calls=%async_computation.3 | async-start | bytes 393216 | tf_op jit(solution)/shard_map/all_to_all | solution.py:335
  103.0 1.5 %collective-permute-done.7.refs_0_ = bf16[4,512,128]{2,1,0:T(8,128)(2,1)S(1)} collective-permute-done((bf16[4,512,128]{2,1,0:T(8,128)(2,1)}, bf16[4,512,128]{2,1,0:T(8,128)(2,1)S(1)}, u32[]{:S(2)}, u32[]{:S(2)}) %collective-permute-start.7) | collective-permute-done | bytes 524320 | tf_op jit(solution)/shard_map/ppermute | solution.py:326
  104.5 5.5 %collective-permute-done.8.refs_1_ = bf16[4,512,128]{2,1,0:T(8,128)(2,1)} collective-permute-done((bf16[4,512,128]{2,1,0:T(8,128)(2,1)}, bf16[4,512,128]{2,1,0:T(8,128)(2,1)}, u32[]{:S(2)}, u32[]{:S(2)}) %collective-permute-start.8) | collective-permute-done | bytes 524320 | tf_op jit(solution)/shard_map/ppermute | solution.py:326
  110.0 4.5 %input_grad.1 = (bf16[384,2048]{1,0:T(8,128)(2,1)}, f32[8,128]{1,0:T(8,128)S(1)}) custom-call(s32[1]{0:T(128)S(6)} %copy.8.counts_ref, bf16[4,512,128]{2,1,0:T(8,128)(2,1)S(1)} %stack_rows.1.own_ref, bf16[4,512,128]{2,1,0:T(8,128)(2,1)S(1)} %collective-permute-done.6.other_ref, bf16[4,512,128]{2,1,0:T(8,128)(2,1)S(1)} %collective-permute-done.7.refs_0_, ...), custom_call_target="tpu_custom_call" | custom-call | flops 805306368 | bytes 3670016 | tf_op jit(solution)/shard_map/input_grad/pallas_call | solution.py:259
  114.5 2.0 %all-to-all-done.3 = bf16[12,64,128]{2,1,0:T(8,128)(2,1)S(1)} async-done(((bf16[12,64,128]{2,1,0:T(8,128)(2,1)}), bf16[12,64,128]{2,1,0:T(8,128)(2,1)S(1)}, u32[]{:S(2)}, u32[]{:S(2)}) %all-to-all-start.3) | async-done | bytes 196640 | tf_op jit(solution)/shard_map/all_to_all | solution.py:335
  (24 shorter events, 8.8 us)
Async XLA Ops:
  0.6 10.0 %copy-start = (bf16[768,128]{1,0:T(8,128)(2,1)S(1)}, bf16[768,128]{1,0:T(8,128)(2,1)}, u32[]{:S(2)}) copy-start(bf16[768,128]{1,0:T(8,128)(2,1)} %param.7) | copy-start | bytes 589828
  8.6 10.3 %collective-permute-start = (bf16[6144,128]{1,0:T(8,128)(2,1)}, bf16[6144,128]{1,0:T(8,128)(2,1)}, u32[]{:S(2)}, u32[]{:S(2)}) collective-permute-start(bf16[6144,128]{1,0:T(8,128)(2,1)} %get-tuple-element.17), channel_id=1, source_target_pairs={{0,4},{4,0},{8,12},{12,8},{16,20},{20,16},{24,28},{28,24},{32,36},... | collective-permute-start | bytes 4718600 | tf_op jit(solution)/shard_map/ppermute | solution.py:311
  11.7 39.8 %all-to-all-start = ((bf16[16,192,128]{2,1,0:T(8,128)(2,1)}), bf16[16,192,128]{2,1,0:T(8,128)(2,1)S(1)}, u32[]{:S(2)}, u32[]{:S(2)}) async-start(bf16[16,192,128]{2,1,0:T(8,128)(2,1)} %bitcast.4), calls=%async_computation | async-start | bytes 1572864 | tf_op jit(solution)/shard_map/all_to_all | solution.py:307
  19.0 1.4 %copy-start.1 = (bf16[6144,128]{1,0:T(8,128)(2,1)S(1)}, bf16[6144,128]{1,0:T(8,128)(2,1)}, u32[]{:S(2)}) copy-start(bf16[6144,128]{1,0:T(8,128)(2,1)} %get-tuple-element.16.keep_ref) | copy-start | bytes 4718596
  22.1 27.1 %collective-permute-start.1 = (bf16[2048,128]{1,0:T(8,128)(2,1)S(1)}, bf16[2048,128]{1,0:T(8,128)(2,1)S(1)}, u32[]{:S(2)}, u32[]{:S(2)}) collective-permute-start(bf16[2048,128]{1,0:T(8,128)(2,1)S(1)} %get-tuple-element.19), channel_id=1, source_target_pairs={{0,64},{64,128},{128,192},{192,256},{256,320},{320,384},{384,448},... | collective-permute-start | bytes 1572872 | tf_op jit(solution)/shard_map/ppermute | solution.py:314
  26.5 24.0 %collective-permute-start.2 = (bf16[2048,128]{1,0:T(8,128)(2,1)S(1)}, bf16[2048,128]{1,0:T(8,128)(2,1)S(1)}, u32[]{:S(2)}, u32[]{:S(2)}) collective-permute-start(bf16[2048,128]{1,0:T(8,128)(2,1)S(1)} %get-tuple-element.20), channel_id=1, source_target_pairs={{0,704},{64,0},{128,64},{192,128},{256,192},{320,256},{384,320},{4... | collective-permute-start | bytes 1572872 | tf_op jit(solution)/shard_map/ppermute | solution.py:314
  50.4 7.8 %copy-start.2 = (bf16[384,128]{1,0:T(8,128)(2,1)S(1)}, bf16[384,128]{1,0:T(8,128)(2,1)}, u32[]{:S(2)}) copy-start(bf16[384,128]{1,0:T(8,128)(2,1)} %grad_ref.3) | copy-start | bytes 294916
  50.4 7.8 %copy-start.3 = (s32[16]{0:T(128)S(1)}, s32[16]{0:T(128)}, u32[]{:S(2)}) copy-start(s32[16]{0:T(128)} %blocks_ref.3) | copy-start | bytes 196
  51.4 24.6 %all-to-all-start.1 = ((bf16[8,256,128]{2,1,0:T(8,128)(2,1)}), bf16[8,256,128]{2,1,0:T(8,128)(2,1)S(1)}, u32[]{:S(2)}, u32[]{:S(2)}) async-start(bf16[8,256,128]{2,1,0:T(8,128)(2,1)} %bitcast.6), calls=%async_computation.1 | async-start | bytes 1048576 | tf_op jit(solution)/shard_map/all_to_all | solution.py:321
  59.0 10.4 %collective-permute-start.3 = (bf16[896,128]{1,0:T(8,128)(2,1)S(1)}, bf16[896,128]{1,0:T(8,128)(2,1)S(1)}, u32[]{:S(2)}, u32[]{:S(2)}) collective-permute-start(bf16[896,128]{1,0:T(8,128)(2,1)S(1)} %get-tuple-element.23), channel_id=1, source_target_pairs={{0,1},{1,2},{2,3},{3,0},{4,5},{5,6},{6,7},{7,4},{8,9},{9,10},{10,1... | collective-permute-start | bytes 688136 | tf_op jit(solution)/shard_map/ppermute | solution.py:318
  61.4 10.7 %collective-permute-start.4 = (bf16[896,128]{1,0:T(8,128)(2,1)S(1)}, bf16[896,128]{1,0:T(8,128)(2,1)S(1)}, u32[]{:S(2)}, u32[]{:S(2)}) collective-permute-start(bf16[896,128]{1,0:T(8,128)(2,1)S(1)} %get-tuple-element.24), channel_id=1, source_target_pairs={{0,2},{1,3},{2,0},{3,1},{4,6},{5,7},{6,4},{7,5},{8,10},{9,11},{10,... | collective-permute-start | bytes 688136 | tf_op jit(solution)/shard_map/ppermute | solution.py:318
  65.7 10.3 %collective-permute-start.5 = (bf16[896,128]{1,0:T(8,128)(2,1)S(1)}, bf16[896,128]{1,0:T(8,128)(2,1)S(1)}, u32[]{:S(2)}, u32[]{:S(2)}) collective-permute-start(bf16[896,128]{1,0:T(8,128)(2,1)S(1)} %get-tuple-element.25), channel_id=1, source_target_pairs={{0,3},{1,0},{2,1},{3,2},{4,7},{5,4},{6,5},{7,6},{8,11},{9,8},{10,9... | collective-permute-start | bytes 688136 | tf_op jit(solution)/shard_map/ppermute | solution.py:318
  76.0 8.5 %collective-permute-start.6 = (bf16[4,512,128]{2,1,0:T(8,128)(2,1)S(1)}, bf16[4,512,128]{2,1,0:T(8,128)(2,1)S(1)}, u32[]{:S(2)}, u32[]{:S(2)}) collective-permute-start(bf16[4,512,128]{2,1,0:T(8,128)(2,1)S(1)} %stack_rows.1.own_ref), channel_id=1, source_target_pairs={{0,4},{4,0},{8,12},{12,8},{16,20},{20,16},{24,28},{28,24},{32,36},... | collective-permute-start | bytes 1572872 | tf_op jit(solution)/shard_map/ppermute | solution.py:324
  78.7 16.6 %all-to-all-start.2 = ((bf16[4,64,128]{2,1,0:T(8,128)(2,1)}), bf16[4,64,128]{2,1,0:T(8,128)(2,1)S(1)}, u32[]{:S(2)}, u32[]{:S(2)}) async-start(bf16[4,64,128]{2,1,0:T(8,128)(2,1)} %bitcast.7), calls=%async_computation.2 | async-start | bytes 131072 | tf_op jit(solution)/shard_map/all_to_all | solution.py:331
  85.6 19.0 %collective-permute-start.7 = (bf16[4,512,128]{2,1,0:T(8,128)(2,1)}, bf16[4,512,128]{2,1,0:T(8,128)(2,1)S(1)}, u32[]{:S(2)}, u32[]{:S(2)}) collective-permute-start(bf16[4,512,128]{2,1,0:T(8,128)(2,1)} %get-tuple-element.26), channel_id=1, source_target_pairs={{0,64},{64,128},{128,192},{192,256},{256,320},{320,384},{384,448},... | collective-permute-start | bytes 1572872 | tf_op jit(solution)/shard_map/ppermute | solution.py:326
  89.5 20.5 %collective-permute-start.8 = (bf16[4,512,128]{2,1,0:T(8,128)(2,1)}, bf16[4,512,128]{2,1,0:T(8,128)(2,1)}, u32[]{:S(2)}, u32[]{:S(2)}) collective-permute-start(bf16[4,512,128]{2,1,0:T(8,128)(2,1)} %get-tuple-element.27), channel_id=1, source_target_pairs={{0,704},{64,0},{128,64},{192,128},{256,192},{320,256},{384,320},{4... | collective-permute-start | bytes 1572872 | tf_op jit(solution)/shard_map/ppermute | solution.py:326
  96.0 20.5 %all-to-all-start.3 = ((bf16[12,64,128]{2,1,0:T(8,128)(2,1)}), bf16[12,64,128]{2,1,0:T(8,128)(2,1)S(1)}, u32[]{:S(2)}, u32[]{:S(2)}) async-start(bf16[12,64,128]{2,1,0:T(8,128)(2,1)} %broadcast_in_dim.18), calls=%async_computation.3 | async-start | bytes 393216 | tf_op jit(solution)/shard_map/all_to_all | solution.py:335

commit v7 on v6

--- a/solution.py
+++ b/solution.py
@@ -124,26 +124,24 @@
     return total.astype(parts[0].dtype)
 
 
-def finish_kernel(share, total_ref, done_ref, out_ref):
-    n_rep = total_ref.shape[0] // share
-    per = out_ref.shape[0] // SPLIT
-    rows = [None] * (out_ref.shape[0] // share)
-    for rep in range(n_rep):
-        first = (rep % SPLIT) * per + (rep // SPLIT) * share
-        rows[first // share] = total_ref[rep * share:(rep + 1) * share, :].astype(out_ref.dtype)
-    slot = jnp.concatenate(rows, axis=0)
-    for at in range(out_ref.shape[0] // BLOCK):
-        out_ref[at * BLOCK:(at + 1) * BLOCK, :] = slot[at * BLOCK:(at + 1) * BLOCK, :].T
-
-
-def finished(total, share, done):
-    return pl.pallas_call(
-        functools.partial(finish_kernel, share),
-        in_specs=[pl.BlockSpec(memory_space=pltpu.VMEM), pl.BlockSpec(memory_space=pl.ANY)],
-        out_shape=jax.ShapeDtypeStruct(total.shape, jnp.float32),
+def finish_kernel(own_ref, before_ref, after_ref, done_ref, out_ref):
+    turn = lax.rem(lax.axis_index("rep"), SPLIT)
+    rows = own_ref.shape[0]
+    for shift, ref in ((0, own_ref), (SPLIT - 1, before_ref), (1, after_ref)):
+        first = lax.rem(turn + shift, SPLIT) * rows
+        for at in range(rows // BLOCK):
+            tile = ref[at * BLOCK:(at + 1) * BLOCK, :].astype(out_ref.dtype)
+            out_ref[pl.ds(pl.multiple_of(first + at * BLOCK, BLOCK), BLOCK), :] = tile.T
+
+
+def finished(own, before, after, done):
+    return pl.pallas_call(
+        finish_kernel,
+        in_specs=[pl.BlockSpec(memory_space=pltpu.VMEM)] * 3 + [pl.BlockSpec(memory_space=pl.ANY)],
+        out_shape=jax.ShapeDtypeStruct((SPLIT * own.shape[0], own.shape[1]), jnp.float32),
         compiler_params=SMALL,
         name="finish_weight_grad",
-    )(total, done)
+    )(own, before, after, done)
 
 
 def compact_kernel(slot_blocks, n_tp, blocks_ref, held_ref, grad_ref, *rest):
@@ -326,14 +324,13 @@
     far = [lax.ppermute(first, "rep", up), lax.ppermute(second, "rep", down)]
     input_grad, done = input_product(token_counts, parts, own, other, far, rows_dev)
 
-    fellows = [[k + SPLIT * q for q in range(n_rep // SPLIT)] for k in range(SPLIT)]
-    share_rows = slot_rows // n_rep
+    n_fellows = n_rep // SPLIT
+    fellows = [[k + SPLIT * q for q in range(n_fellows)] for k in range(SPLIT)]
     shares = lax.all_to_all(
-        owned.reshape(n_rep // SPLIT, share_rows, head), "rep", 0, 0, axis_index_groups=fellows
+        jnp.broadcast_to(owned[None], (n_fellows,) + owned.shape), "rep", 0, 0, axis_index_groups=fellows
     )
-    share = summed([shares[q] for q in range(n_rep // SPLIT)])
-    total = lax.all_to_all(jnp.broadcast_to(share[None], (n_rep,) + share.shape), "rep", 0, 0)
-    weight_grad = finished(total.reshape(slot_rows, head), share_rows, done)
+    third = summed([shares[q] for q in range(n_fellows)])
+    weight_grad = finished(third, lax.ppermute(third, "rep", up), lax.ppermute(third, "rep", down), done)
     return (input_grad, weight_grad)
 
 

time: 119 us -> 116 us (0.975)
  starting transfers between devices: 63.9 us -> 62.7 us
    all_to_all x2 -> x1, starting transfers between devices: 12.9 us -> 5.86 us  [on_device(): lax.all_to_all(jnp.broadcast_to(owned[None], (n_fellows,) + owned.shape),...]
    ppermute x0 -> x2, starting transfers between devices: none -> 5.84 us  [the longest x1 3.92 us: on_device(): lax.ppermute(third, 'rep', up)]
    ppermute x2, waiting for transfers between devices: 7.03 us -> 2.36 us  [on_device(): far = [lax.ppermute(first, 'rep', up), lax.ppermute(second, 'rep', down)]]
    all_to_all x2 -> x1, waiting for transfers between devices: 3.69 us -> 8.01 us  [on_device(): lax.all_to_all(jnp.broadcast_to(owned[None], (n_fellows,) + owned.shape),...]
  transfers between devices with their start and end apart: 13 -> 14, of which waited for: 9 -> 7; matrix products, arithmetic and copies ran while one was open for 3% -> 3% of each run, Pallas kernels for 7% -> 6%
where the time goes in v7:
time: 116 us; the launch traced here: 114 us
  starting transfers between devices  62.7 us (54%)
  waiting for transfers between devices  30.5 us (26%)
  Pallas kernels  15.1 us (13%)
  local copies, waits for them, and re-layouts  3.22 us (3%)
  between operations  1.53 us (1%)
    ppermute x1, starting transfers between devices, on_device(): lax.ppermute(to_last, 'rep', down)  12.2 us
    ppermute x1, waiting for transfers between devices, on_device(): lax.ppermute(to_next, 'rep', up)  10.5 us
    ppermute x3, starting transfers between devices, on_device(): lax.ppermute(sent[k], 'tp', [(i, (i + k) % n_tp) for i in range(n_tp)])  8.61 us
    ppermute x3, waiting for transfers between devices, on_device(): lax.ppermute(sent[k], 'tp', [(i, (i + k) % n_tp) for i in range(n_tp)])  8.33 us
    all_to_all x1, waiting for transfers between devices, on_device(): lax.all_to_all(jnp.broadcast_to(owned[None], (n_fellows,) + owned.shape),...  8.01 us
    ppermute x2, starting transfers between devices, on_device(): far = [lax.ppermute(first, 'rep', up), lax.ppermute(second, 'rep', down)]  7.95 us
    pallas_call x1, Pallas kernels, grad_products(): pl.pallas_call(functools.partial(grad_kernel, chunk, slot_blocks), in_spe...  7.3 us
    all_to_all x1, starting transfers between devices, on_device(): lax.all_to_all(jnp.broadcast_to(quarters, (n_y,) + quarters.shape[1:]).re...  7.28 us
  transfers between devices with their start and end apart: 14, of which 7 were waited for; matrix products, arithmetic and copies ran while one was open for 3% of the time, Pallas kernels for 6%

profile of v7, /device:TPU:6, one launch (start us, length us, event | category | flops | bytes accessed | tf_op | source)
XLA Modules:
  0.0 114.1 jit_solution(17072527410908675101)
XLA Ops:
  1.3 7.3 %grad_products.1 = (bf16[6144,128]{1,0:T(8,128)(2,1)}, bf16[6144,128]{1,0:T(8,128)(2,1)}) custom-call(s32[1]{0:T(128)S(6)} %copy.8.counts_ref, s32[16]{0:T(128)} %blocks_ref.3, bf16[384,8192]{1,0:T(8,128)(2,1)} %hidden_ref.1, bf16[384,128]{1,0:T(8,128)(2,1)} %grad_ref.3), custom_call_target="tpu_custom_call" | custom-call | flops 805306368 | bytes 9437184 | tf_op jit(solution)/shard_map/grad_products/pallas_call | solution.py:83
  8.6 1.9 %collective-permute-start = (bf16[6144,128]{1,0:T(8,128)(2,1)}, bf16[6144,128]{1,0:T(8,128)(2,1)}, u32[]{:S(2)}, u32[]{:S(2)}) collective-permute-start(bf16[6144,128]{1,0:T(8,128)(2,1)} %get-tuple-element.17), channel_id=1, source_target_pairs={{0,4},{4,0},{8,12},{12,8},{16,20},{20,16},{24,28},{28,24},{32,36},... | collective-permute-start | bytes 4718600 | tf_op jit(solution)/shard_map/ppermute | solution.py:309
  11.7 7.3 %all-to-all-start = ((bf16[16,192,128]{2,1,0:T(8,128)(2,1)}), bf16[16,192,128]{2,1,0:T(8,128)(2,1)S(1)}, u32[]{:S(2)}, u32[]{:S(2)}) async-start(bf16[16,192,128]{2,1,0:T(8,128)(2,1)} %bitcast.4), calls=%async_computation | async-start | bytes 1572864 | tf_op jit(solution)/shard_map/all_to_all | solution.py:305
  19.0 1.4 %copy-done.1 = bf16[6144,128]{1,0:T(8,128)(2,1)S(1)} copy-done((bf16[6144,128]{1,0:T(8,128)(2,1)S(1)}, bf16[6144,128]{1,0:T(8,128)(2,1)}, u32[]{:S(2)}) %copy-start.1) | copy-done | bytes 1572888
  20.4 1.8 %pair_parts.1 = (bf16[2048,128]{1,0:T(8,128)(2,1)S(1)}, bf16[2048,128]{1,0:T(8,128)(2,1)S(1)}, bf16[2048,128]{1,0:T(8,128)(2,1)S(1)}) custom-call(bf16[6144,128]{1,0:T(8,128)(2,1)S(1)} %copy-done.1, bf16[6144,128]{1,0:T(8,128)(2,1)} %collective-permute-done.received_ref), custom_call_target="tpu_custom_call" | custom-call | tf_op jit(solution)/shard_map/pair_parts/pallas_call | solution.py:117
  22.1 4.3 %collective-permute-start.1 = (bf16[2048,128]{1,0:T(8,128)(2,1)S(1)}, bf16[2048,128]{1,0:T(8,128)(2,1)S(1)}, u32[]{:S(2)}, u32[]{:S(2)}) collective-permute-start(bf16[2048,128]{1,0:T(8,128)(2,1)S(1)} %get-tuple-element.19), channel_id=1, source_target_pairs={{0,64},{64,128},{128,192},{192,256},{256,320},{320,384},{384,448},... | collective-permute-start | bytes 1572872 | tf_op jit(solution)/shard_map/ppermute | solution.py:312
  26.4 12.2 %collective-permute-start.2 = (bf16[2048,128]{1,0:T(8,128)(2,1)S(1)}, bf16[2048,128]{1,0:T(8,128)(2,1)S(1)}, u32[]{:S(2)}, u32[]{:S(2)}) collective-permute-start(bf16[2048,128]{1,0:T(8,128)(2,1)S(1)} %get-tuple-element.20), channel_id=1, source_target_pairs={{0,704},{64,0},{128,64},{192,128},{256,192},{320,256},{384,320},{4... | collective-permute-start | bytes 1572872 | tf_op jit(solution)/shard_map/ppermute | solution.py:312
  38.7 10.5 %collective-permute-done.1 = bf16[2048,128]{1,0:T(8,128)(2,1)S(1)} collective-permute-done((bf16[2048,128]{1,0:T(8,128)(2,1)S(1)}, bf16[2048,128]{1,0:T(8,128)(2,1)S(1)}, u32[]{:S(2)}, u32[]{:S(2)}) %collective-permute-start.1) | collective-permute-done | bytes 524320 | tf_op jit(solution)/shard_map/ppermute | solution.py:312
  51.4 6.8 %all-to-all-start.1 = ((bf16[8,256,128]{2,1,0:T(8,128)(2,1)}), bf16[8,256,128]{2,1,0:T(8,128)(2,1)S(1)}, u32[]{:S(2)}, u32[]{:S(2)}) async-start(bf16[8,256,128]{2,1,0:T(8,128)(2,1)} %bitcast.6), calls=%async_computation.1 | async-start | bytes 1048576 | tf_op jit(solution)/shard_map/all_to_all | solution.py:319
  59.0 2.4 %collective-permute-start.3 = (bf16[896,128]{1,0:T(8,128)(2,1)S(1)}, bf16[896,128]{1,0:T(8,128)(2,1)S(1)}, u32[]{:S(2)}, u32[]{:S(2)}) collective-permute-start(bf16[896,128]{1,0:T(8,128)(2,1)S(1)} %get-tuple-element.23), channel_id=1, source_target_pairs={{0,1},{1,2},{2,3},{3,0},{4,5},{5,6},{6,7},{7,4},{8,9},{9,10},{10,1... | collective-permute-start | bytes 688136 | tf_op jit(solution)/shard_map/ppermute | solution.py:316
  61.4 4.3 %collective-permute-start.4 = (bf16[896,128]{1,0:T(8,128)(2,1)S(1)}, bf16[896,128]{1,0:T(8,128)(2,1)S(1)}, u32[]{:S(2)}, u32[]{:S(2)}) collective-permute-start(bf16[896,128]{1,0:T(8,128)(2,1)S(1)} %get-tuple-element.24), channel_id=1, source_target_pairs={{0,2},{1,3},{2,0},{3,1},{4,6},{5,7},{6,4},{7,5},{8,10},{9,11},{10,... | collective-permute-start | bytes 688136 | tf_op jit(solution)/shard_map/ppermute | solution.py:316
  65.7 1.9 %collective-permute-start.5 = (bf16[896,128]{1,0:T(8,128)(2,1)S(1)}, bf16[896,128]{1,0:T(8,128)(2,1)S(1)}, u32[]{:S(2)}, u32[]{:S(2)}) collective-permute-start(bf16[896,128]{1,0:T(8,128)(2,1)S(1)} %get-tuple-element.25), channel_id=1, source_target_pairs={{0,3},{1,0},{2,1},{3,2},{4,7},{5,4},{6,5},{7,6},{8,11},{9,8},{10,9... | collective-permute-start | bytes 688136 | tf_op jit(solution)/shard_map/ppermute | solution.py:316
  67.7 1.8 %collective-permute-done.3.refs_1_.refs_3_ = bf16[896,128]{1,0:T(8,128)(2,1)S(1)} collective-permute-done((bf16[896,128]{1,0:T(8,128)(2,1)S(1)}, bf16[896,128]{1,0:T(8,128)(2,1)S(1)}, u32[]{:S(2)}, u32[]{:S(2)}) %collective-permute-start.3) | collective-permute-done | bytes 229408 | tf_op jit(solution)/shard_map/ppermute | solution.py:316
  69.5 2.7 %collective-permute-done.4.refs_2_.refs_4_ = bf16[896,128]{1,0:T(8,128)(2,1)S(1)} collective-permute-done((bf16[896,128]{1,0:T(8,128)(2,1)S(1)}, bf16[896,128]{1,0:T(8,128)(2,1)S(1)}, u32[]{:S(2)}, u32[]{:S(2)}) %collective-permute-start.4) | collective-permute-done | bytes 229408 | tf_op jit(solution)/shard_map/ppermute | solution.py:316
  72.1 3.9 %collective-permute-done.5.refs_3_.refs_5_ = bf16[896,128]{1,0:T(8,128)(2,1)S(1)} collective-permute-done((bf16[896,128]{1,0:T(8,128)(2,1)S(1)}, bf16[896,128]{1,0:T(8,128)(2,1)S(1)}, u32[]{:S(2)}, u32[]{:S(2)}) %collective-permute-start.5) | collective-permute-done | bytes 229408 | tf_op jit(solution)/shard_map/ppermute | solution.py:316
  76.0 1.9 %collective-permute-start.6 = (bf16[4,512,128]{2,1,0:T(8,128)(2,1)S(1)}, bf16[4,512,128]{2,1,0:T(8,128)(2,1)S(1)}, u32[]{:S(2)}, u32[]{:S(2)}) collective-permute-start(bf16[4,512,128]{2,1,0:T(8,128)(2,1)S(1)} %stack_rows.1.own_ref), channel_id=1, source_target_pairs={{0,4},{4,0},{8,12},{12,8},{16,20},{20,16},{24,28},{28,24},{32,36},... | collective-permute-start | bytes 1572872 | tf_op jit(solution)/shard_map/ppermute | solution.py:322
  78.8 5.9 %all-to-all-start.2 = ((bf16[4,256,128]{2,1,0:T(8,128)(2,1)}), bf16[4,256,128]{2,1,0:T(8,128)(2,1)S(1)}, u32[]{:S(2)}, u32[]{:S(2)}) async-start(bf16[4,256,128]{2,1,0:T(8,128)(2,1)} %broadcast_in_dim.18), calls=%async_computation.2 | async-start | bytes 524288 | tf_op jit(solution)/shard_map/all_to_all | solution.py:329
  85.7 4.0 %collective-permute-start.7 = (bf16[4,512,128]{2,1,0:T(8,128)(2,1)}, bf16[4,512,128]{2,1,0:T(8,128)(2,1)S(1)}, u32[]{:S(2)}, u32[]{:S(2)}) collective-permute-start(bf16[4,512,128]{2,1,0:T(8,128)(2,1)} %get-tuple-element.26), channel_id=1, source_target_pairs={{0,64},{64,128},{128,192},{192,256},{256,320},{320,384},{384,448},... | collective-permute-start | bytes 1572872 | tf_op jit(solution)/shard_map/ppermute | solution.py:324
  89.7 4.0 %collective-permute-start.8 = (bf16[4,512,128]{2,1,0:T(8,128)(2,1)}, bf16[4,512,128]{2,1,0:T(8,128)(2,1)S(1)}, u32[]{:S(2)}, u32[]{:S(2)}) collective-permute-start(bf16[4,512,128]{2,1,0:T(8,128)(2,1)} %get-tuple-element.27), channel_id=1, source_target_pairs={{0,704},{64,0},{128,64},{192,128},{256,192},{320,256},{384,320},{4... | collective-permute-start | bytes 1572872 | tf_op jit(solution)/shard_map/ppermute | solution.py:324
  93.7 8.0 %all-to-all-done.2 = bf16[4,256,128]{2,1,0:T(8,128)(2,1)S(1)} async-done(((bf16[4,256,128]{2,1,0:T(8,128)(2,1)}), bf16[4,256,128]{2,1,0:T(8,128)(2,1)S(1)}, u32[]{:S(2)}, u32[]{:S(2)}) %all-to-all-start.2) | async-done | bytes 262176 | tf_op jit(solution)/shard_map/all_to_all | solution.py:329
  101.7 1.9 %collective-permute-start.10 = (bf16[256,128]{1,0:T(8,128)(2,1)S(1)}, bf16[256,128]{1,0:T(8,128)(2,1)S(1)}, u32[]{:S(2)}, u32[]{:S(2)}) collective-permute-start(bf16[256,128]{1,0:T(8,128)(2,1)S(1)} %fusion.1.own_ref), channel_id=1, source_target_pairs={{0,704},{64,0},{128,64},{192,128},{256,192},{320,256},{384,320},{4... | collective-permute-start | bytes 196616 | tf_op jit(solution)/shard_map/ppermute | solution.py:333
  103.6 3.9 %collective-permute-start.9 = (bf16[256,128]{1,0:T(8,128)(2,1)S(1)}, bf16[256,128]{1,0:T(8,128)(2,1)S(1)}, u32[]{:S(2)}, u32[]{:S(2)}) collective-permute-start(bf16[256,128]{1,0:T(8,128)(2,1)S(1)} %fusion.1.own_ref), channel_id=1, source_target_pairs={{0,64},{64,128},{128,192},{192,256},{256,320},{320,384},{384,448},... | collective-permute-start | bytes 196616 | tf_op jit(solution)/shard_map/ppermute | solution.py:333
  107.6 2.4 %collective-permute-done.7.refs_0_ = bf16[4,512,128]{2,1,0:T(8,128)(2,1)S(1)} collective-permute-done((bf16[4,512,128]{2,1,0:T(8,128)(2,1)}, bf16[4,512,128]{2,1,0:T(8,128)(2,1)S(1)}, u32[]{:S(2)}, u32[]{:S(2)}) %collective-permute-start.7) | collective-permute-done | bytes 524320 | tf_op jit(solution)/shard_map/ppermute | solution.py:324
  109.9 3.3 %input_grad.1 = (bf16[384,2048]{1,0:T(8,128)(2,1)}, f32[8,128]{1,0:T(8,128)S(1)}) custom-call(s32[1]{0:T(128)S(6)} %copy.8.counts_ref, bf16[4,512,128]{2,1,0:T(8,128)(2,1)S(1)} %stack_rows.1.own_ref, bf16[4,512,128]{2,1,0:T(8,128)(2,1)S(1)} %collective-permute-done.6.other_ref, bf16[4,512,128]{2,1,0:T(8,128)(2,1)S(1)} %collective-permute-done.7.refs_0_, ...), custom_call_target="tpu_custom_call" | custom-call | flops 805306368 | bytes 3670016 | tf_op jit(solution)/shard_map/input_grad/pallas_call | solution.py:257
  (26 shorter events, 6.8 us)
Async XLA Ops:
  0.6 10.0 %copy-start = (bf16[768,128]{1,0:T(8,128)(2,1)S(1)}, bf16[768,128]{1,0:T(8,128)(2,1)}, u32[]{:S(2)}) copy-start(bf16[768,128]{1,0:T(8,128)(2,1)} %param.7) | copy-start | bytes 589828
  8.6 10.3 %collective-permute-start = (bf16[6144,128]{1,0:T(8,128)(2,1)}, bf16[6144,128]{1,0:T(8,128)(2,1)}, u32[]{:S(2)}, u32[]{:S(2)}) collective-permute-start(bf16[6144,128]{1,0:T(8,128)(2,1)} %get-tuple-element.17), channel_id=1, source_target_pairs={{0,4},{4,0},{8,12},{12,8},{16,20},{20,16},{24,28},{28,24},{32,36},... | collective-permute-start | bytes 4718600 | tf_op jit(solution)/shard_map/ppermute | solution.py:309
  11.7 39.8 %all-to-all-start = ((bf16[16,192,128]{2,1,0:T(8,128)(2,1)}), bf16[16,192,128]{2,1,0:T(8,128)(2,1)S(1)}, u32[]{:S(2)}, u32[]{:S(2)}) async-start(bf16[16,192,128]{2,1,0:T(8,128)(2,1)} %bitcast.4), calls=%async_computation | async-start | bytes 1572864 | tf_op jit(solution)/shard_map/all_to_all | solution.py:305
  19.0 1.4 %copy-start.1 = (bf16[6144,128]{1,0:T(8,128)(2,1)S(1)}, bf16[6144,128]{1,0:T(8,128)(2,1)}, u32[]{:S(2)}) copy-start(bf16[6144,128]{1,0:T(8,128)(2,1)} %get-tuple-element.16.keep_ref) | copy-start | bytes 4718596
  22.1 27.1 %collective-permute-start.1 = (bf16[2048,128]{1,0:T(8,128)(2,1)S(1)}, bf16[2048,128]{1,0:T(8,128)(2,1)S(1)}, u32[]{:S(2)}, u32[]{:S(2)}) collective-permute-start(bf16[2048,128]{1,0:T(8,128)(2,1)S(1)} %get-tuple-element.19), channel_id=1, source_target_pairs={{0,64},{64,128},{128,192},{192,256},{256,320},{320,384},{384,448},... | collective-permute-start | bytes 1572872 | tf_op jit(solution)/shard_map/ppermute | solution.py:312
  26.4 24.0 %collective-permute-start.2 = (bf16[2048,128]{1,0:T(8,128)(2,1)S(1)}, bf16[2048,128]{1,0:T(8,128)(2,1)S(1)}, u32[]{:S(2)}, u32[]{:S(2)}) collective-permute-start(bf16[2048,128]{1,0:T(8,128)(2,1)S(1)} %get-tuple-element.20), channel_id=1, source_target_pairs={{0,704},{64,0},{128,64},{192,128},{256,192},{320,256},{384,320},{4... | collective-permute-start | bytes 1572872 | tf_op jit(solution)/shard_map/ppermute | solution.py:312
  50.4 7.8 %copy-start.2 = (bf16[384,128]{1,0:T(8,128)(2,1)S(1)}, bf16[384,128]{1,0:T(8,128)(2,1)}, u32[]{:S(2)}) copy-start(bf16[384,128]{1,0:T(8,128)(2,1)} %grad_ref.3) | copy-start | bytes 294916
  50.4 7.8 %copy-start.3 = (s32[16]{0:T(128)S(1)}, s32[16]{0:T(128)}, u32[]{:S(2)}) copy-start(s32[16]{0:T(128)} %blocks_ref.3) | copy-start | bytes 196
  51.4 24.5 %all-to-all-start.1 = ((bf16[8,256,128]{2,1,0:T(8,128)(2,1)}), bf16[8,256,128]{2,1,0:T(8,128)(2,1)S(1)}, u32[]{:S(2)}, u32[]{:S(2)}) async-start(bf16[8,256,128]{2,1,0:T(8,128)(2,1)} %bitcast.6), calls=%async_computation.1 | async-start | bytes 1048576 | tf_op jit(solution)/shard_map/all_to_all | solution.py:319
  59.0 10.4 %collective-permute-start.3 = (bf16[896,128]{1,0:T(8,128)(2,1)S(1)}, bf16[896,128]{1,0:T(8,128)(2,1)S(1)}, u32[]{:S(2)}, u32[]{:S(2)}) collective-permute-start(bf16[896,128]{1,0:T(8,128)(2,1)S(1)} %get-tuple-element.23), channel_id=1, source_target_pairs={{0,1},{1,2},{2,3},{3,0},{4,5},{5,6},{6,7},{7,4},{8,9},{9,10},{10,1... | collective-permute-start | bytes 688136 | tf_op jit(solution)/shard_map/ppermute | solution.py:316
  61.4 10.7 %collective-permute-start.4 = (bf16[896,128]{1,0:T(8,128)(2,1)S(1)}, bf16[896,128]{1,0:T(8,128)(2,1)S(1)}, u32[]{:S(2)}, u32[]{:S(2)}) collective-permute-start(bf16[896,128]{1,0:T(8,128)(2,1)S(1)} %get-tuple-element.24), channel_id=1, source_target_pairs={{0,2},{1,3},{2,0},{3,1},{4,6},{5,7},{6,4},{7,5},{8,10},{9,11},{10,... | collective-permute-start | bytes 688136 | tf_op jit(solution)/shard_map/ppermute | solution.py:316
  65.7 10.3 %collective-permute-start.5 = (bf16[896,128]{1,0:T(8,128)(2,1)S(1)}, bf16[896,128]{1,0:T(8,128)(2,1)S(1)}, u32[]{:S(2)}, u32[]{:S(2)}) collective-permute-start(bf16[896,128]{1,0:T(8,128)(2,1)S(1)} %get-tuple-element.25), channel_id=1, source_target_pairs={{0,3},{1,0},{2,1},{3,2},{4,7},{5,4},{6,5},{7,6},{8,11},{9,8},{10,9... | collective-permute-start | bytes 688136 | tf_op jit(solution)/shard_map/ppermute | solution.py:316
  76.0 8.6 %collective-permute-start.6 = (bf16[4,512,128]{2,1,0:T(8,128)(2,1)S(1)}, bf16[4,512,128]{2,1,0:T(8,128)(2,1)S(1)}, u32[]{:S(2)}, u32[]{:S(2)}) collective-permute-start(bf16[4,512,128]{2,1,0:T(8,128)(2,1)S(1)} %stack_rows.1.own_ref), channel_id=1, source_target_pairs={{0,4},{4,0},{8,12},{12,8},{16,20},{20,16},{24,28},{28,24},{32,36},... | collective-permute-start | bytes 1572872 | tf_op jit(solution)/shard_map/ppermute | solution.py:322
  78.8 22.9 %all-to-all-start.2 = ((bf16[4,256,128]{2,1,0:T(8,128)(2,1)}), bf16[4,256,128]{2,1,0:T(8,128)(2,1)S(1)}, u32[]{:S(2)}, u32[]{:S(2)}) async-start(bf16[4,256,128]{2,1,0:T(8,128)(2,1)} %broadcast_in_dim.18), calls=%async_computation.2 | async-start | bytes 524288 | tf_op jit(solution)/shard_map/all_to_all | solution.py:329
  85.7 24.2 %collective-permute-start.7 = (bf16[4,512,128]{2,1,0:T(8,128)(2,1)}, bf16[4,512,128]{2,1,0:T(8,128)(2,1)S(1)}, u32[]{:S(2)}, u32[]{:S(2)}) collective-permute-start(bf16[4,512,128]{2,1,0:T(8,128)(2,1)} %get-tuple-element.26), channel_id=1, source_target_pairs={{0,64},{64,128},{128,192},{192,256},{256,320},{320,384},{384,448},... | collective-permute-start | bytes 1572872 | tf_op jit(solution)/shard_map/ppermute | solution.py:324
  89.7 20.3 %collective-permute-start.8 = (bf16[4,512,128]{2,1,0:T(8,128)(2,1)}, bf16[4,512,128]{2,1,0:T(8,128)(2,1)S(1)}, u32[]{:S(2)}, u32[]{:S(2)}) collective-permute-start(bf16[4,512,128]{2,1,0:T(8,128)(2,1)} %get-tuple-element.27), channel_id=1, source_target_pairs={{0,704},{64,0},{128,64},{192,128},{256,192},{320,256},{384,320},{4... | collective-permute-start | bytes 1572872 | tf_op jit(solution)/shard_map/ppermute | solution.py:324
  101.7 11.6 %collective-permute-start.10 = (bf16[256,128]{1,0:T(8,128)(2,1)S(1)}, bf16[256,128]{1,0:T(8,128)(2,1)S(1)}, u32[]{:S(2)}, u32[]{:S(2)}) collective-permute-start(bf16[256,128]{1,0:T(8,128)(2,1)S(1)} %fusion.1.own_ref), channel_id=1, source_target_pairs={{0,704},{64,0},{128,64},{192,128},{256,192},{320,256},{384,320},{4... | collective-permute-start | bytes 196616 | tf_op jit(solution)/shard_map/ppermute | solution.py:333
  103.6 9.6 %collective-permute-start.9 = (bf16[256,128]{1,0:T(8,128)(2,1)S(1)}, bf16[256,128]{1,0:T(8,128)(2,1)S(1)}, u32[]{:S(2)}, u32[]{:S(2)}) collective-permute-start(bf16[256,128]{1,0:T(8,128)(2,1)S(1)} %fusion.1.own_ref), channel_id=1, source_target_pairs={{0,64},{64,128},{128,192},{192,256},{256,320},{320,384},{384,448},... | collective-permute-start | bytes 196616 | tf_op jit(solution)/shard_map/ppermute | solution.py:333

commit v8 on v7

--- a/solution.py
+++ b/solution.py
@@ -9,6 +9,7 @@
 
 BLOCK = 128
 SPLIT = 3
+AHEAD = 3
 PIECE = 32
 SMALL = pltpu.CompilerParams(vmem_limit_bytes=12 * 1024 * 1024)
 
@@ -31,7 +32,7 @@
             hidden_ref.at[:, pl.ds(step * chunk, chunk)], chunks.at[step], sems.at[step]
         )
 
-    for step in range(steps):
+    for step in range(min(AHEAD, steps)):
         load(step).start()
     core = lax.rem(lax.axis_index("dp"), 2)
     turn = lax.rem(lax.axis_index("rep"), SPLIT)
@@ -53,6 +54,11 @@
 
     def one(step, carry):
         load(step).wait()
+
+        @pl.when(step + AHEAD < steps)
+        def _():
+            load(step + AHEAD).start()
+
         product = jnp.dot(masked_t[...], chunks[step], preferred_element_type=jnp.float32)
         for at in range(chunk // BLOCK):
             row = place[step * (chunk // BLOCK) + at]
@@ -102,19 +108,6 @@
         ),
         name="grad_products",
     )(counts, shard_blocks, hidden, grad)
-
-
-def pair_kernel(keep_ref, received_ref, *outs):
-    rows = outs[0].shape[0]
-    for k, out in enumerate(outs):
-        here = pl.ds(k * rows, rows)
-        total = keep_ref[here, :].astype(jnp.float32) + received_ref[here, :].astype(jnp.float32)
-        out[...] = total.astype(out.dtype)
-
-
-def paired_parts(keep, received):
-    out = jax.ShapeDtypeStruct((keep.shape[0] // SPLIT, keep.shape[1]), keep.dtype)
-    return pl.pallas_call(pair_kernel, out_shape=[out] * SPLIT, compiler_params=SMALL, name="pair_parts")(keep, received)
 
 
 def summed(parts):
@@ -307,7 +300,10 @@
     ).reshape(n_dp * slot_blocks * PIECE, head)
     send, keep = grad_products(token_counts, shard_blocks, hidden_in, value_grad, slot_rows)
     received = lax.ppermute(send, "dp", core_swap)
-    stay, to_next, to_last = paired_parts(keep, received)
+    third = send.shape[0] // SPLIT
+    stay, to_next, to_last = (
+        summed([half[k * third:(k + 1) * third] for half in (keep, received)]) for k in range(SPLIT)
+    )
 
     part = summed([stay, lax.ppermute(to_next, "rep", up), lax.ppermute(to_last, "rep", down)])
     held = ordered(held, part)

time: 116 us -> 116 us (level)
  other arithmetic: 1.11 us -> 3.7 us
  Pallas kernels: 15.1 us -> 13.3 us
  local copies, waits for them, and re-layouts: 3.22 us -> 1.83 us
    convert_element_type x1 -> x2, other arithmetic: 1 us -> 3.58 us  [summed(): return total.astype(parts[0].dtype)]
    pallas_call x1 -> x0, Pallas kernels: 1.76 us -> none  [paired_parts(): pl.pallas_call(pair_kernel, out_shape=[out] * SPLIT, compiler_params=SMAL...]
    unnamed x8, local copies, waits for them, and re-layouts: 1.42 us -> 0.03 us
  transfers between devices with their start and end apart: 14 -> 14, of which waited for: 7 -> 7; matrix products, arithmetic and copies ran while one was open for 3% -> 5% of each run, Pallas kernels for 6% -> 4%
where the time goes in v8:
time: 116 us; the launch traced here: 114 us
  starting transfers between devices  63 us (54%)
  waiting for transfers between devices  30.5 us (26%)
  Pallas kernels  13.3 us (11%)
  other arithmetic  3.7 us (3%)
  local copies, waits for them, and re-layouts  1.83 us (2%)
  between operations  1.55 us (1%)
    ppermute x1, starting transfers between devices, on_device(): lax.ppermute(to_last, 'rep', down)  12.4 us
    ppermute x1, waiting for transfers between devices, on_device(): lax.ppermute(to_next, 'rep', up)  10.4 us
    ppermute x3, starting transfers between devices, on_device(): lax.ppermute(sent[k], 'tp', [(i, (i + k) % n_tp) for i in range(n_tp)])  8.63 us
    ppermute x3, waiting for transfers between devices, on_device(): lax.ppermute(sent[k], 'tp', [(i, (i + k) % n_tp) for i in range(n_tp)])  8.32 us
    all_to_all x1, waiting for transfers between devices, on_device(): lax.all_to_all(jnp.broadcast_to(owned[None], (n_fellows,) + owned.shape),...  8.01 us
    ppermute x2, starting transfers between devices, on_device(): far = [lax.ppermute(first, 'rep', up), lax.ppermute(second, 'rep', down)]  7.95 us
    all_to_all x1, starting transfers between devices, on_device(): lax.all_to_all(jnp.broadcast_to(quarters, (n_y,) + quarters.shape[1:]).re...  7.31 us
    pallas_call x1, Pallas kernels, grad_products(): pl.pallas_call(functools.partial(grad_kernel, chunk, slot_blocks), in_spe...  7.28 us
  transfers between devices with their start and end apart: 14, of which 7 were waited for; matrix products, arithmetic and copies ran while one was open for 5% of the time, Pallas kernels for 4%

profile of v8, /device:TPU:6, one launch (start us, length us, event | category | flops | bytes accessed | tf_op | source)
XLA Modules:
  0.0 113.9 jit_solution(11659998062982331546)
XLA Ops:
  1.3 7.3 %grad_products.1 = (bf16[6144,128]{1,0:T(8,128)(2,1)}, bf16[6144,128]{1,0:T(8,128)(2,1)}) custom-call(s32[1]{0:T(128)S(6)} %copy.8.counts_ref, s32[16]{0:T(128)} %blocks_ref.3, bf16[384,8192]{1,0:T(8,128)(2,1)} %hidden_ref.1, bf16[384,128]{1,0:T(8,128)(2,1)} %grad_ref.3), custom_call_target="tpu_custom_call" | custom-call | flops 805306368 | bytes 9437184 | tf_op jit(solution)/shard_map/grad_products/pallas_call | solution.py:89
  8.6 2.1 %collective-permute-start = (bf16[6144,128]{1,0:T(8,128)(2,1)}, bf16[6144,128]{1,0:T(8,128)(2,1)}, u32[]{:S(2)}, u32[]{:S(2)}) collective-permute-start(bf16[6144,128]{1,0:T(8,128)(2,1)} %get-tuple-element.14), channel_id=1, source_target_pairs={{0,4},{4,0},{8,12},{12,8},{16,20},{20,16},{24,28},{28,24},{32,36},... | collective-permute-start | bytes 4718600 | tf_op jit(solution)/shard_map/ppermute | solution.py:302
  11.8 7.3 %all-to-all-start = ((bf16[16,192,128]{2,1,0:T(8,128)(2,1)}), bf16[16,192,128]{2,1,0:T(8,128)(2,1)S(1)}, u32[]{:S(2)}, u32[]{:S(2)}) async-start(bf16[16,192,128]{2,1,0:T(8,128)(2,1)} %bitcast.4), calls=%async_computation | async-start | bytes 1572864 | tf_op jit(solution)/shard_map/all_to_all | solution.py:298
  19.1 1.5 %add_convert_fusion.2 = (bf16[2048,128]{1,0:T(8,128)(2,1)S(1)}, bf16[2048,128]{1,0:T(8,128)(2,1)S(1)}) fusion(bf16[6144,128]{1,0:T(8,128)(2,1)} %collective-permute-done, bf16[6144,128]{1,0:T(8,128)(2,1)S(1)} %copy-done.3), kind=kLoop, calls=%fused_computation.2 | loop fusion | flops 2097152 | bytes 3145728 | tf_op jit(solution)/shard_map/convert_element_type | solution.py:117
  20.6 4.3 %collective-permute-start.1 = (bf16[2048,128]{1,0:T(8,128)(2,1)S(1)}, bf16[2048,128]{1,0:T(8,128)(2,1)S(1)}, u32[]{:S(2)}, u32[]{:S(2)}) collective-permute-start(bf16[2048,128]{1,0:T(8,128)(2,1)S(1)} %get-tuple-element.24), channel_id=1, source_target_pairs={{0,64},{64,128},{128,192},{192,256},{256,320},{320,384},{384,448},... | collective-permute-start | bytes 1572872 | tf_op jit(solution)/shard_map/ppermute | solution.py:308
  24.9 12.4 %collective-permute-start.2 = (bf16[2048,128]{1,0:T(8,128)(2,1)S(1)}, bf16[2048,128]{1,0:T(8,128)(2,1)S(1)}, u32[]{:S(2)}, u32[]{:S(2)}) collective-permute-start(bf16[2048,128]{1,0:T(8,128)(2,1)S(1)} %get-tuple-element.25), channel_id=1, source_target_pairs={{0,704},{64,0},{128,64},{192,128},{256,192},{320,256},{384,320},{4... | collective-permute-start | bytes 1572872 | tf_op jit(solution)/shard_map/ppermute | solution.py:308
  37.3 10.4 %collective-permute-done.1 = bf16[2048,128]{1,0:T(8,128)(2,1)S(1)} collective-permute-done((bf16[2048,128]{1,0:T(8,128)(2,1)S(1)}, bf16[2048,128]{1,0:T(8,128)(2,1)S(1)}, u32[]{:S(2)}, u32[]{:S(2)}) %collective-permute-start.1) | collective-permute-done | bytes 524320 | tf_op jit(solution)/shard_map/ppermute | solution.py:308
  49.1 2.1 %add_convert_fusion = bf16[2048,128]{1,0:T(8,128)(2,1)} fusion(bf16[2048,128]{1,0:T(8,128)(2,1)S(1)} %collective-permute-done.2, bf16[2048,128]{1,0:T(8,128)(2,1)S(1)} %collective-permute-done.1, bf16[6144,128]{1,0:T(8,128)(2,1)} %collective-permute-done, bf16[6144,128]{1,0:T(8,128)(2,1)S(1)} %copy-done.3), kind=kLoop, calls=%fused_computation | loop fusion | flops 2621440 | bytes 2621440 | tf_op jit(solution)/shard_map/convert_element_type | solution.py:117
  51.2 6.8 %all-to-all-start.1 = ((bf16[8,256,128]{2,1,0:T(8,128)(2,1)}), bf16[8,256,128]{2,1,0:T(8,128)(2,1)S(1)}, u32[]{:S(2)}, u32[]{:S(2)}) async-start(bf16[8,256,128]{2,1,0:T(8,128)(2,1)} %bitcast.6), calls=%async_computation.1 | async-start | bytes 1048576 | tf_op jit(solution)/shard_map/all_to_all | solution.py:315
  58.7 2.4 %collective-permute-start.3 = (bf16[896,128]{1,0:T(8,128)(2,1)S(1)}, bf16[896,128]{1,0:T(8,128)(2,1)S(1)}, u32[]{:S(2)}, u32[]{:S(2)}) collective-permute-start(bf16[896,128]{1,0:T(8,128)(2,1)S(1)} %get-tuple-element.17), channel_id=1, source_target_pairs={{0,1},{1,2},{2,3},{3,0},{4,5},{5,6},{6,7},{7,4},{8,9},{9,10},{10,1... | collective-permute-start | bytes 688136 | tf_op jit(solution)/shard_map/ppermute | solution.py:312
  61.1 4.3 %collective-permute-start.4 = (bf16[896,128]{1,0:T(8,128)(2,1)S(1)}, bf16[896,128]{1,0:T(8,128)(2,1)S(1)}, u32[]{:S(2)}, u32[]{:S(2)}) collective-permute-start(bf16[896,128]{1,0:T(8,128)(2,1)S(1)} %get-tuple-element.18), channel_id=1, source_target_pairs={{0,2},{1,3},{2,0},{3,1},{4,6},{5,7},{6,4},{7,5},{8,10},{9,11},{10,... | collective-permute-start | bytes 688136 | tf_op jit(solution)/shard_map/ppermute | solution.py:312
  65.5 1.9 %collective-permute-start.5 = (bf16[896,128]{1,0:T(8,128)(2,1)S(1)}, bf16[896,128]{1,0:T(8,128)(2,1)S(1)}, u32[]{:S(2)}, u32[]{:S(2)}) collective-permute-start(bf16[896,128]{1,0:T(8,128)(2,1)S(1)} %get-tuple-element.19), channel_id=1, source_target_pairs={{0,3},{1,0},{2,1},{3,2},{4,7},{5,4},{6,5},{7,6},{8,11},{9,8},{10,9... | collective-permute-start | bytes 688136 | tf_op jit(solution)/shard_map/ppermute | solution.py:312
  67.4 1.8 %collective-permute-done.3.refs_1_.refs_3_ = bf16[896,128]{1,0:T(8,128)(2,1)S(1)} collective-permute-done((bf16[896,128]{1,0:T(8,128)(2,1)S(1)}, bf16[896,128]{1,0:T(8,128)(2,1)S(1)}, u32[]{:S(2)}, u32[]{:S(2)}) %collective-permute-start.3) | collective-permute-done | bytes 229408 | tf_op jit(solution)/shard_map/ppermute | solution.py:312
  69.2 2.7 %collective-permute-done.4.refs_2_.refs_4_ = bf16[896,128]{1,0:T(8,128)(2,1)S(1)} collective-permute-done((bf16[896,128]{1,0:T(8,128)(2,1)S(1)}, bf16[896,128]{1,0:T(8,128)(2,1)S(1)}, u32[]{:S(2)}, u32[]{:S(2)}) %collective-permute-start.4) | collective-permute-done | bytes 229408 | tf_op jit(solution)/shard_map/ppermute | solution.py:312
  71.9 3.9 %collective-permute-done.5.refs_3_.refs_5_ = bf16[896,128]{1,0:T(8,128)(2,1)S(1)} collective-permute-done((bf16[896,128]{1,0:T(8,128)(2,1)S(1)}, bf16[896,128]{1,0:T(8,128)(2,1)S(1)}, u32[]{:S(2)}, u32[]{:S(2)}) %collective-permute-start.5) | collective-permute-done | bytes 229408 | tf_op jit(solution)/shard_map/ppermute | solution.py:312
  75.8 1.9 %collective-permute-start.6 = (bf16[4,512,128]{2,1,0:T(8,128)(2,1)S(1)}, bf16[4,512,128]{2,1,0:T(8,128)(2,1)S(1)}, u32[]{:S(2)}, u32[]{:S(2)}) collective-permute-start(bf16[4,512,128]{2,1,0:T(8,128)(2,1)S(1)} %stack_rows.1.own_ref), channel_id=1, source_target_pairs={{0,4},{4,0},{8,12},{12,8},{16,20},{20,16},{24,28},{28,24},{32,36},... | collective-permute-start | bytes 1572872 | tf_op jit(solution)/shard_map/ppermute | solution.py:318
  78.5 5.9 %all-to-all-start.2 = ((bf16[4,256,128]{2,1,0:T(8,128)(2,1)}), bf16[4,256,128]{2,1,0:T(8,128)(2,1)S(1)}, u32[]{:S(2)}, u32[]{:S(2)}) async-start(bf16[4,256,128]{2,1,0:T(8,128)(2,1)} %broadcast_in_dim.18), calls=%async_computation.2 | async-start | bytes 524288 | tf_op jit(solution)/shard_map/all_to_all | solution.py:325
  85.4 4.0 %collective-permute-start.7 = (bf16[4,512,128]{2,1,0:T(8,128)(2,1)}, bf16[4,512,128]{2,1,0:T(8,128)(2,1)S(1)}, u32[]{:S(2)}, u32[]{:S(2)}) collective-permute-start(bf16[4,512,128]{2,1,0:T(8,128)(2,1)} %get-tuple-element.20), channel_id=1, source_target_pairs={{0,64},{64,128},{128,192},{192,256},{256,320},{320,384},{384,448},... | collective-permute-start | bytes 1572872 | tf_op jit(solution)/shard_map/ppermute | solution.py:320
  89.4 4.0 %collective-permute-start.8 = (bf16[4,512,128]{2,1,0:T(8,128)(2,1)}, bf16[4,512,128]{2,1,0:T(8,128)(2,1)S(1)}, u32[]{:S(2)}, u32[]{:S(2)}) collective-permute-start(bf16[4,512,128]{2,1,0:T(8,128)(2,1)} %get-tuple-element.21), channel_id=1, source_target_pairs={{0,704},{64,0},{128,64},{192,128},{256,192},{320,256},{384,320},{4... | collective-permute-start | bytes 1572872 | tf_op jit(solution)/shard_map/ppermute | solution.py:320
  93.4 8.0 %all-to-all-done.2 = bf16[4,256,128]{2,1,0:T(8,128)(2,1)S(1)} async-done(((bf16[4,256,128]{2,1,0:T(8,128)(2,1)}), bf16[4,256,128]{2,1,0:T(8,128)(2,1)S(1)}, u32[]{:S(2)}, u32[]{:S(2)}) %all-to-all-start.2) | async-done | bytes 262176 | tf_op jit(solution)/shard_map/all_to_all | solution.py:325
  101.4 1.9 %collective-permute-start.10 = (bf16[256,128]{1,0:T(8,128)(2,1)S(1)}, bf16[256,128]{1,0:T(8,128)(2,1)S(1)}, u32[]{:S(2)}, u32[]{:S(2)}) collective-permute-start(bf16[256,128]{1,0:T(8,128)(2,1)S(1)} %fusion.1.own_ref), channel_id=1, source_target_pairs={{0,704},{64,0},{128,64},{192,128},{256,192},{320,256},{384,320},{4... | collective-permute-start | bytes 196616 | tf_op jit(solution)/shard_map/ppermute | solution.py:329
  103.4 3.9 %collective-permute-start.9 = (bf16[256,128]{1,0:T(8,128)(2,1)S(1)}, bf16[256,128]{1,0:T(8,128)(2,1)S(1)}, u32[]{:S(2)}, u32[]{:S(2)}) collective-permute-start(bf16[256,128]{1,0:T(8,128)(2,1)S(1)} %fusion.1.own_ref), channel_id=1, source_target_pairs={{0,64},{64,128},{128,192},{192,256},{256,320},{320,384},{384,448},... | collective-permute-start | bytes 196616 | tf_op jit(solution)/shard_map/ppermute | solution.py:329
  107.3 2.4 %collective-permute-done.7.refs_0_ = bf16[4,512,128]{2,1,0:T(8,128)(2,1)S(1)} collective-permute-done((bf16[4,512,128]{2,1,0:T(8,128)(2,1)}, bf16[4,512,128]{2,1,0:T(8,128)(2,1)S(1)}, u32[]{:S(2)}, u32[]{:S(2)}) %collective-permute-start.7) | collective-permute-done | bytes 524320 | tf_op jit(solution)/shard_map/ppermute | solution.py:320
  109.7 3.3 %input_grad.1 = (bf16[384,2048]{1,0:T(8,128)(2,1)}, f32[8,128]{1,0:T(8,128)S(1)}) custom-call(s32[1]{0:T(128)S(6)} %copy.8.counts_ref, bf16[4,512,128]{2,1,0:T(8,128)(2,1)S(1)} %stack_rows.1.own_ref, bf16[4,512,128]{2,1,0:T(8,128)(2,1)S(1)} %collective-permute-done.6.other_ref, bf16[4,512,128]{2,1,0:T(8,128)(2,1)S(1)} %collective-permute-done.7.refs_0_, ...), custom_call_target="tpu_custom_call" | custom-call | flops 805306368 | bytes 3670016 | tf_op jit(solution)/shard_map/input_grad/pallas_call | solution.py:250
  (26 shorter events, 6.0 us)
Async XLA Ops:
  0.6 10.1 %copy-start = (bf16[768,128]{1,0:T(8,128)(2,1)S(1)}, bf16[768,128]{1,0:T(8,128)(2,1)}, u32[]{:S(2)}) copy-start(bf16[768,128]{1,0:T(8,128)(2,1)} %param.7) | copy-start | bytes 589828
  8.6 10.5 %copy-start.3 = (bf16[6144,128]{1,0:T(8,128)(2,1)S(1)}, bf16[6144,128]{1,0:T(8,128)(2,1)}, u32[]{:S(2)}) copy-start(bf16[6144,128]{1,0:T(8,128)(2,1)} %get-tuple-element.13) | copy-start | bytes 4718596
  8.6 10.5 %collective-permute-start = (bf16[6144,128]{1,0:T(8,128)(2,1)}, bf16[6144,128]{1,0:T(8,128)(2,1)}, u32[]{:S(2)}, u32[]{:S(2)}) collective-permute-start(bf16[6144,128]{1,0:T(8,128)(2,1)} %get-tuple-element.14), channel_id=1, source_target_pairs={{0,4},{4,0},{8,12},{12,8},{16,20},{20,16},{24,28},{28,24},{32,36},... | collective-permute-start | bytes 4718600 | tf_op jit(solution)/shard_map/ppermute | solution.py:302
  11.8 39.4 %all-to-all-start = ((bf16[16,192,128]{2,1,0:T(8,128)(2,1)}), bf16[16,192,128]{2,1,0:T(8,128)(2,1)S(1)}, u32[]{:S(2)}, u32[]{:S(2)}) async-start(bf16[16,192,128]{2,1,0:T(8,128)(2,1)} %bitcast.4), calls=%async_computation | async-start | bytes 1572864 | tf_op jit(solution)/shard_map/all_to_all | solution.py:298
  20.6 27.1 %collective-permute-start.1 = (bf16[2048,128]{1,0:T(8,128)(2,1)S(1)}, bf16[2048,128]{1,0:T(8,128)(2,1)S(1)}, u32[]{:S(2)}, u32[]{:S(2)}) collective-permute-start(bf16[2048,128]{1,0:T(8,128)(2,1)S(1)} %get-tuple-element.24), channel_id=1, source_target_pairs={{0,64},{64,128},{128,192},{192,256},{256,320},{320,384},{384,448},... | collective-permute-start | bytes 1572872 | tf_op jit(solution)/shard_map/ppermute | solution.py:308
  24.9 33.1 %copy-start.1 = (bf16[384,128]{1,0:T(8,128)(2,1)S(1)}, bf16[384,128]{1,0:T(8,128)(2,1)}, u32[]{:S(2)}) copy-start(bf16[384,128]{1,0:T(8,128)(2,1)} %grad_ref.3) | copy-start | bytes 294916
  24.9 33.1 %copy-start.2 = (s32[16]{0:T(128)S(1)}, s32[16]{0:T(128)}, u32[]{:S(2)}) copy-start(s32[16]{0:T(128)} %blocks_ref.3) | copy-start | bytes 196
  24.9 24.1 %collective-permute-start.2 = (bf16[2048,128]{1,0:T(8,128)(2,1)S(1)}, bf16[2048,128]{1,0:T(8,128)(2,1)S(1)}, u32[]{:S(2)}, u32[]{:S(2)}) collective-permute-start(bf16[2048,128]{1,0:T(8,128)(2,1)S(1)} %get-tuple-element.25), channel_id=1, source_target_pairs={{0,704},{64,0},{128,64},{192,128},{256,192},{320,256},{384,320},{4... | collective-permute-start | bytes 1572872 | tf_op jit(solution)/shard_map/ppermute | solution.py:308
  51.2 24.6 %all-to-all-start.1 = ((bf16[8,256,128]{2,1,0:T(8,128)(2,1)}), bf16[8,256,128]{2,1,0:T(8,128)(2,1)S(1)}, u32[]{:S(2)}, u32[]{:S(2)}) async-start(bf16[8,256,128]{2,1,0:T(8,128)(2,1)} %bitcast.6), calls=%async_computation.1 | async-start | bytes 1048576 | tf_op jit(solution)/shard_map/all_to_all | solution.py:315
  58.7 10.4 %collective-permute-start.3 = (bf16[896,128]{1,0:T(8,128)(2,1)S(1)}, bf16[896,128]{1,0:T(8,128)(2,1)S(1)}, u32[]{:S(2)}, u32[]{:S(2)}) collective-permute-start(bf16[896,128]{1,0:T(8,128)(2,1)S(1)} %get-tuple-element.17), channel_id=1, source_target_pairs={{0,1},{1,2},{2,3},{3,0},{4,5},{5,6},{6,7},{7,4},{8,9},{9,10},{10,1... | collective-permute-start | bytes 688136 | tf_op jit(solution)/shard_map/ppermute | solution.py:312
  61.1 10.7 %collective-permute-start.4 = (bf16[896,128]{1,0:T(8,128)(2,1)S(1)}, bf16[896,128]{1,0:T(8,128)(2,1)S(1)}, u32[]{:S(2)}, u32[]{:S(2)}) collective-permute-start(bf16[896,128]{1,0:T(8,128)(2,1)S(1)} %get-tuple-element.18), channel_id=1, source_target_pairs={{0,2},{1,3},{2,0},{3,1},{4,6},{5,7},{6,4},{7,5},{8,10},{9,11},{10,... | collective-permute-start | bytes 688136 | tf_op jit(solution)/shard_map/ppermute | solution.py:312
  65.5 10.3 %collective-permute-start.5 = (bf16[896,128]{1,0:T(8,128)(2,1)S(1)}, bf16[896,128]{1,0:T(8,128)(2,1)S(1)}, u32[]{:S(2)}, u32[]{:S(2)}) collective-permute-start(bf16[896,128]{1,0:T(8,128)(2,1)S(1)} %get-tuple-element.19), channel_id=1, source_target_pairs={{0,3},{1,0},{2,1},{3,2},{4,7},{5,4},{6,5},{7,6},{8,11},{9,8},{10,9... | collective-permute-start | bytes 688136 | tf_op jit(solution)/shard_map/ppermute | solution.py:312
  75.8 8.6 %collective-permute-start.6 = (bf16[4,512,128]{2,1,0:T(8,128)(2,1)S(1)}, bf16[4,512,128]{2,1,0:T(8,128)(2,1)S(1)}, u32[]{:S(2)}, u32[]{:S(2)}) collective-permute-start(bf16[4,512,128]{2,1,0:T(8,128)(2,1)S(1)} %stack_rows.1.own_ref), channel_id=1, source_target_pairs={{0,4},{4,0},{8,12},{12,8},{16,20},{20,16},{24,28},{28,24},{32,36},... | collective-permute-start | bytes 1572872 | tf_op jit(solution)/shard_map/ppermute | solution.py:318
  78.5 22.9 %all-to-all-start.2 = ((bf16[4,256,128]{2,1,0:T(8,128)(2,1)}), bf16[4,256,128]{2,1,0:T(8,128)(2,1)S(1)}, u32[]{:S(2)}, u32[]{:S(2)}) async-start(bf16[4,256,128]{2,1,0:T(8,128)(2,1)} %broadcast_in_dim.18), calls=%async_computation.2 | async-start | bytes 524288 | tf_op jit(solution)/shard_map/all_to_all | solution.py:325
  85.4 24.2 %collective-permute-start.7 = (bf16[4,512,128]{2,1,0:T(8,128)(2,1)}, bf16[4,512,128]{2,1,0:T(8,128)(2,1)S(1)}, u32[]{:S(2)}, u32[]{:S(2)}) collective-permute-start(bf16[4,512,128]{2,1,0:T(8,128)(2,1)} %get-tuple-element.20), channel_id=1, source_target_pairs={{0,64},{64,128},{128,192},{192,256},{256,320},{320,384},{384,448},... | collective-permute-start | bytes 1572872 | tf_op jit(solution)/shard_map/ppermute | solution.py:320
  89.4 20.3 %collective-permute-start.8 = (bf16[4,512,128]{2,1,0:T(8,128)(2,1)}, bf16[4,512,128]{2,1,0:T(8,128)(2,1)S(1)}, u32[]{:S(2)}, u32[]{:S(2)}) collective-permute-start(bf16[4,512,128]{2,1,0:T(8,128)(2,1)} %get-tuple-element.21), channel_id=1, source_target_pairs={{0,704},{64,0},{128,64},{192,128},{256,192},{320,256},{384,320},{4... | collective-permute-start | bytes 1572872 | tf_op jit(solution)/shard_map/ppermute | solution.py:320
  101.4 11.6 %collective-permute-start.10 = (bf16[256,128]{1,0:T(8,128)(2,1)S(1)}, bf16[256,128]{1,0:T(8,128)(2,1)S(1)}, u32[]{:S(2)}, u32[]{:S(2)}) collective-permute-start(bf16[256,128]{1,0:T(8,128)(2,1)S(1)} %fusion.1.own_ref), channel_id=1, source_target_pairs={{0,704},{64,0},{128,64},{192,128},{256,192},{320,256},{384,320},{4... | collective-permute-start | bytes 196616 | tf_op jit(solution)/shard_map/ppermute | solution.py:329
  103.4 9.6 %collective-permute-start.9 = (bf16[256,128]{1,0:T(8,128)(2,1)S(1)}, bf16[256,128]{1,0:T(8,128)(2,1)S(1)}, u32[]{:S(2)}, u32[]{:S(2)}) collective-permute-start(bf16[256,128]{1,0:T(8,128)(2,1)S(1)} %fusion.1.own_ref), channel_id=1, source_target_pairs={{0,64},{64,128},{128,192},{192,256},{256,320},{320,384},{384,448},... | collective-permute-start | bytes 196616 | tf_op jit(solution)/shard_map/ppermute | solution.py:329

commit v9 on v8

--- a/solution.py
+++ b/solution.py
@@ -168,9 +168,10 @@
 
 
 def stack_kernel(heads, *refs):
-    own, out_ref = refs[:heads], refs[-1]
+    own, outs = refs[:heads], refs[-2:]
+    half = heads // 2
     for h in range(heads):
-        out_ref[h] = own[h][: out_ref.shape[1], :]
+        outs[h // half][h % half] = own[h][: outs[0].shape[1], :]
 
 
 def stacked(own, pieces, done):
@@ -179,40 +180,21 @@
     return pl.pallas_call(
         functools.partial(stack_kernel, n),
         in_specs=[vmem] * n + [pl.BlockSpec(memory_space=pl.ANY)],
-        out_specs=vmem,
-        out_shape=jax.ShapeDtypeStruct((n, pieces, head), own[0].dtype),
+        out_specs=[vmem] * 2,
+        out_shape=[jax.ShapeDtypeStruct((n // 2, pieces, head), own[0].dtype)] * 2,
         compiler_params=SMALL,
         cost_estimate=pl.CostEstimate(flops=0, bytes_accessed=4 * n * pieces * head, transcendentals=0),
         name="stack_rows",
     )(*own, done)
 
 
-def halve_kernel(own_ref, other_ref, *outs):
-    half = own_ref.shape[0] // 2
-    for k, out_ref in enumerate(outs):
-        out_ref[:half] = own_ref[k * half:(k + 1) * half]
-        out_ref[half:] = other_ref[k * half:(k + 1) * half]
-
-
-def halved(own, other):
-    vmem = pl.BlockSpec(memory_space=pltpu.VMEM)
-    return pl.pallas_call(
-        halve_kernel,
-        in_specs=[vmem] * 2,
-        out_specs=[vmem] * 2,
-        out_shape=[jax.ShapeDtypeStruct(own.shape, own.dtype)] * 2,
-        compiler_params=SMALL,
-        cost_estimate=pl.CostEstimate(flops=0, bytes_accessed=8 * own.size, transcendentals=0),
-        name="halve_heads",
-    )(own, other)
-
-
-def input_kernel(heads, counts_ref, own_ref, other_ref, *refs):
-    far, grads = refs[:2], refs[2:heads + 2]
-    out_ref, done_ref, masked, weight = refs[heads + 2:]
+def input_kernel(heads, counts_ref, *refs):
+    own, other, far, far_other = refs[:2], refs[2:4], refs[4:6], refs[6:8]
+    grads = refs[8:heads + 8]
+    out_ref, done_ref, masked, weight = refs[heads + 8:]
     turn = lax.rem(lax.axis_index("rep"), 2)
     core = lax.rem(lax.axis_index("dp"), 2)
-    blocks = own_ref.shape[1] // PIECE
+    blocks = own[0].shape[1] // PIECE
     half = heads // 2
 
     @pl.when(pl.program_id(0) == 0)
@@ -224,11 +206,12 @@
             masked[:, h * BLOCK:(h + 1) * BLOCK] = jnp.where(live, grad, 0.0).astype(masked.dtype)
 
     for h in range(heads):
+        part, at = h // half, h % half
         sources = (
-            (own_ref.at[h], turn, core),
-            (other_ref.at[h], turn, 1 - core),
-            (far[h // half].at[h % half], 1 - turn, core),
-            (far[h // half].at[half + h % half], 1 - turn, 1 - core),
+            (own[part].at[at], turn, core),
+            (other[part].at[at], turn, 1 - core),
+            (far[part].at[at], 1 - turn, core),
+            (far_other[part].at[at], 1 - turn, 1 - core),
         )
         for ref, its_turn, its_core in sources:
             first = (2 * its_turn + its_core) * PIECE
@@ -241,17 +224,18 @@
     ).astype(out_ref.dtype)
 
 
-def input_product(counts, parts, own, other, far, rows_dev):
-    n_tp, pieces, head = own.shape
+def input_product(counts, parts, own, other, far, far_other, rows_dev):
+    n_tp = len(parts)
+    _, pieces, head = own[0].shape
     steps = 4
     blocks = pieces // PIECE // steps
     chunk = blocks * BLOCK
-    piece = pl.BlockSpec((n_tp, blocks * PIECE, head), lambda i: (0, i, 0))
+    piece = pl.BlockSpec((n_tp // 2, blocks * PIECE, head), lambda i: (0, i, 0))
     return pl.pallas_call(
         functools.partial(input_kernel, n_tp),
         grid=(steps,),
         in_specs=[pl.BlockSpec(memory_space=pltpu.SMEM)]
-        + [piece] * 4
+        + [piece] * 8
         + [pl.BlockSpec((pl.Element(rows_dev), pl.Element(head)), lambda i: (pieces, 0))] * n_tp,
         out_specs=[
             pl.BlockSpec((rows_dev, chunk), lambda i: (0, i)),
@@ -272,7 +256,7 @@
             transcendentals=0,
         ),
         name="input_grad",
-    )(counts, own, other, *far, *parts)
+    )(counts, *own, *other, *far, *far_other, *parts)
 
 
 def ordered(array, other):
@@ -313,12 +297,13 @@
     ]
 
     spread = lax.all_to_all(part.reshape(n_y, slot_rows // SPLIT, head), "dp", 0, 0, axis_index_groups=along_y)
+    spread = ordered(spread, parts)
     owned = summed([spread[y] for y in range(n_y)])
     own = stacked(parts, parts[0].shape[0] - rows_dev, spread)
-    other = lax.ppermute(own, "dp", core_swap)
-    first, second = halved(own, other)
-    far = [lax.ppermute(first, "rep", up), lax.ppermute(second, "rep", down)]
-    input_grad, done = input_product(token_counts, parts, own, other, far, rows_dev)
+    other = [lax.ppermute(part, "dp", core_swap) for part in own]
+    far = [lax.ppermute(own[0], "rep", up), lax.ppermute(own[1], "rep", down)]
+    far_other = [lax.ppermute(part, "dp", core_swap) for part in far]
+    input_grad, done = input_product(token_counts, parts, own, other, far, far_other, rows_dev)
 
     n_fellows = n_rep // SPLIT
     fellows = [[k + SPLIT * q for q in range(n_fellows)] for k in range(SPLIT)]

time: 116 us -> 119 us (1.026)
  the two profiles are of different devices: /device:TPU:6 before, /device:TPU:10 now
where the time goes in v9:
time: 119 us; the launch traced here: 118 us
  starting transfers between devices  72.4 us (61%)
  waiting for transfers between devices  25.5 us (21%)
  Pallas kernels  12.4 us (10%)
  other arithmetic  4.63 us (4%)
  local copies, waits for them, and re-layouts  1.83 us (2%)
  between operations  1.6 us (1%)
    ppermute x1, starting transfers between devices, on_device(): lax.ppermute(to_last, 'rep', down)  12.3 us
    ppermute x3, starting transfers between devices, on_device(): lax.ppermute(sent[k], 'tp', [(i, (i + k) % n_tp) for i in range(n_tp)])  10.5 us
    ppermute x1, waiting for transfers between devices, on_device(): lax.ppermute(to_next, 'rep', up)  10.1 us
    ppermute x2, starting transfers between devices, on_device(): far = [lax.ppermute(own[0], 'rep', up), lax.ppermute(own[1], 'rep', down)]  8.05 us
    all_to_all x1, starting transfers between devices, on_device(): lax.all_to_all(jnp.broadcast_to(quarters, (n_y,) + quarters.shape[1:]).re...  7.67 us
    pallas_call x1, Pallas kernels, grad_products(): pl.pallas_call(functools.partial(grad_kernel, chunk, slot_blocks), in_spe...  7.33 us
    all_to_all x1, starting transfers between devices, on_device(): lax.all_to_all(part.reshape(n_y, slot_rows // SPLIT, head), 'dp', 0, 0, a...  7.21 us
    ppermute x3, waiting for transfers between devices, on_device(): lax.ppermute(sent[k], 'tp', [(i, (i + k) % n_tp) for i in range(n_tp)])  7.19 us
  transfers between devices with their start and end apart: 17, of which 6 were waited for; matrix products, arithmetic and copies ran while one was open for 5% of the time, Pallas kernels for 4%

profile of v9, /device:TPU:10, one launch (start us, length us, event | category | flops | bytes accessed | tf_op | source)
XLA Modules:
  0.0 118.3 jit_solution(481307504543085495)
XLA Ops:
  1.3 7.3 %grad_products.1 = (bf16[6144,128]{1,0:T(8,128)(2,1)}, bf16[6144,128]{1,0:T(8,128)(2,1)}) custom-call(s32[1]{0:T(128)S(6)} %copy.8.counts_ref, s32[16]{0:T(128)} %blocks_ref.3, bf16[384,8192]{1,0:T(8,128)(2,1)} %hidden_ref.1, bf16[384,128]{1,0:T(8,128)(2,1)} %grad_ref.3), custom_call_target="tpu_custom_call" | custom-call | flops 805306368 | bytes 9437184 | tf_op jit(solution)/shard_map/grad_products/pallas_call | solution.py:89
  8.7 2.1 %collective-permute-start = (bf16[6144,128]{1,0:T(8,128)(2,1)}, bf16[6144,128]{1,0:T(8,128)(2,1)}, u32[]{:S(2)}, u32[]{:S(2)}) collective-permute-start(bf16[6144,128]{1,0:T(8,128)(2,1)} %get-tuple-element.15), channel_id=1, source_target_pairs={{0,4},{4,0},{8,12},{12,8},{16,20},{20,16},{24,28},{28,24},{32,36},... | collective-permute-start | bytes 4718600 | tf_op jit(solution)/shard_map/ppermute | solution.py:286
  11.8 7.7 %all-to-all-start = ((bf16[16,192,128]{2,1,0:T(8,128)(2,1)}), bf16[16,192,128]{2,1,0:T(8,128)(2,1)S(1)}, u32[]{:S(2)}, u32[]{:S(2)}) async-start(bf16[16,192,128]{2,1,0:T(8,128)(2,1)} %bitcast.4), calls=%async_computation | async-start | bytes 1572864 | tf_op jit(solution)/shard_map/all_to_all | solution.py:282
  21.0 4.3 %collective-permute-start.1 = (bf16[2048,128]{1,0:T(8,128)(2,1)S(1)}, bf16[2048,128]{1,0:T(8,128)(2,1)S(1)}, u32[]{:S(2)}, u32[]{:S(2)}) collective-permute-start(bf16[2048,128]{1,0:T(8,128)(2,1)S(1)} %get-tuple-element.26), channel_id=1, source_target_pairs={{0,64},{64,128},{128,192},{192,256},{256,320},{320,384},{384,448},... | collective-permute-start | bytes 1572872 | tf_op jit(solution)/shard_map/ppermute | solution.py:292
  25.3 12.3 %collective-permute-start.2 = (bf16[2048,128]{1,0:T(8,128)(2,1)S(1)}, bf16[2048,128]{1,0:T(8,128)(2,1)S(1)}, u32[]{:S(2)}, u32[]{:S(2)}) collective-permute-start(bf16[2048,128]{1,0:T(8,128)(2,1)S(1)} %get-tuple-element.27), channel_id=1, source_target_pairs={{0,704},{64,0},{128,64},{192,128},{256,192},{320,256},{384,320},{4... | collective-permute-start | bytes 1572872 | tf_op jit(solution)/shard_map/ppermute | solution.py:292
  37.7 10.1 %collective-permute-done.1 = bf16[2048,128]{1,0:T(8,128)(2,1)S(1)} collective-permute-done((bf16[2048,128]{1,0:T(8,128)(2,1)S(1)}, bf16[2048,128]{1,0:T(8,128)(2,1)S(1)}, u32[]{:S(2)}, u32[]{:S(2)}) %collective-permute-start.1) | collective-permute-done | bytes 524320 | tf_op jit(solution)/shard_map/ppermute | solution.py:292
  49.1 2.1 %add_convert_fusion = bf16[2048,128]{1,0:T(8,128)(2,1)} fusion(bf16[2048,128]{1,0:T(8,128)(2,1)S(1)} %collective-permute-done.2, bf16[2048,128]{1,0:T(8,128)(2,1)S(1)} %collective-permute-done.1, bf16[6144,128]{1,0:T(8,128)(2,1)} %collective-permute-done, bf16[6144,128]{1,0:T(8,128)(2,1)S(1)} %copy-done.3), kind=kLoop, calls=%fused_computation | loop fusion | flops 2621440 | bytes 2621440 | tf_op jit(solution)/shard_map/convert_element_type | solution.py:117
  51.2 7.2 %all-to-all-start.1 = ((bf16[8,256,128]{2,1,0:T(8,128)(2,1)}), bf16[8,256,128]{2,1,0:T(8,128)(2,1)S(1)}, u32[]{:S(2)}, u32[]{:S(2)}) async-start(bf16[8,256,128]{2,1,0:T(8,128)(2,1)} %bitcast.6), calls=%async_computation.1 | async-start | bytes 1048576 | tf_op jit(solution)/shard_map/all_to_all | solution.py:299
  59.2 3.4 %collective-permute-start.3 = (bf16[896,128]{1,0:T(8,128)(2,1)S(1)}, bf16[896,128]{1,0:T(8,128)(2,1)S(1)}, u32[]{:S(2)}, u32[]{:S(2)}) collective-permute-start(bf16[896,128]{1,0:T(8,128)(2,1)S(1)} %get-tuple-element.18), channel_id=1, source_target_pairs={{0,1},{1,2},{2,3},{3,0},{4,5},{5,6},{6,7},{7,4},{8,9},{9,10},{10,1... | collective-permute-start | bytes 688136 | tf_op jit(solution)/shard_map/ppermute | solution.py:296
  62.6 3.0 %collective-permute-start.4 = (bf16[896,128]{1,0:T(8,128)(2,1)S(1)}, bf16[896,128]{1,0:T(8,128)(2,1)S(1)}, u32[]{:S(2)}, u32[]{:S(2)}) collective-permute-start(bf16[896,128]{1,0:T(8,128)(2,1)S(1)} %get-tuple-element.19), channel_id=1, source_target_pairs={{0,2},{1,3},{2,0},{3,1},{4,6},{5,7},{6,4},{7,5},{8,10},{9,11},{10,... | collective-permute-start | bytes 688136 | tf_op jit(solution)/shard_map/ppermute | solution.py:296
  65.7 4.1 %collective-permute-start.5 = (bf16[896,128]{1,0:T(8,128)(2,1)S(1)}, bf16[896,128]{1,0:T(8,128)(2,1)S(1)}, u32[]{:S(2)}, u32[]{:S(2)}) collective-permute-start(bf16[896,128]{1,0:T(8,128)(2,1)S(1)} %get-tuple-element.20), channel_id=1, source_target_pairs={{0,3},{1,0},{2,1},{3,2},{4,7},{5,4},{6,5},{7,6},{8,11},{9,8},{10,9... | collective-permute-start | bytes 688136 | tf_op jit(solution)/shard_map/ppermute | solution.py:296
  69.7 4.7 %collective-permute-done.4.refs_2_.refs_10_ = bf16[896,128]{1,0:T(8,128)(2,1)S(1)} collective-permute-done((bf16[896,128]{1,0:T(8,128)(2,1)S(1)}, bf16[896,128]{1,0:T(8,128)(2,1)S(1)}, u32[]{:S(2)}, u32[]{:S(2)}) %collective-permute-start.4) | collective-permute-done | bytes 229408 | tf_op jit(solution)/shard_map/ppermute | solution.py:296
  74.5 2.5 %collective-permute-done.5.refs_3_.refs_11_ = bf16[896,128]{1,0:T(8,128)(2,1)S(1)} collective-permute-done((bf16[896,128]{1,0:T(8,128)(2,1)S(1)}, bf16[896,128]{1,0:T(8,128)(2,1)S(1)}, u32[]{:S(2)}, u32[]{:S(2)}) %collective-permute-start.5) | collective-permute-done | bytes 229408 | tf_op jit(solution)/shard_map/ppermute | solution.py:296
  77.7 5.8 %all-to-all-start.2 = ((bf16[4,256,128]{2,1,0:T(8,128)(2,1)}), bf16[4,256,128]{2,1,0:T(8,128)(2,1)}, u32[]{:S(2)}, u32[]{:S(2)}) async-start(bf16[4,256,128]{2,1,0:T(8,128)(2,1)} %broadcast_in_dim.18), calls=%async_computation.2 | async-start | bytes 524288 | tf_op jit(solution)/shard_map/all_to_all | solution.py:310
  83.6 4.0 %collective-permute-start.8 = (bf16[2,512,128]{2,1,0:T(8,128)(2,1)S(1)}, bf16[2,512,128]{2,1,0:T(8,128)(2,1)S(1)}, u32[]{:S(2)}, u32[]{:S(2)}) collective-permute-start(bf16[2,512,128]{2,1,0:T(8,128)(2,1)S(1)} %get-tuple-element.22.refs_0_), channel_id=1, source_target_pairs={{0,64},{64,128},{128,192},{192,256},{256,320},{320,384},{384,448},... | collective-permute-start | bytes 786440 | tf_op jit(solution)/shard_map/ppermute | solution.py:304
  87.5 4.1 %collective-permute-start.9 = (bf16[2,512,128]{2,1,0:T(8,128)(2,1)S(1)}, bf16[2,512,128]{2,1,0:T(8,128)(2,1)S(1)}, u32[]{:S(2)}, u32[]{:S(2)}) collective-permute-start(bf16[2,512,128]{2,1,0:T(8,128)(2,1)S(1)} %get-tuple-element.23.refs_1_), channel_id=1, source_target_pairs={{0,704},{64,0},{128,64},{192,128},{256,192},{320,256},{384,320},{4... | collective-permute-start | bytes 786440 | tf_op jit(solution)/shard_map/ppermute | solution.py:304
  91.6 1.9 %collective-permute-start.6 = (bf16[2,512,128]{2,1,0:T(8,128)(2,1)S(1)}, bf16[2,512,128]{2,1,0:T(8,128)(2,1)S(1)}, u32[]{:S(2)}, u32[]{:S(2)}) collective-permute-start(bf16[2,512,128]{2,1,0:T(8,128)(2,1)S(1)} %get-tuple-element.22.refs_0_), channel_id=1, source_target_pairs={{0,4},{4,0},{8,12},{12,8},{16,20},{20,16},{24,28},{28,24},{32,36},... | collective-permute-start | bytes 786440 | tf_op jit(solution)/shard_map/ppermute | solution.py:303
  93.6 2.4 %collective-permute-start.7 = (bf16[2,512,128]{2,1,0:T(8,128)(2,1)S(1)}, bf16[2,512,128]{2,1,0:T(8,128)(2,1)S(1)}, u32[]{:S(2)}, u32[]{:S(2)}) collective-permute-start(bf16[2,512,128]{2,1,0:T(8,128)(2,1)S(1)} %get-tuple-element.23.refs_1_), channel_id=1, source_target_pairs={{0,4},{4,0},{8,12},{12,8},{16,20},{20,16},{24,28},{28,24},{32,36},... | collective-permute-start | bytes 786440 | tf_op jit(solution)/shard_map/ppermute | solution.py:303
  96.0 5.5 %collective-permute-done.8.refs_4_ = bf16[2,512,128]{2,1,0:T(8,128)(2,1)S(1)} collective-permute-done((bf16[2,512,128]{2,1,0:T(8,128)(2,1)S(1)}, bf16[2,512,128]{2,1,0:T(8,128)(2,1)S(1)}, u32[]{:S(2)}, u32[]{:S(2)}) %collective-permute-start.8) | collective-permute-done | bytes 262176 | tf_op jit(solution)/shard_map/ppermute | solution.py:304
  101.5 1.9 %collective-permute-start.10 = (bf16[2,512,128]{2,1,0:T(8,128)(2,1)S(1)}, bf16[2,512,128]{2,1,0:T(8,128)(2,1)S(1)}, u32[]{:S(2)}, u32[]{:S(2)}) collective-permute-start(bf16[2,512,128]{2,1,0:T(8,128)(2,1)S(1)} %collective-permute-done.8.refs_4_), channel_id=1, source_target_pairs={{0,4},{4,0},{8,12},{12,8},{16,20},{20,16},{24,28},{28,24},{32,36},... | collective-permute-start | bytes 786440 | tf_op jit(solution)/shard_map/ppermute | solution.py:305
  103.4 2.4 %collective-permute-start.11 = (bf16[2,512,128]{2,1,0:T(8,128)(2,1)S(1)}, bf16[2,512,128]{2,1,0:T(8,128)(2,1)S(1)}, u32[]{:S(2)}, u32[]{:S(2)}) collective-permute-start(bf16[2,512,128]{2,1,0:T(8,128)(2,1)S(1)} %collective-permute-done.9.refs_5_), channel_id=1, source_target_pairs={{0,4},{4,0},{8,12},{12,8},{16,20},{20,16},{24,28},{28,24},{32,36},... | collective-permute-start | bytes 786440 | tf_op jit(solution)/shard_map/ppermute | solution.py:305
  106.8 3.2 %collective-permute-start.13 = (bf16[256,128]{1,0:T(8,128)(2,1)S(1)}, bf16[256,128]{1,0:T(8,128)(2,1)S(1)}, u32[]{:S(2)}, u32[]{:S(2)}) collective-permute-start(bf16[256,128]{1,0:T(8,128)(2,1)S(1)} %fusion.1.own_ref), channel_id=1, source_target_pairs={{0,704},{64,0},{128,64},{192,128},{256,192},{320,256},{384,320},{4... | collective-permute-start | bytes 196616 | tf_op jit(solution)/shard_map/ppermute | solution.py:314
  110.1 2.6 %collective-permute-start.12 = (bf16[256,128]{1,0:T(8,128)(2,1)S(1)}, bf16[256,128]{1,0:T(8,128)(2,1)S(1)}, u32[]{:S(2)}, u32[]{:S(2)}) collective-permute-start(bf16[256,128]{1,0:T(8,128)(2,1)S(1)} %fusion.1.own_ref), channel_id=1, source_target_pairs={{0,64},{64,128},{128,192},{192,256},{256,320},{320,384},{384,448},... | collective-permute-start | bytes 196616 | tf_op jit(solution)/shard_map/ppermute | solution.py:314
  112.7 3.4 %input_grad.1 = (bf16[384,2048]{1,0:T(8,128)(2,1)}, f32[8,128]{1,0:T(8,128)S(1)}) custom-call(s32[1]{0:T(128)S(6)} %copy.8.counts_ref, bf16[2,512,128]{2,1,0:T(8,128)(2,1)S(1)} %get-tuple-element.22.refs_0_, bf16[2,512,128]{2,1,0:T(8,128)(2,1)S(1)} %get-tuple-element.23.refs_1_, bf16[2,512,128]{2,1,0:T(8,128)(2,1)S(1)} %collective-permute-done.6.refs_2_, ...), custom_call_target="tpu_custom_call" | custom-call | flops 805306368 | bytes 3670016 | tf_op jit(solution)/shard_map/input_grad/pallas_call | solution.py:234
  (31 shorter events, 8.6 us)
Async XLA Ops:
  0.6 10.1 %copy-start = (bf16[768,128]{1,0:T(8,128)(2,1)S(1)}, bf16[768,128]{1,0:T(8,128)(2,1)}, u32[]{:S(2)}) copy-start(bf16[768,128]{1,0:T(8,128)(2,1)} %param.7) | copy-start | bytes 589828
  8.7 10.9 %copy-start.3 = (bf16[6144,128]{1,0:T(8,128)(2,1)S(1)}, bf16[6144,128]{1,0:T(8,128)(2,1)}, u32[]{:S(2)}) copy-start(bf16[6144,128]{1,0:T(8,128)(2,1)} %get-tuple-element.14) | copy-start | bytes 4718596
  8.7 10.8 %collective-permute-start = (bf16[6144,128]{1,0:T(8,128)(2,1)}, bf16[6144,128]{1,0:T(8,128)(2,1)}, u32[]{:S(2)}, u32[]{:S(2)}) collective-permute-start(bf16[6144,128]{1,0:T(8,128)(2,1)} %get-tuple-element.15), channel_id=1, source_target_pairs={{0,4},{4,0},{8,12},{12,8},{16,20},{20,16},{24,28},{28,24},{32,36},... | collective-permute-start | bytes 4718600 | tf_op jit(solution)/shard_map/ppermute | solution.py:286
  11.8 39.4 %all-to-all-start = ((bf16[16,192,128]{2,1,0:T(8,128)(2,1)}), bf16[16,192,128]{2,1,0:T(8,128)(2,1)S(1)}, u32[]{:S(2)}, u32[]{:S(2)}) async-start(bf16[16,192,128]{2,1,0:T(8,128)(2,1)} %bitcast.4), calls=%async_computation | async-start | bytes 1572864 | tf_op jit(solution)/shard_map/all_to_all | solution.py:282
  21.0 26.8 %collective-permute-start.1 = (bf16[2048,128]{1,0:T(8,128)(2,1)S(1)}, bf16[2048,128]{1,0:T(8,128)(2,1)S(1)}, u32[]{:S(2)}, u32[]{:S(2)}) collective-permute-start(bf16[2048,128]{1,0:T(8,128)(2,1)S(1)} %get-tuple-element.26), channel_id=1, source_target_pairs={{0,64},{64,128},{128,192},{192,256},{256,320},{320,384},{384,448},... | collective-permute-start | bytes 1572872 | tf_op jit(solution)/shard_map/ppermute | solution.py:292
  25.3 33.1 %copy-start.1 = (bf16[384,128]{1,0:T(8,128)(2,1)S(1)}, bf16[384,128]{1,0:T(8,128)(2,1)}, u32[]{:S(2)}) copy-start(bf16[384,128]{1,0:T(8,128)(2,1)} %grad_ref.3) | copy-start | bytes 294916
  25.3 33.1 %copy-start.2 = (s32[16]{0:T(128)S(1)}, s32[16]{0:T(128)}, u32[]{:S(2)}) copy-start(s32[16]{0:T(128)} %blocks_ref.3) | copy-start | bytes 196
  25.3 23.8 %collective-permute-start.2 = (bf16[2048,128]{1,0:T(8,128)(2,1)S(1)}, bf16[2048,128]{1,0:T(8,128)(2,1)S(1)}, u32[]{:S(2)}, u32[]{:S(2)}) collective-permute-start(bf16[2048,128]{1,0:T(8,128)(2,1)S(1)} %get-tuple-element.27), channel_id=1, source_target_pairs={{0,704},{64,0},{128,64},{192,128},{256,192},{320,256},{384,320},{4... | collective-permute-start | bytes 1572872 | tf_op jit(solution)/shard_map/ppermute | solution.py:292
  51.2 25.7 %all-to-all-start.1 = ((bf16[8,256,128]{2,1,0:T(8,128)(2,1)}), bf16[8,256,128]{2,1,0:T(8,128)(2,1)S(1)}, u32[]{:S(2)}, u32[]{:S(2)}) async-start(bf16[8,256,128]{2,1,0:T(8,128)(2,1)} %bitcast.6), calls=%async_computation.1 | async-start | bytes 1048576 | tf_op jit(solution)/shard_map/all_to_all | solution.py:299
  59.2 10.5 %collective-permute-start.3 = (bf16[896,128]{1,0:T(8,128)(2,1)S(1)}, bf16[896,128]{1,0:T(8,128)(2,1)S(1)}, u32[]{:S(2)}, u32[]{:S(2)}) collective-permute-start(bf16[896,128]{1,0:T(8,128)(2,1)S(1)} %get-tuple-element.18), channel_id=1, source_target_pairs={{0,1},{1,2},{2,3},{3,0},{4,5},{5,6},{6,7},{7,4},{8,9},{9,10},{10,1... | collective-permute-start | bytes 688136 | tf_op jit(solution)/shard_map/ppermute | solution.py:296
  62.6 11.9 %collective-permute-start.4 = (bf16[896,128]{1,0:T(8,128)(2,1)S(1)}, bf16[896,128]{1,0:T(8,128)(2,1)S(1)}, u32[]{:S(2)}, u32[]{:S(2)}) collective-permute-start(bf16[896,128]{1,0:T(8,128)(2,1)S(1)} %get-tuple-element.19), channel_id=1, source_target_pairs={{0,2},{1,3},{2,0},{3,1},{4,6},{5,7},{6,4},{7,5},{8,10},{9,11},{10,... | collective-permute-start | bytes 688136 | tf_op jit(solution)/shard_map/ppermute | solution.py:296
  65.7 11.3 %collective-permute-start.5 = (bf16[896,128]{1,0:T(8,128)(2,1)S(1)}, bf16[896,128]{1,0:T(8,128)(2,1)S(1)}, u32[]{:S(2)}, u32[]{:S(2)}) collective-permute-start(bf16[896,128]{1,0:T(8,128)(2,1)S(1)} %get-tuple-element.20), channel_id=1, source_target_pairs={{0,3},{1,0},{2,1},{3,2},{4,7},{5,4},{6,5},{7,6},{8,11},{9,8},{10,9... | collective-permute-start | bytes 688136 | tf_op jit(solution)/shard_map/ppermute | solution.py:296
  77.7 28.1 %all-to-all-start.2 = ((bf16[4,256,128]{2,1,0:T(8,128)(2,1)}), bf16[4,256,128]{2,1,0:T(8,128)(2,1)}, u32[]{:S(2)}, u32[]{:S(2)}) async-start(bf16[4,256,128]{2,1,0:T(8,128)(2,1)} %broadcast_in_dim.18), calls=%async_computation.2 | async-start | bytes 524288 | tf_op jit(solution)/shard_map/all_to_all | solution.py:310
  83.6 17.9 %collective-permute-start.8 = (bf16[2,512,128]{2,1,0:T(8,128)(2,1)S(1)}, bf16[2,512,128]{2,1,0:T(8,128)(2,1)S(1)}, u32[]{:S(2)}, u32[]{:S(2)}) collective-permute-start(bf16[2,512,128]{2,1,0:T(8,128)(2,1)S(1)} %get-tuple-element.22.refs_0_), channel_id=1, source_target_pairs={{0,64},{64,128},{128,192},{192,256},{256,320},{320,384},{384,448},... | collective-permute-start | bytes 786440 | tf_op jit(solution)/shard_map/ppermute | solution.py:304
  87.5 15.9 %collective-permute-start.9 = (bf16[2,512,128]{2,1,0:T(8,128)(2,1)S(1)}, bf16[2,512,128]{2,1,0:T(8,128)(2,1)S(1)}, u32[]{:S(2)}, u32[]{:S(2)}) collective-permute-start(bf16[2,512,128]{2,1,0:T(8,128)(2,1)S(1)} %get-tuple-element.23.refs_1_), channel_id=1, source_target_pairs={{0,704},{64,0},{128,64},{192,128},{256,192},{320,256},{384,320},{4... | collective-permute-start | bytes 786440 | tf_op jit(solution)/shard_map/ppermute | solution.py:304
  91.6 18.4 %collective-permute-start.6 = (bf16[2,512,128]{2,1,0:T(8,128)(2,1)S(1)}, bf16[2,512,128]{2,1,0:T(8,128)(2,1)S(1)}, u32[]{:S(2)}, u32[]{:S(2)}) collective-permute-start(bf16[2,512,128]{2,1,0:T(8,128)(2,1)S(1)} %get-tuple-element.22.refs_0_), channel_id=1, source_target_pairs={{0,4},{4,0},{8,12},{12,8},{16,20},{20,16},{24,28},{28,24},{32,36},... | collective-permute-start | bytes 786440 | tf_op jit(solution)/shard_map/ppermute | solution.py:303
  93.6 19.2 %collective-permute-start.7 = (bf16[2,512,128]{2,1,0:T(8,128)(2,1)S(1)}, bf16[2,512,128]{2,1,0:T(8,128)(2,1)S(1)}, u32[]{:S(2)}, u32[]{:S(2)}) collective-permute-start(bf16[2,512,128]{2,1,0:T(8,128)(2,1)S(1)} %get-tuple-element.23.refs_1_), channel_id=1, source_target_pairs={{0,4},{4,0},{8,12},{12,8},{16,20},{20,16},{24,28},{28,24},{32,36},... | collective-permute-start | bytes 786440 | tf_op jit(solution)/shard_map/ppermute | solution.py:303
  101.5 11.2 %collective-permute-start.10 = (bf16[2,512,128]{2,1,0:T(8,128)(2,1)S(1)}, bf16[2,512,128]{2,1,0:T(8,128)(2,1)S(1)}, u32[]{:S(2)}, u32[]{:S(2)}) collective-permute-start(bf16[2,512,128]{2,1,0:T(8,128)(2,1)S(1)} %collective-permute-done.8.refs_4_), channel_id=1, source_target_pairs={{0,4},{4,0},{8,12},{12,8},{16,20},{20,16},{24,28},{28,24},{32,36},... | collective-permute-start | bytes 786440 | tf_op jit(solution)/shard_map/ppermute | solution.py:305
  103.4 9.3 %collective-permute-start.11 = (bf16[2,512,128]{2,1,0:T(8,128)(2,1)S(1)}, bf16[2,512,128]{2,1,0:T(8,128)(2,1)S(1)}, u32[]{:S(2)}, u32[]{:S(2)}) collective-permute-start(bf16[2,512,128]{2,1,0:T(8,128)(2,1)S(1)} %collective-permute-done.9.refs_5_), channel_id=1, source_target_pairs={{0,4},{4,0},{8,12},{12,8},{16,20},{20,16},{24,28},{28,24},{32,36},... | collective-permute-start | bytes 786440 | tf_op jit(solution)/shard_map/ppermute | solution.py:305
  106.8 9.3 %collective-permute-start.13 = (bf16[256,128]{1,0:T(8,128)(2,1)S(1)}, bf16[256,128]{1,0:T(8,128)(2,1)S(1)}, u32[]{:S(2)}, u32[]{:S(2)}) collective-permute-start(bf16[256,128]{1,0:T(8,128)(2,1)S(1)} %fusion.1.own_ref), channel_id=1, source_target_pairs={{0,704},{64,0},{128,64},{192,128},{256,192},{320,256},{384,320},{4... | collective-permute-start | bytes 196616 | tf_op jit(solution)/shard_map/ppermute | solution.py:314
  110.1 7.4 %collective-permute-start.12 = (bf16[256,128]{1,0:T(8,128)(2,1)S(1)}, bf16[256,128]{1,0:T(8,128)(2,1)S(1)}, u32[]{:S(2)}, u32[]{:S(2)}) collective-permute-start(bf16[256,128]{1,0:T(8,128)(2,1)S(1)} %fusion.1.own_ref), channel_id=1, source_target_pairs={{0,64},{64,128},{128,192},{192,256},{256,320},{320,384},{384,448},... | collective-permute-start | bytes 196616 | tf_op jit(solution)/shard_map/ppermute | solution.py:314

commit v10 on v8

--- a/solution.py
+++ b/solution.py
@@ -117,7 +117,7 @@
     return total.astype(parts[0].dtype)
 
 
-def finish_kernel(own_ref, before_ref, after_ref, done_ref, out_ref):
+def finish_kernel(own_ref, before_ref, after_ref, out_ref):
     turn = lax.rem(lax.axis_index("rep"), SPLIT)
     rows = own_ref.shape[0]
     for shift, ref in ((0, own_ref), (SPLIT - 1, before_ref), (1, after_ref)):
@@ -127,14 +127,13 @@
             out_ref[pl.ds(pl.multiple_of(first + at * BLOCK, BLOCK), BLOCK), :] = tile.T
 
 
-def finished(own, before, after, done):
+def finished(own, before, after):
     return pl.pallas_call(
         finish_kernel,
-        in_specs=[pl.BlockSpec(memory_space=pltpu.VMEM)] * 3 + [pl.BlockSpec(memory_space=pl.ANY)],
         out_shape=jax.ShapeDtypeStruct((SPLIT * own.shape[0], own.shape[1]), jnp.float32),
         compiler_params=SMALL,
         name="finish_weight_grad",
-    )(own, before, after, done)
+    )(own, before, after)
 
 
 def compact_kernel(slot_blocks, n_tp, blocks_ref, held_ref, grad_ref, *rest):
@@ -209,7 +208,7 @@
 
 def input_kernel(heads, counts_ref, own_ref, other_ref, *refs):
     far, grads = refs[:2], refs[2:heads + 2]
-    out_ref, done_ref, masked, weight = refs[heads + 2:]
+    out_ref, masked, weight = refs[heads + 2:]
     turn = lax.rem(lax.axis_index("rep"), 2)
     core = lax.rem(lax.axis_index("dp"), 2)
     blocks = own_ref.shape[1] // PIECE
@@ -217,7 +216,6 @@
 
     @pl.when(pl.program_id(0) == 0)
     def _():
-        done_ref[...] = jnp.zeros_like(done_ref)
         for h in range(heads):
             grad = grads[h][...].astype(jnp.float32)
             live = lax.broadcasted_iota(jnp.int32, grad.shape, 0) < counts_ref[0]
@@ -253,14 +251,8 @@
         in_specs=[pl.BlockSpec(memory_space=pltpu.SMEM)]
         + [piece] * 4
         + [pl.BlockSpec((pl.Element(rows_dev), pl.Element(head)), lambda i: (pieces, 0))] * n_tp,
-        out_specs=[
-            pl.BlockSpec((rows_dev, chunk), lambda i: (0, i)),
-            pl.BlockSpec((8, 128), lambda i: (0, 0)),
-        ],
-        out_shape=[
-            jax.ShapeDtypeStruct((rows_dev, steps * chunk), jnp.bfloat16),
-            jax.ShapeDtypeStruct((8, 128), jnp.float32),
-        ],
+        out_specs=pl.BlockSpec((rows_dev, chunk), lambda i: (0, i)),
+        out_shape=jax.ShapeDtypeStruct((rows_dev, steps * chunk), jnp.bfloat16),
         scratch_shapes=[
             pltpu.VMEM((rows_dev, head * n_tp), jnp.bfloat16),
             pltpu.VMEM((chunk, head * n_tp), jnp.bfloat16),
@@ -318,7 +310,7 @@
     other = lax.ppermute(own, "dp", core_swap)
     first, second = halved(own, other)
     far = [lax.ppermute(first, "rep", up), lax.ppermute(second, "rep", down)]
-    input_grad, done = input_product(token_counts, parts, own, other, far, rows_dev)
+    input_grad = input_product(token_counts, parts, own, other, far, rows_dev)
 
     n_fellows = n_rep // SPLIT
     fellows = [[k + SPLIT * q for q in range(n_fellows)] for k in range(SPLIT)]
@@ -326,7 +318,7 @@
         jnp.broadcast_to(owned[None], (n_fellows,) + owned.shape), "rep", 0, 0, axis_index_groups=fellows
     )
     third = summed([shares[q] for q in range(n_fellows)])
-    weight_grad = finished(third, lax.ppermute(third, "rep", up), lax.ppermute(third, "rep", down), done)
+    weight_grad = finished(third, lax.ppermute(third, "rep", up), lax.ppermute(third, "rep", down))
     return (input_grad, weight_grad)
 
 

time: 116 us -> 117 us (level)
    ppermute x1, waiting for transfers between devices: 0.01 us -> 2.52 us  [on_device(): lax.ppermute(third, 'rep', up)]
    ppermute x2, waiting for transfers between devices: 2.37 us -> 0.01 us  [on_device(): far = [lax.ppermute(first, 'rep', up), lax.ppermute(second, 'rep', down)]]
  transfers between devices with their start and end apart: 14 -> 14, of which waited for: 7 -> 8; matrix products, arithmetic and copies ran while one was open for 5% -> 5% of each run, Pallas kernels for 4% -> 2%
where the time goes in v10:
time: 117 us; the launch traced here: 115 us
  starting transfers between devices  63.1 us (54%)
  waiting for transfers between devices  31.5 us (27%)
  Pallas kernels  13.3 us (11%)
  other arithmetic  3.7 us (3%)
  local copies, waits for them, and re-layouts  1.82 us (2%)
  between operations  1.55 us (1%)
    ppermute x1, starting transfers between devices, on_device(): lax.ppermute(to_last, 'rep', down)  12.4 us
    ppermute x1, waiting for transfers between devices, on_device(): lax.ppermute(to_next, 'rep', up)  10.4 us
    ppermute x3, starting transfers between devices, on_device(): lax.ppermute(sent[k], 'tp', [(i, (i + k) % n_tp) for i in range(n_tp)])  8.63 us
    ppermute x3, waiting for transfers between devices, on_device(): lax.ppermute(sent[k], 'tp', [(i, (i + k) % n_tp) for i in range(n_tp)])  8.32 us
    all_to_all x1, waiting for transfers between devices, on_device(): lax.all_to_all(jnp.broadcast_to(owned[None], (n_fellows,) + owned.shape),...  8.01 us
    ppermute x2, starting transfers between devices, on_device(): far = [lax.ppermute(first, 'rep', up), lax.ppermute(second, 'rep', down)]  7.95 us
    all_to_all x1, starting transfers between devices, on_device(): lax.all_to_all(jnp.broadcast_to(quarters, (n_y,) + quarters.shape[1:]).re...  7.33 us
    pallas_call x1, Pallas kernels, grad_products(): pl.pallas_call(functools.partial(grad_kernel, chunk, slot_blocks), in_spe...  7.28 us
  transfers between devices with their start and end apart: 14, of which 8 were waited for; matrix products, arithmetic and copies ran while one was open for 5% of the time, Pallas kernels for 2%

profile of v10, /device:TPU:6, one launch (start us, length us, event | category | flops | bytes accessed | tf_op | source)
XLA Modules:
  0.0 115.0 jit_solution(14727897701369318248)
XLA Ops:
  1.3 7.3 %grad_products.1 = (bf16[6144,128]{1,0:T(8,128)(2,1)}, bf16[6144,128]{1,0:T(8,128)(2,1)}) custom-call(s32[1]{0:T(128)S(6)} %copy.8.counts_ref, s32[16]{0:T(128)} %blocks_ref.3, bf16[384,8192]{1,0:T(8,128)(2,1)} %hidden_ref.1, bf16[384,128]{1,0:T(8,128)(2,1)} %grad_ref.3), custom_call_target="tpu_custom_call" | custom-call | flops 805306368 | bytes 9437184 | tf_op jit(solution)/shard_map/grad_products/pallas_call | solution.py:89
  8.6 2.1 %collective-permute-start = (bf16[6144,128]{1,0:T(8,128)(2,1)}, bf16[6144,128]{1,0:T(8,128)(2,1)}, u32[]{:S(2)}, u32[]{:S(2)}) collective-permute-start(bf16[6144,128]{1,0:T(8,128)(2,1)} %get-tuple-element.12), channel_id=1, source_target_pairs={{0,4},{4,0},{8,12},{12,8},{16,20},{20,16},{24,28},{28,24},{32,36},... | collective-permute-start | bytes 4718600 | tf_op jit(solution)/shard_map/ppermute | solution.py:294
  11.8 7.3 %all-to-all-start = ((bf16[16,192,128]{2,1,0:T(8,128)(2,1)}), bf16[16,192,128]{2,1,0:T(8,128)(2,1)S(1)}, u32[]{:S(2)}, u32[]{:S(2)}) async-start(bf16[16,192,128]{2,1,0:T(8,128)(2,1)} %bitcast.4), calls=%async_computation | async-start | bytes 1572864 | tf_op jit(solution)/shard_map/all_to_all | solution.py:290
  19.2 1.5 %add_convert_fusion.2 = (bf16[2048,128]{1,0:T(8,128)(2,1)S(1)}, bf16[2048,128]{1,0:T(8,128)(2,1)S(1)}) fusion(bf16[6144,128]{1,0:T(8,128)(2,1)} %collective-permute-done, bf16[6144,128]{1,0:T(8,128)(2,1)S(1)} %copy-done.3), kind=kLoop, calls=%fused_computation.2 | loop fusion | flops 2097152 | bytes 3145728 | tf_op jit(solution)/shard_map/convert_element_type | solution.py:117
  20.6 4.3 %collective-permute-start.1 = (bf16[2048,128]{1,0:T(8,128)(2,1)S(1)}, bf16[2048,128]{1,0:T(8,128)(2,1)S(1)}, u32[]{:S(2)}, u32[]{:S(2)}) collective-permute-start(bf16[2048,128]{1,0:T(8,128)(2,1)S(1)} %get-tuple-element.20), channel_id=1, source_target_pairs={{0,64},{64,128},{128,192},{192,256},{256,320},{320,384},{384,448},... | collective-permute-start | bytes 1572872 | tf_op jit(solution)/shard_map/ppermute | solution.py:300
  25.0 12.4 %collective-permute-start.2 = (bf16[2048,128]{1,0:T(8,128)(2,1)S(1)}, bf16[2048,128]{1,0:T(8,128)(2,1)S(1)}, u32[]{:S(2)}, u32[]{:S(2)}) collective-permute-start(bf16[2048,128]{1,0:T(8,128)(2,1)S(1)} %get-tuple-element.21), channel_id=1, source_target_pairs={{0,704},{64,0},{128,64},{192,128},{256,192},{320,256},{384,320},{4... | collective-permute-start | bytes 1572872 | tf_op jit(solution)/shard_map/ppermute | solution.py:300
  37.3 10.4 %collective-permute-done.1 = bf16[2048,128]{1,0:T(8,128)(2,1)S(1)} collective-permute-done((bf16[2048,128]{1,0:T(8,128)(2,1)S(1)}, bf16[2048,128]{1,0:T(8,128)(2,1)S(1)}, u32[]{:S(2)}, u32[]{:S(2)}) %collective-permute-start.1) | collective-permute-done | bytes 524320 | tf_op jit(solution)/shard_map/ppermute | solution.py:300
  49.1 2.1 %add_convert_fusion = bf16[2048,128]{1,0:T(8,128)(2,1)} fusion(bf16[2048,128]{1,0:T(8,128)(2,1)S(1)} %collective-permute-done.2, bf16[2048,128]{1,0:T(8,128)(2,1)S(1)} %collective-permute-done.1, bf16[6144,128]{1,0:T(8,128)(2,1)} %collective-permute-done, bf16[6144,128]{1,0:T(8,128)(2,1)S(1)} %copy-done.3), kind=kLoop, calls=%fused_computation | loop fusion | flops 2621440 | bytes 2621440 | tf_op jit(solution)/shard_map/convert_element_type | solution.py:117
  51.2 6.8 %all-to-all-start.1 = ((bf16[8,256,128]{2,1,0:T(8,128)(2,1)}), bf16[8,256,128]{2,1,0:T(8,128)(2,1)S(1)}, u32[]{:S(2)}, u32[]{:S(2)}) async-start(bf16[8,256,128]{2,1,0:T(8,128)(2,1)} %bitcast.6), calls=%async_computation.1 | async-start | bytes 1048576 | tf_op jit(solution)/shard_map/all_to_all | solution.py:307
  58.8 2.4 %collective-permute-start.3 = (bf16[896,128]{1,0:T(8,128)(2,1)S(1)}, bf16[896,128]{1,0:T(8,128)(2,1)S(1)}, u32[]{:S(2)}, u32[]{:S(2)}) collective-permute-start(bf16[896,128]{1,0:T(8,128)(2,1)S(1)} %get-tuple-element.15), channel_id=1, source_target_pairs={{0,1},{1,2},{2,3},{3,0},{4,5},{5,6},{6,7},{7,4},{8,9},{9,10},{10,1... | collective-permute-start | bytes 688136 | tf_op jit(solution)/shard_map/ppermute | solution.py:304
  61.2 4.3 %collective-permute-start.4 = (bf16[896,128]{1,0:T(8,128)(2,1)S(1)}, bf16[896,128]{1,0:T(8,128)(2,1)S(1)}, u32[]{:S(2)}, u32[]{:S(2)}) collective-permute-start(bf16[896,128]{1,0:T(8,128)(2,1)S(1)} %get-tuple-element.16), channel_id=1, source_target_pairs={{0,2},{1,3},{2,0},{3,1},{4,6},{5,7},{6,4},{7,5},{8,10},{9,11},{10,... | collective-permute-start | bytes 688136 | tf_op jit(solution)/shard_map/ppermute | solution.py:304
  65.5 1.9 %collective-permute-start.5 = (bf16[896,128]{1,0:T(8,128)(2,1)S(1)}, bf16[896,128]{1,0:T(8,128)(2,1)S(1)}, u32[]{:S(2)}, u32[]{:S(2)}) collective-permute-start(bf16[896,128]{1,0:T(8,128)(2,1)S(1)} %get-tuple-element.17), channel_id=1, source_target_pairs={{0,3},{1,0},{2,1},{3,2},{4,7},{5,4},{6,5},{7,6},{8,11},{9,8},{10,9... | collective-permute-start | bytes 688136 | tf_op jit(solution)/shard_map/ppermute | solution.py:304
  67.4 1.8 %collective-permute-done.3.refs_1_.refs_3_ = bf16[896,128]{1,0:T(8,128)(2,1)S(1)} collective-permute-done((bf16[896,128]{1,0:T(8,128)(2,1)S(1)}, bf16[896,128]{1,0:T(8,128)(2,1)S(1)}, u32[]{:S(2)}, u32[]{:S(2)}) %collective-permute-start.3) | collective-permute-done | bytes 229408 | tf_op jit(solution)/shard_map/ppermute | solution.py:304
  69.2 2.7 %collective-permute-done.4.refs_2_.refs_4_ = bf16[896,128]{1,0:T(8,128)(2,1)S(1)} collective-permute-done((bf16[896,128]{1,0:T(8,128)(2,1)S(1)}, bf16[896,128]{1,0:T(8,128)(2,1)S(1)}, u32[]{:S(2)}, u32[]{:S(2)}) %collective-permute-start.4) | collective-permute-done | bytes 229408 | tf_op jit(solution)/shard_map/ppermute | solution.py:304
  71.9 3.9 %collective-permute-done.5.refs_3_.refs_5_ = bf16[896,128]{1,0:T(8,128)(2,1)S(1)} collective-permute-done((bf16[896,128]{1,0:T(8,128)(2,1)S(1)}, bf16[896,128]{1,0:T(8,128)(2,1)S(1)}, u32[]{:S(2)}, u32[]{:S(2)}) %collective-permute-start.5) | collective-permute-done | bytes 229408 | tf_op jit(solution)/shard_map/ppermute | solution.py:304
  75.8 1.9 %collective-permute-start.6 = (bf16[4,512,128]{2,1,0:T(8,128)(2,1)S(1)}, bf16[4,512,128]{2,1,0:T(8,128)(2,1)S(1)}, u32[]{:S(2)}, u32[]{:S(2)}) collective-permute-start(bf16[4,512,128]{2,1,0:T(8,128)(2,1)S(1)} %stack_rows.1.own_ref), channel_id=1, source_target_pairs={{0,4},{4,0},{8,12},{12,8},{16,20},{20,16},{24,28},{28,24},{32,36},... | collective-permute-start | bytes 1572872 | tf_op jit(solution)/shard_map/ppermute | solution.py:310
  78.5 5.9 %all-to-all-start.2 = ((bf16[4,256,128]{2,1,0:T(8,128)(2,1)}), bf16[4,256,128]{2,1,0:T(8,128)(2,1)S(1)}, u32[]{:S(2)}, u32[]{:S(2)}) async-start(bf16[4,256,128]{2,1,0:T(8,128)(2,1)} %broadcast_in_dim.18), calls=%async_computation.2 | async-start | bytes 524288 | tf_op jit(solution)/shard_map/all_to_all | solution.py:317
  85.4 4.0 %collective-permute-start.7 = (bf16[4,512,128]{2,1,0:T(8,128)(2,1)}, bf16[4,512,128]{2,1,0:T(8,128)(2,1)S(1)}, u32[]{:S(2)}, u32[]{:S(2)}) collective-permute-start(bf16[4,512,128]{2,1,0:T(8,128)(2,1)} %get-tuple-element.18), channel_id=1, source_target_pairs={{0,64},{64,128},{128,192},{192,256},{256,320},{320,384},{384,448},... | collective-permute-start | bytes 1572872 | tf_op jit(solution)/shard_map/ppermute | solution.py:312
  89.4 4.0 %collective-permute-start.8 = (bf16[4,512,128]{2,1,0:T(8,128)(2,1)}, bf16[4,512,128]{2,1,0:T(8,128)(2,1)S(1)}, u32[]{:S(2)}, u32[]{:S(2)}) collective-permute-start(bf16[4,512,128]{2,1,0:T(8,128)(2,1)} %get-tuple-element.19), channel_id=1, source_target_pairs={{0,704},{64,0},{128,64},{192,128},{256,192},{320,256},{384,320},{4... | collective-permute-start | bytes 1572872 | tf_op jit(solution)/shard_map/ppermute | solution.py:312
  93.4 8.0 %all-to-all-done.2 = bf16[4,256,128]{2,1,0:T(8,128)(2,1)S(1)} async-done(((bf16[4,256,128]{2,1,0:T(8,128)(2,1)}), bf16[4,256,128]{2,1,0:T(8,128)(2,1)S(1)}, u32[]{:S(2)}, u32[]{:S(2)}) %all-to-all-start.2) | async-done | bytes 262176 | tf_op jit(solution)/shard_map/all_to_all | solution.py:317
  101.5 1.9 %collective-permute-start.10 = (bf16[256,128]{1,0:T(8,128)(2,1)S(1)}, bf16[256,128]{1,0:T(8,128)(2,1)S(1)}, u32[]{:S(2)}, u32[]{:S(2)}) collective-permute-start(bf16[256,128]{1,0:T(8,128)(2,1)S(1)} %fusion.1.own_ref), channel_id=1, source_target_pairs={{0,704},{64,0},{128,64},{192,128},{256,192},{320,256},{384,320},{4... | collective-permute-start | bytes 196616 | tf_op jit(solution)/shard_map/ppermute | solution.py:321
  103.4 3.9 %collective-permute-start.9 = (bf16[256,128]{1,0:T(8,128)(2,1)S(1)}, bf16[256,128]{1,0:T(8,128)(2,1)S(1)}, u32[]{:S(2)}, u32[]{:S(2)}) collective-permute-start(bf16[256,128]{1,0:T(8,128)(2,1)S(1)} %fusion.1.own_ref), channel_id=1, source_target_pairs={{0,64},{64,128},{128,192},{192,256},{256,320},{320,384},{384,448},... | collective-permute-start | bytes 196616 | tf_op jit(solution)/shard_map/ppermute | solution.py:321
  108.2 2.5 %collective-permute-done.9.before_ref = bf16[256,128]{1,0:T(8,128)(2,1)S(1)} collective-permute-done((bf16[256,128]{1,0:T(8,128)(2,1)S(1)}, bf16[256,128]{1,0:T(8,128)(2,1)S(1)}, u32[]{:S(2)}, u32[]{:S(2)}) %collective-permute-start.9) | collective-permute-done | bytes 65568 | tf_op jit(solution)/shard_map/ppermute | solution.py:321
  111.7 3.3 %input_grad.1 = bf16[384,2048]{1,0:T(8,128)(2,1)} custom-call(s32[1]{0:T(128)S(6)} %copy.8.counts_ref, bf16[4,512,128]{2,1,0:T(8,128)(2,1)S(1)} %stack_rows.1.own_ref, bf16[4,512,128]{2,1,0:T(8,128)(2,1)S(1)} %collective-permute-done.6.other_ref, bf16[4,512,128]{2,1,0:T(8,128)(2,1)S(1)} %collective-permute-done.7.refs_0_, ...), custom_call_target="tpu_custom_call" | custom-call | flops 805306368 | bytes 3670016 | tf_op jit(solution)/shard_map/input_grad/pallas_call | solution.py:248
  (26 shorter events, 6.9 us)
Async XLA Ops:
  0.6 10.1 %copy-start = (bf16[768,128]{1,0:T(8,128)(2,1)S(1)}, bf16[768,128]{1,0:T(8,128)(2,1)}, u32[]{:S(2)}) copy-start(bf16[768,128]{1,0:T(8,128)(2,1)} %param.7) | copy-start | bytes 589828
  8.6 10.5 %copy-start.3 = (bf16[6144,128]{1,0:T(8,128)(2,1)S(1)}, bf16[6144,128]{1,0:T(8,128)(2,1)}, u32[]{:S(2)}) copy-start(bf16[6144,128]{1,0:T(8,128)(2,1)} %get-tuple-element.11) | copy-start | bytes 4718596
  8.6 10.5 %collective-permute-start = (bf16[6144,128]{1,0:T(8,128)(2,1)}, bf16[6144,128]{1,0:T(8,128)(2,1)}, u32[]{:S(2)}, u32[]{:S(2)}) collective-permute-start(bf16[6144,128]{1,0:T(8,128)(2,1)} %get-tuple-element.12), channel_id=1, source_target_pairs={{0,4},{4,0},{8,12},{12,8},{16,20},{20,16},{24,28},{28,24},{32,36},... | collective-permute-start | bytes 4718600 | tf_op jit(solution)/shard_map/ppermute | solution.py:294
  11.8 39.4 %all-to-all-start = ((bf16[16,192,128]{2,1,0:T(8,128)(2,1)}), bf16[16,192,128]{2,1,0:T(8,128)(2,1)S(1)}, u32[]{:S(2)}, u32[]{:S(2)}) async-start(bf16[16,192,128]{2,1,0:T(8,128)(2,1)} %bitcast.4), calls=%async_computation | async-start | bytes 1572864 | tf_op jit(solution)/shard_map/all_to_all | solution.py:290
  20.6 27.1 %collective-permute-start.1 = (bf16[2048,128]{1,0:T(8,128)(2,1)S(1)}, bf16[2048,128]{1,0:T(8,128)(2,1)S(1)}, u32[]{:S(2)}, u32[]{:S(2)}) collective-permute-start(bf16[2048,128]{1,0:T(8,128)(2,1)S(1)} %get-tuple-element.20), channel_id=1, source_target_pairs={{0,64},{64,128},{128,192},{192,256},{256,320},{320,384},{384,448},... | collective-permute-start | bytes 1572872 | tf_op jit(solution)/shard_map/ppermute | solution.py:300
  24.9 33.1 %copy-start.1 = (bf16[384,128]{1,0:T(8,128)(2,1)S(1)}, bf16[384,128]{1,0:T(8,128)(2,1)}, u32[]{:S(2)}) copy-start(bf16[384,128]{1,0:T(8,128)(2,1)} %grad_ref.3) | copy-start | bytes 294916
  24.9 33.1 %copy-start.2 = (s32[16]{0:T(128)S(1)}, s32[16]{0:T(128)}, u32[]{:S(2)}) copy-start(s32[16]{0:T(128)} %blocks_ref.3) | copy-start | bytes 196
  25.0 24.1 %collective-permute-start.2 = (bf16[2048,128]{1,0:T(8,128)(2,1)S(1)}, bf16[2048,128]{1,0:T(8,128)(2,1)S(1)}, u32[]{:S(2)}, u32[]{:S(2)}) collective-permute-start(bf16[2048,128]{1,0:T(8,128)(2,1)S(1)} %get-tuple-element.21), channel_id=1, source_target_pairs={{0,704},{64,0},{128,64},{192,128},{256,192},{320,256},{384,320},{4... | collective-permute-start | bytes 1572872 | tf_op jit(solution)/shard_map/ppermute | solution.py:300
  51.2 24.6 %all-to-all-start.1 = ((bf16[8,256,128]{2,1,0:T(8,128)(2,1)}), bf16[8,256,128]{2,1,0:T(8,128)(2,1)S(1)}, u32[]{:S(2)}, u32[]{:S(2)}) async-start(bf16[8,256,128]{2,1,0:T(8,128)(2,1)} %bitcast.6), calls=%async_computation.1 | async-start | bytes 1048576 | tf_op jit(solution)/shard_map/all_to_all | solution.py:307
  58.8 10.4 %collective-permute-start.3 = (bf16[896,128]{1,0:T(8,128)(2,1)S(1)}, bf16[896,128]{1,0:T(8,128)(2,1)S(1)}, u32[]{:S(2)}, u32[]{:S(2)}) collective-permute-start(bf16[896,128]{1,0:T(8,128)(2,1)S(1)} %get-tuple-element.15), channel_id=1, source_target_pairs={{0,1},{1,2},{2,3},{3,0},{4,5},{5,6},{6,7},{7,4},{8,9},{9,10},{10,1... | collective-permute-start | bytes 688136 | tf_op jit(solution)/shard_map/ppermute | solution.py:304
  61.2 10.7 %collective-permute-start.4 = (bf16[896,128]{1,0:T(8,128)(2,1)S(1)}, bf16[896,128]{1,0:T(8,128)(2,1)S(1)}, u32[]{:S(2)}, u32[]{:S(2)}) collective-permute-start(bf16[896,128]{1,0:T(8,128)(2,1)S(1)} %get-tuple-element.16), channel_id=1, source_target_pairs={{0,2},{1,3},{2,0},{3,1},{4,6},{5,7},{6,4},{7,5},{8,10},{9,11},{10,... | collective-permute-start | bytes 688136 | tf_op jit(solution)/shard_map/ppermute | solution.py:304
  65.5 10.3 %collective-permute-start.5 = (bf16[896,128]{1,0:T(8,128)(2,1)S(1)}, bf16[896,128]{1,0:T(8,128)(2,1)S(1)}, u32[]{:S(2)}, u32[]{:S(2)}) collective-permute-start(bf16[896,128]{1,0:T(8,128)(2,1)S(1)} %get-tuple-element.17), channel_id=1, source_target_pairs={{0,3},{1,0},{2,1},{3,2},{4,7},{5,4},{6,5},{7,6},{8,11},{9,8},{10,9... | collective-permute-start | bytes 688136 | tf_op jit(solution)/shard_map/ppermute | solution.py:304
  75.8 8.6 %collective-permute-start.6 = (bf16[4,512,128]{2,1,0:T(8,128)(2,1)S(1)}, bf16[4,512,128]{2,1,0:T(8,128)(2,1)S(1)}, u32[]{:S(2)}, u32[]{:S(2)}) collective-permute-start(bf16[4,512,128]{2,1,0:T(8,128)(2,1)S(1)} %stack_rows.1.own_ref), channel_id=1, source_target_pairs={{0,4},{4,0},{8,12},{12,8},{16,20},{20,16},{24,28},{28,24},{32,36},... | collective-permute-start | bytes 1572872 | tf_op jit(solution)/shard_map/ppermute | solution.py:310
  78.5 22.9 %all-to-all-start.2 = ((bf16[4,256,128]{2,1,0:T(8,128)(2,1)}), bf16[4,256,128]{2,1,0:T(8,128)(2,1)S(1)}, u32[]{:S(2)}, u32[]{:S(2)}) async-start(bf16[4,256,128]{2,1,0:T(8,128)(2,1)} %broadcast_in_dim.18), calls=%async_computation.2 | async-start | bytes 524288 | tf_op jit(solution)/shard_map/all_to_all | solution.py:317
  85.4 26.2 %collective-permute-start.7 = (bf16[4,512,128]{2,1,0:T(8,128)(2,1)}, bf16[4,512,128]{2,1,0:T(8,128)(2,1)S(1)}, u32[]{:S(2)}, u32[]{:S(2)}) collective-permute-start(bf16[4,512,128]{2,1,0:T(8,128)(2,1)} %get-tuple-element.18), channel_id=1, source_target_pairs={{0,64},{64,128},{128,192},{192,256},{256,320},{320,384},{384,448},... | collective-permute-start | bytes 1572872 | tf_op jit(solution)/shard_map/ppermute | solution.py:312
  89.4 22.2 %collective-permute-start.8 = (bf16[4,512,128]{2,1,0:T(8,128)(2,1)}, bf16[4,512,128]{2,1,0:T(8,128)(2,1)S(1)}, u32[]{:S(2)}, u32[]{:S(2)}) collective-permute-start(bf16[4,512,128]{2,1,0:T(8,128)(2,1)} %get-tuple-element.19), channel_id=1, source_target_pairs={{0,704},{64,0},{128,64},{192,128},{256,192},{320,256},{384,320},{4... | collective-permute-start | bytes 1572872 | tf_op jit(solution)/shard_map/ppermute | solution.py:312
  101.5 6.8 %collective-permute-start.10 = (bf16[256,128]{1,0:T(8,128)(2,1)S(1)}, bf16[256,128]{1,0:T(8,128)(2,1)S(1)}, u32[]{:S(2)}, u32[]{:S(2)}) collective-permute-start(bf16[256,128]{1,0:T(8,128)(2,1)S(1)} %fusion.1.own_ref), channel_id=1, source_target_pairs={{0,704},{64,0},{128,64},{192,128},{256,192},{320,256},{384,320},{4... | collective-permute-start | bytes 196616 | tf_op jit(solution)/shard_map/ppermute | solution.py:321
  103.4 7.4 %collective-permute-start.9 = (bf16[256,128]{1,0:T(8,128)(2,1)S(1)}, bf16[256,128]{1,0:T(8,128)(2,1)S(1)}, u32[]{:S(2)}, u32[]{:S(2)}) collective-permute-start(bf16[256,128]{1,0:T(8,128)(2,1)S(1)} %fusion.1.own_ref), channel_id=1, source_target_pairs={{0,64},{64,128},{128,192},{192,256},{256,320},{320,384},{384,448},... | collective-permute-start | bytes 196616 | tf_op jit(solution)/shard_map/ppermute | solution.py:321
